TPU v7x, 32 devices: a whole 2x2x4 slice. The times are simulated.
32 devices in a mesh: dp: 8 (over y, x, core), head: 4 (over z).
Axes of the slice: x: 2, y: 2, z: 4, core: 2. Of those that a mesh axis runs over, the one named last changes fastest.
Arguments:
- frames_in: bfloat16 [8192, 768], P(('dp', 'head')), may hold values from -6 to 6
- step_embed: bfloat16 [24, 768], P('dp'), may hold values from -6 to 6
- text_feats: bfloat16 [6144, 768], P('dp'), may hold values from -6 to 6
- clip_frames: int32 [8, 3], P('dp'), may hold values from 250 to 512, as said below
- text_tokens: int32 [8, 3], P('dp'), may hold values from 5 to 256
- out_grad: bfloat16 [8192, 768], P(('dp', 'head')), may hold values from -6 to 6
- ada_weight: bfloat16 [768, 4608], P('dp'), may hold values from -0.21875 to 0.21875
- ada_bias: bfloat16 [4608], P('dp'), may hold values from -1.75 to 1.75
- qkv_weight: bfloat16 [768, 3, 768], P('dp', None, 'head'), may hold values from -0.21875 to 0.21875
- qv_bias: bfloat16 [2, 12, 64], P(None, 'head', 'dp'), may hold values from -1.75 to 1.75
- attn_out_weight: bfloat16 [768, 768], P('head', 'dp'), may hold values from -1.25 to 1.25
- attn_out_bias: bfloat16 [768], P('dp'), may hold values from -1.75 to 1.75
- cross_gain: bfloat16 [768], P('dp'), may hold values from 0.5 to 1.5
- cross_q_weight: bfloat16 [768, 768], P('dp', 'head'), may hold values from -0.21875 to 0.21875
- cross_q_bias: bfloat16 [12, 64], P('head', 'dp'), may hold values from -1.75 to 1.75
- cross_kv_weight: bfloat16 [768, 2, 768], P('dp', None, 'head'), may hold values from -0.21875 to 0.21875
- cross_v_bias: bfloat16 [12, 64], P('head', 'dp'), may hold values from -1.75 to 1.75
- cross_out_weight: bfloat16 [768, 768], P('head', 'dp'), may hold values from -0.875 to 0.875
- cross_out_bias: bfloat16 [768], P('dp'), may hold values from -1.75 to 1.75
- mlp_in_weight: bfloat16 [768, 3072], P('dp', 'head'), may hold values from -0.21875 to 0.21875
- mlp_in_bias: bfloat16 [12, 256], P('head', 'dp'), may hold values from -1.75 to 1.75
- mlp_out_weight: bfloat16 [3072, 768], P('head', 'dp'), may hold values from -0.109375 to 0.109375
- mlp_out_bias: bfloat16 [768], P('dp'), may hold values from -1.75 to 1.75
Outputs:
- layer_out: bfloat16 [8192, 768], P(('dp', 'head'))
- frames_grad: float32 [8192, 768], P(('dp', 'head'))
- step_grad: float32 [24, 768], P('dp')
- text_grad: float32 [6144, 768], P(('dp', 'head'))
- ada_weight_grad: float32 [768, 4608], P('dp')
- ada_bias_grad: float32 [4608], P('dp')
- qkv_weight_grad: float32 [768, 3, 768], P('dp', None, 'head')
- qv_bias_grad: float32 [2, 12, 64], P(None, 'head', 'dp')
- attn_out_weight_grad: float32 [768, 768], P('head', 'dp')
- attn_out_bias_grad: float32 [768], P('dp')
- cross_gain_grad: float32 [768], P('dp')
- cross_q_weight_grad: float32 [768, 768], P('dp', 'head')
- cross_q_bias_grad: float32 [12, 64], P('head', 'dp')
- cross_kv_weight_grad: float32 [768, 2, 768], P('dp', None, 'head')
- cross_v_bias_grad: float32 [12, 64], P('head', 'dp')
- cross_out_weight_grad: float32 [768, 768], P('head', 'dp')
- cross_out_bias_grad: float32 [768], P('dp')
- mlp_in_weight_grad: float32 [768, 3072], P('dp', 'head')
- mlp_in_bias_grad: float32 [12, 256], P('head', 'dp')
- mlp_out_weight_grad: float32 [3072, 768], P('head', 'dp')
- mlp_out_bias_grad: float32 [768], P('dp')
Inputs may be any that keep to these rules, and one draw needn't show every extreme that they name: Each row of clip_frames sums to 1024; exactly one entry of each row is 512, every entry is 250 or more.
All inputs are finite; a program needn't handle non-finite values.
Results may differ from a plain program's by a relative error of at most 0.029.
Values may be sent and summed in bfloat16 or wider, within the bound.
No kernel may reach another device: no remote copies, remote signals or barrier semaphores. Data moves between devices by JAX's collectives and lax.ppermute only.
A program may use at most 192 MiB of HBM per device.

v0:
```python
from functools import partial

import jax
import jax.numpy as jnp
from jax import lax
from jax.sharding import PartitionSpec as P

HD = 64
TXT = 256


epsilon = 1e-06
highest = lax.Precision.HIGHEST


def matmul(former, latter):
    return jnp.dot(former, latter, preferred_element_type=jnp.float32)


def matmul_left(former, latter):
    return lax.dot_general(
        former, latter, (((0,), (0,)), ((), ())), preferred_element_type=jnp.float32
    )


def matmul_right(former, latter):
    return lax.dot_general(
        former, latter, (((1,), (1,)), ((), ())), preferred_element_type=jnp.float32
    )


def normalize(tensor):
    average = jnp.mean(tensor, axis=-1, keepdims=True)
    centered = tensor - average
    inverse = lax.rsqrt(jnp.mean(centered * centered, axis=-1, keepdims=True) + epsilon)
    return (centered * inverse, inverse)


def normalize_back(upstream, normed, inverse):
    return inverse * (
        upstream
        - jnp.mean(upstream, axis=-1, keepdims=True)
        - normed * jnp.mean(upstream * normed, axis=-1, keepdims=True)
    )


def clip_index(position, lengths):
    clip_ends = jnp.cumsum(lengths)
    return jnp.sum((position[:, None] >= clip_ends[None, :]).astype(jnp.int32), axis=1)


def block_shape(tensor, block_count):
    return tensor.reshape((block_count, tensor.shape[0] // block_count) + tensor.shape[1:])


def masked_scores(query_block, clip_block, key_heads, key_clip, key_live):
    allowed = (clip_block[:, None] == key_clip[None, :]) & key_live[None, :]
    scores = (
        jnp.einsum("rhd,khd->hrk", query_block, key_heads, preferred_element_type=jnp.float32)
        * 0.125
    )
    return jnp.where(allowed[None], scores, -1e30)


def attend_forward(queries, key_heads, value_heads, query_clip, key_clip, key_live):
    block_count = queries.shape[0] // min(512, queries.shape[0])

    def one_block(pieces):
        query_block, clip_block = pieces
        scores = masked_scores(query_block, clip_block, key_heads, key_clip, key_live)
        highest_score = jnp.max(scores, axis=-1, keepdims=True)
        exponent = jnp.exp(scores - highest_score)
        summed = jnp.sum(exponent, axis=-1, keepdims=True)
        weights = (exponent / summed).astype(jnp.bfloat16)
        output = jnp.einsum(
            "hrk,khd->rhd", weights, value_heads, preferred_element_type=jnp.float32
        )
        return (output.astype(jnp.bfloat16), highest_score[..., 0] + jnp.log(summed[..., 0]))

    outputs, log_total = lax.map(
        one_block, (block_shape(queries, block_count), block_shape(query_clip, block_count))
    )
    return (outputs.reshape(queries.shape), log_total)


def attend_backward(
    queries, key_heads, value_heads, out_grads, log_total, query_clip, key_clip, key_live
):
    block_count = log_total.shape[0]

    def one_block(running, pieces):
        key_grad, value_grad = running
        query_block, grad_block, total_block, clip_block = pieces
        scores = masked_scores(query_block, clip_block, key_heads, key_clip, key_live)
        weights = jnp.exp(scores - total_block[..., None])
        weight_grad = jnp.einsum(
            "rhd,khd->hrk", grad_block, value_heads, preferred_element_type=jnp.float32
        )
        offset = jnp.sum(weight_grad * weights, axis=-1, keepdims=True)
        score_grad = (weights * (weight_grad - offset)).astype(jnp.bfloat16)
        query_grad = (
            jnp.einsum("hrk,khd->rhd", score_grad, key_heads, preferred_element_type=jnp.float32)
            * 0.125
        )
        key_grad = (
            key_grad
            + jnp.einsum(
                "hrk,rhd->khd", score_grad, query_block, preferred_element_type=jnp.float32
            )
            * 0.125
        )
        value_grad = value_grad + jnp.einsum(
            "hrk,rhd->khd",
            weights.astype(jnp.bfloat16),
            grad_block,
            preferred_element_type=jnp.float32,
        )
        return ((key_grad, value_grad), query_grad)

    initial = jnp.zeros(key_heads.shape, jnp.float32)
    (key_grad, value_grad), query_grad = lax.scan(
        one_block,
        (initial, initial),
        (
            block_shape(queries, block_count),
            block_shape(out_grads, block_count),
            log_total,
            block_shape(query_clip, block_count),
        ),
    )
    return (
        query_grad.reshape(queries.shape).astype(jnp.bfloat16),
        key_grad.astype(jnp.bfloat16),
        value_grad.astype(jnp.bfloat16),
    )


def on_device(
    frames_in,
    step_embed,
    text_feats,
    clip_frames,
    text_tokens,
    out_grad,
    ada_weight,
    ada_bias,
    qkv_weight,
    qv_bias,
    attn_out_weight,
    attn_out_bias,
    cross_gain,
    cross_q_weight,
    cross_q_bias,
    cross_kv_weight,
    cross_v_bias,
    cross_out_weight,
    cross_out_bias,
    mlp_in_weight,
    mlp_in_bias,
    mlp_out_weight,
    mlp_out_bias,
):
    (
        whole_ada,
        whole_ada_bias,
        whole_qkv,
        whole_qv_bias,
        whole_attn_out,
        whole_attn_bias,
        whole_gain,
        whole_cross_q,
        whole_cross_q_bias,
        whole_cross_kv,
        whole_cross_v_bias,
        whole_cross_out,
        whole_cross_bias,
        whole_mlp_in,
        whole_mlp_in_bias,
        whole_mlp_out,
        whole_mlp_bias,
    ) = (
        lax.all_gather(ada_weight, "dp", axis=0, tiled=True),
        lax.all_gather(ada_bias, "dp", axis=0, tiled=True),
        lax.all_gather(qkv_weight, "dp", axis=0, tiled=True),
        lax.all_gather(qv_bias, "dp", axis=2, tiled=True),
        lax.all_gather(attn_out_weight, "dp", axis=1, tiled=True),
        lax.all_gather(attn_out_bias, "dp", axis=0, tiled=True),
        lax.all_gather(cross_gain, "dp", axis=0, tiled=True),
        lax.all_gather(cross_q_weight, "dp", axis=0, tiled=True),
        lax.all_gather(cross_q_bias, "dp", axis=1, tiled=True),
        lax.all_gather(cross_kv_weight, "dp", axis=0, tiled=True),
        lax.all_gather(cross_v_bias, "dp", axis=1, tiled=True),
        lax.all_gather(cross_out_weight, "dp", axis=1, tiled=True),
        lax.all_gather(cross_out_bias, "dp", axis=0, tiled=True),
        lax.all_gather(mlp_in_weight, "dp", axis=0, tiled=True),
        lax.all_gather(mlp_in_bias, "dp", axis=1, tiled=True),
        lax.all_gather(mlp_out_weight, "dp", axis=1, tiled=True),
        lax.all_gather(mlp_out_bias, "dp", axis=0, tiled=True),
    )
    splits = lax.axis_size("head")
    head_index = lax.axis_index("head")
    group_count = lax.axis_size("dp")
    group_index = lax.axis_index("dp")
    row_count = frames_in.shape[0]
    group_rows = row_count * splits
    row_start = head_index * row_count
    clip_count = clip_frames.shape[1]
    text_count = text_feats.shape[0]
    local_width = whole_qkv.shape[2]
    local_heads = local_width // HD
    lengths = clip_frames[0]
    group_clip = clip_index(jnp.arange(group_rows, dtype=jnp.int32), lengths)
    text_position = jnp.arange(text_count, dtype=jnp.int32)
    text_clip = text_position // TXT
    clip_range = jnp.arange(clip_count, dtype=jnp.int32)
    text_limit = jnp.sum(
        jnp.where(text_clip[:, None] == clip_range[None, :], text_tokens[0][None, :], 0), axis=1
    )
    text_live = text_position % TXT < text_limit
    all_live = group_clip >= 0
    choose = (group_clip[:, None] == clip_range[None, :]).astype(jnp.float32)

    def own_rows(tensor):
        return lax.dynamic_slice_in_dim(tensor, row_start, row_count, 0)

    frame_rows, grad_rows = (
        lax.all_gather(frames_in, "head", axis=0, tiled=True),
        lax.all_gather(out_grad, "head", axis=0, tiled=True),
    )
    silu_value, silu_pull = jax.vjp(jax.nn.silu, step_embed.astype(jnp.float32))
    silu_low = silu_value.astype(jnp.bfloat16)
    modulation = matmul(silu_low, whole_ada) + whole_ada_bias.astype(jnp.float32)
    per_frame = jnp.dot(choose, modulation, precision=highest)
    shift_one, scale_one, gate_one, shift_two, scale_two, gate_two = jnp.split(per_frame, 6, axis=1)
    frames = frame_rows.astype(jnp.float32)
    normed_one, inverse_one = normalize(frames)
    hidden_one = (normed_one * (1.0 + scale_one) + shift_one).astype(jnp.bfloat16)
    zeros_local = jnp.zeros((local_width,), jnp.float32)
    qv_rows = whole_qv_bias.astype(jnp.float32).reshape(2, local_width)
    qkv_bias = jnp.stack([qv_rows[0], zeros_local, qv_rows[1]])
    qkv_rows = (
        jnp.einsum("gd,djc->gjc", hidden_one, whole_qkv, preferred_element_type=jnp.float32)
        + qkv_bias
    ).astype(jnp.bfloat16)
    self_query = qkv_rows[:, 0].reshape(group_rows, local_heads, HD)
    self_key = qkv_rows[:, 1].reshape(group_rows, local_heads, HD)
    self_value = qkv_rows[:, 2].reshape(group_rows, local_heads, HD)
    self_heads_out, self_total = attend_forward(
        self_query, self_key, self_value, group_clip, group_clip, all_live
    )
    attended = self_heads_out.reshape(group_rows, local_width)
    attn_branch = lax.psum(matmul(attended, whole_attn_out).astype(jnp.bfloat16), "head").astype(
        jnp.float32
    ) + whole_attn_bias.astype(jnp.float32)
    after_self = frames + gate_one * attn_branch
    normed_two, inverse_two = normalize(after_self)
    gain_values = whole_gain.astype(jnp.float32)
    hidden_two = (normed_two * gain_values).astype(jnp.bfloat16)
    cross_query = (
        matmul(hidden_two, whole_cross_q)
        + whole_cross_q_bias.astype(jnp.float32).reshape(local_width)
    ).astype(jnp.bfloat16)
    kv_bias = jnp.stack([zeros_local, whole_cross_v_bias.astype(jnp.float32).reshape(local_width)])
    cross_kv = (
        jnp.einsum("td,djc->tjc", text_feats, whole_cross_kv, preferred_element_type=jnp.float32)
        + kv_bias
    ).astype(jnp.bfloat16)
    cross_q_heads = cross_query.reshape(group_rows, local_heads, HD)
    cross_k_heads = cross_kv[:, 0].reshape(text_count, local_heads, HD)
    cross_v_heads = cross_kv[:, 1].reshape(text_count, local_heads, HD)
    cross_heads_out, cross_total = attend_forward(
        cross_q_heads, cross_k_heads, cross_v_heads, group_clip, text_clip, text_live
    )
    cross_attended = cross_heads_out.reshape(group_rows, local_width)
    cross_branch = lax.psum(
        matmul(cross_attended, whole_cross_out).astype(jnp.bfloat16), "head"
    ).astype(jnp.float32) + whole_cross_bias.astype(jnp.float32)
    after_cross = after_self + cross_branch
    normed_three, inverse_three = normalize(after_cross)
    hidden_three = (normed_three * (1.0 + scale_two) + shift_two).astype(jnp.bfloat16)
    pre_activation = matmul(hidden_three, whole_mlp_in) + whole_mlp_in_bias.astype(
        jnp.float32
    ).reshape(-1)
    activated, gelu_pull = jax.vjp(partial(jax.nn.gelu, approximate=True), pre_activation)
    activated_low = activated.astype(jnp.bfloat16)
    mlp_branch = lax.psum_scatter(
        matmul(
            lax.slice_in_dim(activated_low, 0, row_count * lax.axis_size("head"), axis=0),
            whole_mlp_out,
        ).astype(jnp.bfloat16),
        "head",
        scatter_dimension=0,
        tiled=True,
    ).astype(jnp.float32) + whole_mlp_bias.astype(jnp.float32)
    after_cross_own = own_rows(after_cross)
    gate_two_own = own_rows(gate_two)
    layer_out = (after_cross_own + gate_two_own * mlp_branch).astype(jnp.bfloat16)
    upstream = grad_rows.astype(jnp.float32)
    upstream_own = own_rows(upstream)
    gate_two_grad = upstream_own * mlp_branch
    mlp_grad = (upstream * gate_two).astype(jnp.bfloat16)
    grad_mlp_out = matmul_left(activated_low, mlp_grad)
    grad_mlp_bias = jnp.sum(mlp_grad.astype(jnp.float32), axis=0)
    inner_grad = gelu_pull(matmul_right(mlp_grad, whole_mlp_out))[0].astype(jnp.bfloat16)
    grad_mlp_in = matmul_left(hidden_three, inner_grad)
    grad_mlp_in_bias = jnp.sum(inner_grad.astype(jnp.float32), axis=0).reshape(
        whole_mlp_in_bias.shape
    )
    hidden_three_grad = lax.psum_scatter(
        matmul_right(inner_grad, whole_mlp_in).astype(jnp.bfloat16),
        "head",
        scatter_dimension=0,
        tiled=True,
    ).astype(jnp.float32)
    normed_three_own = own_rows(normed_three)
    scale_two_grad = hidden_three_grad * normed_three_own
    cross_grad_rows = upstream_own + normalize_back(
        hidden_three_grad * (1.0 + own_rows(scale_two)), normed_three_own, own_rows(inverse_three)
    )
    cross_branch_grad = lax.all_gather(
        cross_grad_rows.astype(jnp.bfloat16), "head", axis=0, tiled=True
    )
    grad_cross_out = matmul_left(cross_attended, cross_branch_grad)
    grad_cross_bias = jnp.sum(cross_branch_grad.astype(jnp.float32), axis=0)
    cross_heads_grad = (
        matmul_right(cross_branch_grad, whole_cross_out)
        .astype(jnp.bfloat16)
        .reshape(group_rows, local_heads, HD)
    )
    cross_q_grad, cross_k_grad, cross_v_grad = attend_backward(
        cross_q_heads,
        cross_k_heads,
        cross_v_heads,
        cross_heads_grad,
        cross_total,
        group_clip,
        text_clip,
        text_live,
    )
    query_back = cross_q_grad.reshape(group_rows, local_width)
    text_back = jnp.stack(
        [
            cross_k_grad.reshape(text_count, local_width),
            cross_v_grad.reshape(text_count, local_width),
        ],
        axis=1,
    )
    grad_cross_q = matmul_left(hidden_two, query_back)
    grad_cross_q_bias = jnp.sum(query_back.astype(jnp.float32), axis=0).reshape(
        whole_cross_q_bias.shape
    )
    grad_cross_kv = jnp.einsum(
        "td,tjc->djc", text_feats, text_back, preferred_element_type=jnp.float32
    )
    grad_cross_v_bias = jnp.sum(text_back[:, 1].astype(jnp.float32), axis=0).reshape(
        whole_cross_v_bias.shape
    )
    hidden_two_part = matmul_right(query_back, whole_cross_q)
    text_part = jnp.einsum(
        "tjc,djc->td", text_back, whole_cross_kv, preferred_element_type=jnp.float32
    )
    hidden_two_grad, text_grad = (
        lax.psum_scatter(
            hidden_two_part.astype(jnp.bfloat16), "head", scatter_dimension=0, tiled=True
        ).astype(jnp.float32),
        lax.psum_scatter(
            text_part.astype(jnp.bfloat16), "head", scatter_dimension=0, tiled=True
        ).astype(jnp.float32),
    )
    normed_two_own = own_rows(normed_two)
    gain_part = jnp.sum(hidden_two_grad * normed_two_own, axis=0)
    self_grad_rows = cross_grad_rows + normalize_back(
        hidden_two_grad * gain_values, normed_two_own, own_rows(inverse_two)
    )
    gate_one_grad = self_grad_rows * own_rows(attn_branch)
    attn_branch_grad = lax.all_gather(
        (self_grad_rows * own_rows(gate_one)).astype(jnp.bfloat16), "head", axis=0, tiled=True
    )
    grad_attn_out = matmul_left(attended, attn_branch_grad)
    grad_attn_bias = jnp.sum(attn_branch_grad.astype(jnp.float32), axis=0)
    self_heads_grad = (
        matmul_right(attn_branch_grad, whole_attn_out)
        .astype(jnp.bfloat16)
        .reshape(group_rows, local_heads, HD)
    )
    self_q_grad, self_k_grad, self_v_grad = attend_backward(
        self_query,
        self_key,
        self_value,
        self_heads_grad,
        self_total,
        group_clip,
        group_clip,
        all_live,
    )
    qkv_back = jnp.stack(
        [
            self_q_grad.reshape(group_rows, local_width),
            self_k_grad.reshape(group_rows, local_width),
            self_v_grad.reshape(group_rows, local_width),
        ],
        axis=1,
    )
    grad_qkv = jnp.einsum("gd,gjc->djc", hidden_one, qkv_back, preferred_element_type=jnp.float32)
    qkv_sums = jnp.sum(qkv_back.astype(jnp.float32), axis=0)
    grad_qv_bias = jnp.stack([qkv_sums[0], qkv_sums[2]]).reshape(whole_qv_bias.shape)
    hidden_one_grad = lax.psum_scatter(
        jnp.einsum("gjc,djc->gd", qkv_back, whole_qkv, preferred_element_type=jnp.float32).astype(
            jnp.bfloat16
        ),
        "head",
        scatter_dimension=0,
        tiled=True,
    ).astype(jnp.float32)
    normed_one_own = own_rows(normed_one)
    frames_grad = self_grad_rows + normalize_back(
        hidden_one_grad * (1.0 + own_rows(scale_one)), normed_one_own, own_rows(inverse_one)
    )
    frame_mod_grad = jnp.concatenate(
        [
            hidden_one_grad,
            hidden_one_grad * normed_one_own,
            gate_one_grad,
            hidden_three_grad,
            scale_two_grad,
            gate_two_grad,
        ],
        axis=1,
    )
    clip_mod_part = lax.dot_general(
        own_rows(choose), frame_mod_grad, (((0,), (0,)), ((), ())), precision=highest
    )
    clip_sum, gain_group = (
        lax.psum(clip_mod_part.astype(jnp.bfloat16), "head").astype(jnp.float32),
        lax.psum(gain_part.astype(jnp.bfloat16), "head").astype(jnp.float32),
    )
    clip_mod_grad = clip_sum.astype(jnp.bfloat16)
    silu_all, mod_all = (
        lax.all_gather(silu_low, "dp", axis=0, tiled=True),
        lax.all_gather(clip_mod_grad, "dp", axis=0, tiled=True),
    )
    step_grad = silu_pull(matmul_right(clip_mod_grad, whole_ada))[0]
    ada_rows = whole_ada.shape[0] // group_count
    grad_ada = matmul_left(
        lax.dynamic_slice_in_dim(silu_all, group_index * ada_rows, ada_rows, 1), mod_all
    )
    bias_width = whole_ada_bias.shape[0] // group_count
    grad_ada_bias = lax.dynamic_slice_in_dim(
        jnp.sum(mod_all.astype(jnp.float32), axis=0), group_index * bias_width, bias_width, 0
    )
    shards = (
        lax.psum_scatter(grad_qkv, "dp", scatter_dimension=0, tiled=True),
        lax.psum_scatter(grad_qv_bias, "dp", scatter_dimension=2, tiled=True),
        lax.psum_scatter(grad_attn_out, "dp", scatter_dimension=1, tiled=True),
        lax.psum_scatter(grad_attn_bias, "dp", scatter_dimension=0, tiled=True),
        lax.psum_scatter(gain_group, "dp", scatter_dimension=0, tiled=True),
        lax.psum_scatter(grad_cross_q, "dp", scatter_dimension=0, tiled=True),
        lax.psum_scatter(grad_cross_q_bias, "dp", scatter_dimension=1, tiled=True),
        lax.psum_scatter(grad_cross_kv, "dp", scatter_dimension=0, tiled=True),
        lax.psum_scatter(grad_cross_v_bias, "dp", scatter_dimension=1, tiled=True),
        lax.psum_scatter(grad_cross_out, "dp", scatter_dimension=1, tiled=True),
        lax.psum_scatter(grad_cross_bias, "dp", scatter_dimension=0, tiled=True),
        lax.psum_scatter(grad_mlp_in, "dp", scatter_dimension=0, tiled=True),
        lax.psum_scatter(grad_mlp_in_bias, "dp", scatter_dimension=1, tiled=True),
        lax.psum_scatter(grad_mlp_out, "dp", scatter_dimension=1, tiled=True),
        lax.psum_scatter(grad_mlp_bias, "dp", scatter_dimension=0, tiled=True),
    )
    return (layer_out, frames_grad, step_grad, text_grad, grad_ada, grad_ada_bias) + tuple(shards)


def solution(mesh):
    return jax.shard_map(
        on_device,
        mesh=mesh,
        in_specs=(
            P(("dp", "head"), None),
            P("dp", None),
            P("dp", None),
            P("dp", None),
            P("dp", None),
            P(("dp", "head"), None),
            P("dp", None),
            P("dp"),
            P("dp", None, "head"),
            P(None, "head", "dp"),
            P("head", "dp"),
            P("dp"),
            P("dp"),
            P("dp", "head"),
            P("head", "dp"),
            P("dp", None, "head"),
            P("head", "dp"),
            P("head", "dp"),
            P("dp"),
            P("dp", "head"),
            P("head", "dp"),
            P("head", "dp"),
            P("dp"),
        ),
        out_specs=(
            P(("dp", "head"), None),
            P(("dp", "head"), None),
            P("dp", None),
            P(("dp", "head"), None),
            P("dp", None),
            P("dp"),
            P("dp", None, "head"),
            P(None, "head", "dp"),
            P("head", "dp"),
            P("dp"),
            P("dp"),
            P("dp", "head"),
            P("head", "dp"),
            P("dp", None, "head"),
            P("head", "dp"),
            P("head", "dp"),
            P("dp"),
            P("dp", "head"),
            P("head", "dp"),
            P("head", "dp"),
            P("dp"),
        ),
        check_vma=False,
    )
```

profile of v0, /device:TPU:0, one launch (start us, length us, event | category | flops | bytes accessed | tf_op | source)
XLA Modules:
  0.0 999.6 jit_solution(4152683704405314949)
XLA Ops:
  17.3 27.3 %all-reduce.14 = (bf16[768]{0:T(1024)(128)(2,1)S(1)}, bf16[4608]{0:T(1024)(128)(2,1)S(1)}, bf16[768]{0:T(1024)(128)(2,1)S(1)}, bf16[768]{0:T(1024)(128)(2,1)}, bf16[768]{0:T(1024)(128)(2,1)}) all-reduce(bf16[768]{0:T(1024)(128)(2,1)S(1)} %dynamic-update-slice.1, ...), channel_id=1, replica_groups=mesh['dp'=8,'head'=4] {'dp'}, use_global_device_ids=true, to_apply=%add.2 | all-reduce | flops 7680 | bytes 30720
  45.7 12.7 %all_gather.72 = bf16[768,3,192]{2,1,0:T(4,128)(2,1)S(1)} all-gather(bf16[96,3,192]{2,1,0:T(4,128)(2,1)S(1)} %copy.129), channel_id=1, replica_groups=mesh['dp'=8,'head'=4] {'dp'}, dimensions={0}, use_global_device_ids=true | all-gather | bytes 995328 | tf_op jit(solution)/shard_map/all_gather | solution.py:184
  123.2 14.1 %while.55 = (s32[]{:T(128)}, bf16[2,512,3,64]{1,3,2,0:T(8,128)(2,1)}, f32[2,3,512]{2,1,0:T(4,128)}, s32[2,512]{1,0:T(2,128)S(1)}, s32[1024]{0:T(1024)S(1)}, /*in...) while((s32[]{:T(128)}, ...), condition=%wide.region_7.8_spmd, body=%wide.region_4.7_spmd.sunk | while | flops 422672896 | bytes 23787656 | solution.py:80
  189.7 22.6 %all-reduce.19.cloned.1.call-done = bf16[1024,768]{1,0:T(8,128)(2,1)} async-done(((bf16[1024,768]{1,0:T(8,128)(2,1)}), bf16[1024,768]{1,0:T(8,128)(2,1)}) %all-reduce.19.cloned.1.call-update) | async-done | bytes 1572880 | tf_op jit(solution)/shard_map/psum | solution.py:252
  212.2 13.0 %convert_reduce_fusion.1 = (f32[768]{0:T(1024)}, bf16[1024,768]{1,0:T(8,128)(2,1)}, f32[1024,768]{1,0:T(8,128)}, f32[1024]{0:T(1024)S(1)}, f32[1024,768]{1,0:T(8...) fusion(f32[1024,4608]{1,0:T(8,128)} %copy-done.5, ...), kind=kLoop, calls=%fused_computation.140 | loop fusion | flops 8648960 | bytes 37758976 | tf_op jit(solution)/shard_map/reduce_sum | solution.py:303
  252.5 58.0 %all-reduce.21.cloned.1.call-done = bf16[1024,768]{1,0:T(8,128)(2,1)} async-done(((bf16[1024,768]{1,0:T(8,128)(2,1)}), bf16[1024,768]{1,0:T(8,128)(2,1)}) %all-reduce.21.cloned.1.call-update) | async-done | bytes 1572880 | tf_op jit(solution)/shard_map/psum | solution.py:275
  319.9 15.5 %all-gather.17.cloned.1.call-done = bf16[768,768]{1,0:T(8,128)(2,1)} async-done(((bf16[96,768]{1,0:T(8,128)(2,1)}), bf16[768,768]{1,0:T(8,128)(2,1)}) %all-gather.17.cloned.1.call-update) | async-done | bytes 1179664 | tf_op jit(solution)/shard_map/all_gather | solution.py:195
  340.2 21.2 %all-gather.19.cloned.1.call-done = bf16[768,768]{0,1:T(8,128)(2,1)} async-done(((bf16[768,96]{0,1:T(8,128)(2,1)}), bf16[768,768]{0,1:T(8,128)(2,1)}) %all-gather.19.cloned.1.call-update) | async-done | bytes 1179664 | tf_op jit(solution)/shard_map/all_gather | solution.py:197
  375.0 32.0 %reduce-scatter.27.cloned.1.call-done = bf16[256,768]{1,0:T(8,128)(2,1)} async-done(((bf16[1024,768]{1,0:T(8,128)(2,1)}), bf16[256,768]{1,0:T(8,128)(2,1)}) %reduce-scatter.27.cloned.1.call-update) | async-done | bytes 393232 | tf_op jit(solution)/shard_map/reduce_scatter | solution.py:309
  411.8 36.1 %all-gather.23.cloned.1.call-done = bf16[1024,768]{1,0:T(8,128)(2,1)} async-done(((bf16[256,768]{1,0:T(8,128)(2,1)}), bf16[1024,768]{1,0:T(8,128)(2,1)}) %all-gather.23.cloned.1.call-update) | async-done | bytes 1572880 | tf_op jit(solution)/shard_map/all_gather | solution.py:320
  451.2 26.7 %while.57 = (s32[]{:T(128)}, f32[768,3,64]{0,2,1:T(8,128)}, f32[768,3,64]{0,2,1:T(8,128)}, bf16[2,512,3,64]{1,3,2,0:T(8,128)(2,1)}, bf16[2,512,3,64]{1,3,2,0:T(8...) while((s32[]{:T(128)}, f32[768,3,64]{0,2,1:T(8,128)}, ...), condition=%wide.region_25.26_spmd.clone, body=%wide.region_23.25_spmd.clone.sunk | while | flops 774296064 | bytes 96594312 | solution.py:121
  483.9 33.4 %reduce-scatter.29.cloned.1.call-done = bf16[256,768]{1,0:T(8,128)(2,1)} async-done(((bf16[1024,768]{1,0:T(8,128)(2,1)}), bf16[256,768]{1,0:T(8,128)(2,1)}) %reduce-scatter.29.cloned.1.call-update) | async-done | bytes 393232 | tf_op jit(solution)/shard_map/reduce_scatter | solution.py:363
  532.1 26.6 %all-gather.25.cloned.1.call-done = bf16[1024,768]{1,0:T(8,128)(2,1)} async-done(((bf16[256,768]{1,0:T(8,128)(2,1)}), bf16[1024,768]{1,0:T(8,128)(2,1)}) %all-gather.25.cloned.1.call-update) | async-done | bytes 1572880 | tf_op jit(solution)/shard_map/all_gather | solution.py:376
  569.3 35.7 %while.58 = (s32[]{:T(128)}, f32[1024,3,64]{0,2,1:T(8,128)S(1)}, f32[1024,3,64]{0,2,1:T(8,128)}, bf16[2,512,3,64]{1,3,2,0:T(8,128)(2,1)}, bf16[2,512,3,64]{1,3,2...) while((s32[]{:T(128)}, f32[1024,3,64]{0,2,1:T(8,128)S(1)}, ...), condition=%wide.region_31.32_spmd.clone, body=%wide.region_29.31_spmd.clone.sunk | while | flops 1032354304 | bytes 109897528 | solution.py:121
  639.4 33.7 %reduce-scatter.45.cloned.1.call-done = f32[96,384]{1,0:T(8,128)} async-done(((f32[768,384]{1,0:T(8,128)}), f32[96,384]{1,0:T(8,128)}) %reduce-scatter.45.cloned.1.call-update) | async-done | bytes 147472
  674.9 29.5 %reduce-scatter.33.cloned.1.call-done = bf16[192,768]{1,0:T(8,128)(2,1)} async-done(((bf16[768,768]{1,0:T(8,128)(2,1)}), bf16[192,768]{1,0:T(8,128)(2,1)}) %reduce-scatter.33.cloned.1.call-update) | async-done | bytes 294928 | tf_op jit(solution)/shard_map/reduce_scatter | solution.py:366
  713.7 27.5 %reduce-scatter.43.cloned.1.call-done = f32[96,192]{1,0:T(8,128)} async-done(((f32[768,192]{1,0:T(8,128)}), f32[96,192]{1,0:T(8,128)}) %reduce-scatter.43.cloned.1.call-update) | async-done | bytes 73744
  742.8 35.8 %reduce-scatter.31.cloned.1.call-done = bf16[256,768]{1,0:T(8,128)(2,1)} async-done(((bf16[1024,768]{1,0:T(8,128)(2,1)}), bf16[256,768]{1,0:T(8,128)(2,1)}) %reduce-scatter.31.cloned.1.call-update) | async-done | bytes 393232 | tf_op jit(solution)/shard_map/reduce_scatter | solution.py:407
  789.4 25.7 %reduce-scatter.25.cloned.1.call-done = bf16[256,768]{1,0:T(8,128)(2,1)} async-done(((bf16[1024,768]{1,0:T(8,128)(2,1)}), bf16[256,768]{1,0:T(8,128)(2,1)}) %reduce-scatter.25.cloned.1.call-update) | async-done | bytes 393232 | tf_op jit(solution)/shard_map/reduce_scatter | solution.py:286
  822.0 17.4 %all-reduce.15 = (bf16[768]{0:T(1024)(128)(2,1)S(1)}, bf16[3,4608]{1,0:T(4,128)(2,1)S(1)}) all-reduce(bf16[768]{0:T(1024)(128)(2,1)S(1)} %copy-done.71, bf16[3,4608]{1,0:T(4,128)(2,1)S(1)} %convolution_convert_fusion), channel_id=1, replica_groups=mesh['dp'=8,'head'=4] {'head'}, use_global_device_ids=true, to_apply=%region_45.46 | all-reduce | flops 14592 | bytes 58368 | tf_op jit(solution)/shard_map/psum | solution.py:435
  839.5 22.8 %all-reduce.13 = (f32[2,3,64]{2,1,0:T(4,128)S(1)}, f32[768]{0:T(1024)S(1)}, f32[768]{0:T(1024)S(1)}, f32[3,64]{1,0:T(4,128)S(1)}, f32[3,64]{1,0:T(4,128)S(1)}, /*index=5*/f32[768]{0:T(1024)S(1)}, f32[768]{0:T(1024)S(1)}) all-reduce(f32[2,3,64]{2,1,0:T(4,128)S(1)} %reshape.460, ...), channel_id=8, replica_groups=mesh['dp'=8,'head'=4] {'dp'}, use_global_device_ids=true, to_apply=%region_40.41.clone | all-reduce | flops 3840 | bytes 29184
  892.9 14.4 %reduce-scatter.41.cloned.1.call-done = f32[768,96]{0,1:T(8,128)} async-done(((f32[768,768]{0,1:T(8,128)}), f32[768,96]{0,1:T(8,128)}) %reduce-scatter.41.cloned.1.call-update) | async-done | bytes 294928 | tf_op jit(solution)/shard_map/reduce_scatter | solution.py:465
  907.4 38.8 %reduce-scatter.37.cloned.1.call-done = f32[96,192]{1,0:T(8,128)} async-done(((f32[768,192]{1,0:T(8,128)}), f32[96,192]{1,0:T(8,128)}) %reduce-scatter.37.cloned.1.call-update) | async-done | bytes 73744 | tf_op jit(solution)/shard_map/reduce_scatter | solution.py:457
  946.1 46.4 %reduce-scatter.35.cloned.1.call-done = f32[96,3,192]{2,0,1:T(8,128)} async-done(((f32[768,3,192]{2,0,1:T(8,128)}), f32[96,3,192]{2,0,1:T(8,128)}) %reduce-scatter.35.cloned.1.call-update) | async-done | bytes 221200 | tf_op jit(solution)/shard_map/reduce_scatter | solution.py:452
  (507 shorter events, 398.9 us)
Async XLA Ops:
  7.2 179.9 %copy-start = (bf16[768,768]{1,0:T(8,128)(2,1)S(1)}, bf16[768,768]{1,0:T(8,128)(2,1)}, u32[]{:S(2)}) copy-start(bf16[768,768]{1,0:T(8,128)(2,1)} %param.33) | copy-start | bytes 3538948
  7.2 83.8 %all-gather.13.cloned.1.call-start = ((), (), s32[]{:S(2)}) async-start(), calls=%async_computation.13 | async-start | bytes 1966080 | tf_op jit(solution)/shard_map/all_gather | solution.py:227
  8.0 91.4 %all-gather.15.cloned.1.call-start = ((), (), s32[]{:S(2)}) async-start(), calls=%async_computation.14 | async-start | bytes 7962624 | tf_op jit(solution)/shard_map/all_gather | solution.py:182
  8.7 181.0 %all-gather.21.cloned.1.call-start = ((), (), s32[]{:S(2)}) async-start(), calls=%async_computation.20 | async-start | bytes 1966080 | tf_op jit(solution)/shard_map/all_gather | solution.py:228
  9.5 202.8 %all-reduce.19.cloned.1.call-start = ((), (), s32[]{:S(2)}) async-start(), calls=%async_computation.15 | async-start | bytes 3145728 | tf_op jit(solution)/shard_map/psum | solution.py:252
  142.6 167.8 %all-reduce.21.cloned.1.call-start = ((), (), s32[]{:S(2)}) async-start(), calls=%async_computation.16 | async-start | bytes 3145728 | tf_op jit(solution)/shard_map/psum | solution.py:275
  242.2 93.2 %all-gather.17.cloned.1.call-start = ((), (), s32[]{:S(2)}) async-start(), calls=%async_computation.17 | async-start | bytes 1327104 | tf_op jit(solution)/shard_map/all_gather | solution.py:195
  242.7 118.6 %all-gather.19.cloned.1.call-start = ((), (), s32[]{:S(2)}) async-start(), calls=%async_computation.18 | async-start | bytes 1327104 | tf_op jit(solution)/shard_map/all_gather | solution.py:197
  243.5 163.5 %reduce-scatter.27.cloned.1.call-start = ((), (), s32[]{:S(2)}) async-start(), calls=%async_computation.21 | async-start | bytes 1966080 | tf_op jit(solution)/shard_map/reduce_scatter | solution.py:309
  252.5 108.8 %copy-start.75 = (f32[768]{0:T(1024)}, f32[768]{0:T(1024)S(1)}, u32[]{:S(2)}) copy-start(f32[768]{0:T(1024)S(1)} %reshape.463) | copy-start | bytes 9220
  371.5 76.4 %all-gather.23.cloned.1.call-start = ((), (), s32[]{:S(2)}) async-start(), calls=%async_computation.22 | async-start | bytes 1966080 | tf_op jit(solution)/shard_map/all_gather | solution.py:320
  411.8 105.5 %reduce-scatter.29.cloned.1.call-start = ((), (), s32[]{:S(2)}) async-start(), calls=%async_computation.23 | async-start | bytes 1966080 | tf_op jit(solution)/shard_map/reduce_scatter | solution.py:363
  482.9 75.7 %all-gather.25.cloned.1.call-start = ((), (), s32[]{:S(2)}) async-start(), calls=%async_computation.24 | async-start | bytes 1966080 | tf_op jit(solution)/shard_map/all_gather | solution.py:376
  522.5 109.3 %reduce-scatter.49.cloned.1.call-start = ((), (), s32[]{:S(2)}) async-start(), calls=%async_computation.34 | async-start | bytes 147456
  523.4 114.4 %reduce-scatter.47.cloned.1.call-start = ((), (), s32[]{:S(2)}) async-start(), calls=%async_computation.33 | async-start | bytes 884736
  526.1 147.0 %reduce-scatter.45.cloned.1.call-start = ((), (), s32[]{:S(2)}) async-start(), calls=%async_computation.32 | async-start | bytes 1327104
  530.1 174.4 %reduce-scatter.33.cloned.1.call-start = ((), (), s32[]{:S(2)}) async-start(), calls=%async_computation.26 | async-start | bytes 1474560 | tf_op jit(solution)/shard_map/reduce_scatter | solution.py:366
  532.0 209.1 %reduce-scatter.43.cloned.1.call-start = ((), (), s32[]{:S(2)}) async-start(), calls=%async_computation.31 | async-start | bytes 884736
  568.5 210.1 %reduce-scatter.31.cloned.1.call-start = ((), (), s32[]{:S(2)}) async-start(), calls=%async_computation.25 | async-start | bytes 1966080 | tf_op jit(solution)/shard_map/reduce_scatter | solution.py:407
  612.2 202.9 %reduce-scatter.25.cloned.1.call-start = ((), (), s32[]{:S(2)}) async-start(), calls=%async_computation.19 | async-start | bytes 1966080 | tf_op jit(solution)/shard_map/reduce_scatter | solution.py:286
  617.8 275.1 %reduce-scatter.39.cloned.1.call-start = ((), (), s32[]{:S(2)}) async-start(), calls=%async_computation.29 | async-start | bytes 2654208 | tf_op jit(solution)/shard_map/reduce_scatter | solution.py:463
  622.9 284.4 %reduce-scatter.41.cloned.1.call-start = ((), (), s32[]{:S(2)}) async-start(), calls=%async_computation.30 | async-start | bytes 2654208 | tf_op jit(solution)/shard_map/reduce_scatter | solution.py:465
  628.1 318.0 %reduce-scatter.37.cloned.1.call-start = ((), (), s32[]{:S(2)}) async-start(), calls=%async_computation.28 | async-start | bytes 884736 | tf_op jit(solution)/shard_map/reduce_scatter | solution.py:457
  636.6 355.9 %reduce-scatter.35.cloned.1.call-start = ((), (), s32[]{:S(2)}) async-start(), calls=%async_computation.27 | async-start | bytes 2654208 | tf_op jit(solution)/shard_map/reduce_scatter | solution.py:452
  (105 other events, 1303.8 us)
Sparse Core Ops, SparseCore 0:
  9.6 39.7 all-gather.12
  51.3 47.9 all-gather.14
  100.9 37.4 all-gather.20
  142.8 69.4 all-reduce.18
  242.3 68.1 all-reduce.20
  312.2 23.0 all-gather.16
  337.2 24.0 all-gather.18
  371.7 35.2 reduce-scatter.26
  411.9 36.0 all-gather.22
  483.0 34.1 reduce-scatter.28
  522.6 36.0 all-gather.24
  562.1 32.1 reduce-scatter.48
  597.8 34.9 reduce-scatter.46
  636.3 36.7 reduce-scatter.44
  675.2 29.1 reduce-scatter.32
  707.4 33.6 reduce-scatter.42
  743.3 35.2 reduce-scatter.30
  780.8 34.2 reduce-scatter.24
  819.0 41.6 reduce-scatter.38
  864.9 42.4 reduce-scatter.40
  911.1 34.9 reduce-scatter.36
  950.0 42.4 reduce-scatter.34
where the time goes:
time: 1010 us; the launch traced here: 1000 us
  waiting for transfers between devices  505 us (50%)
  blocking collectives  174 us (17%)
  matrix products  150 us (15%)
  other arithmetic  86.6 us (9%)
  local copies, waits for them, and re-layouts  62.5 us (6%)
  between operations  18.2 us (2%)
    unnamed x26, waiting for transfers between devices  64.8 us
    psum x1, waiting for transfers between devices, on_device(): lax.psum(matmul(cross_attended, whole_cross_out).astype(jnp.bfloat16), 'h...  58 us
    unnamed x2, blocking collectives  50.1 us
    reduce_scatter x1, waiting for transfers between devices, on_device(): lax.psum_scatter(grad_qkv, 'dp', scatter_dimension=0, tiled=True)  46.4 us
    reduce_scatter x1, waiting for transfers between devices, on_device(): lax.psum_scatter(grad_cross_q, 'dp', scatter_dimension=0, tiled=True)  38.8 us
    all_gather x1, waiting for transfers between devices, on_device(): lax.all_gather(cross_grad_rows.astype(jnp.bfloat16), 'head', axis=0, tile...  36.1 us
    reduce_scatter x1, waiting for transfers between devices, on_device(): lax.psum_scatter(jnp.einsum('gjc,djc->gd', qkv_back, whole_qkv, preferred...  35.8 us
    unnamed x165, local copies, waits for them, and re-layouts  35.2 us
  transfers between devices with their start and end apart: 22, of which 17 were waited for; matrix products, arithmetic and copies ran while one was open for 21% of the time, Pallas kernels for 0%

commit v1 on v0

v1 whole, which is shorter than its diff:
```python
from functools import partial

import jax
import jax.numpy as jnp
from jax import lax
from jax.experimental import pallas as pl
from jax.experimental.pallas import tpu as pltpu
from jax.sharding import PartitionSpec as P

D = 768
HD = 64
TXT = 256
WIN = 128
EPS = 1e-06
NEG = -1e30
F32 = jnp.float32
BF16 = jnp.bfloat16
HIGH = lax.Precision.HIGHEST
S_Z, S_END, S_TOK, S_OFF = 0, 1, 3, 8
S_LEN = 16


def nn(a, b):
    return lax.dot_general(a, b, (((1,), (0,)), ((), ())), preferred_element_type=F32)


def nt(a, b):
    return lax.dot_general(a, b, (((1,), (1,)), ((), ())), preferred_element_type=F32)


def tn(a, b):
    return lax.dot_general(a, b, (((0,), (0,)), ((), ())), preferred_element_type=F32)


def normalize(v):
    centered = v - jnp.mean(v, axis=-1, keepdims=True)
    inverse = lax.rsqrt(jnp.mean(centered * centered, axis=-1, keepdims=True) + EPS)
    return centered * inverse, inverse


def normalize_back(u, normed, inverse):
    return inverse * (
        u
        - jnp.mean(u, axis=-1, keepdims=True)
        - normed * jnp.mean(u * normed, axis=-1, keepdims=True)
    )


def clip_of(position, scal):
    return (position >= scal[S_END]).astype(jnp.int32) + (position >= scal[S_END + 1]).astype(
        jnp.int32
    )


def frame_position(index, block, rows, splits, scal):
    return lax.rem(scal[S_Z] - block + splits, splits) * rows + index


def per_row(mod_ref, part, clip):
    cols = slice(part * D, (part + 1) * D)
    first, second, third = (mod_ref[c : c + 1, cols] for c in range(3))
    return jnp.where(clip == 0, first, jnp.where(clip == 1, second, third))


def clip_sums(clip_row, value):
    which = lax.broadcasted_iota(jnp.int32, (8, clip_row.shape[1]), 0)
    choose = (which == clip_row).astype(F32)
    return lax.dot_general(
        choose, value, (((1,), (0,)), ((), ())), precision=HIGH, preferred_element_type=F32
    )


def lanes(rows, low):
    lane = lax.broadcasted_iota(jnp.int32, (rows, WIN), 1)
    return lane < HD if low else lane >= HD


def keep(value, low):
    return jnp.where(lanes(value.shape[0], low), value, jnp.zeros_like(value))


def swap(value):
    return pltpu.roll(value, HD, 1)


def load_start(pieces, buffer, sems, scal, first):
    copies = []
    for j, piece in enumerate(pieces):
        rows = piece.shape[1]
        start = pl.multiple_of(scal[S_OFF + j], 32)
        copy = pltpu.make_async_copy(piece, buffer.at[:, pl.ds(start, rows), :], sems.at[first + j])
        copy.start()
        copies.append(copy)
    return copies


def store_copies(buffer, z, outs, sems, scal, first):
    copies = []
    j = 0
    for out in outs:
        for i in range(out.shape[0]):
            rows = out.shape[2]
            start = pl.multiple_of(scal[S_OFF + j], 32)
            copies.append(
                pltpu.make_async_copy(
                    buffer.at[z, pl.ds(start, rows), :], out.at[i, z], sems.at[first + j, z]
                )
            )
            j += 1
    return copies


def attend(queries, kv, mask, scores, probs, count):
    rows = queries.shape[0]
    step = 256
    outs, totals = [], []
    for h in range(3):
        if h < 2:
            query = keep(queries[:, :WIN], h == 0)
            kcol, vcol = 0, 1
        else:
            query = queries[:, WIN:]
            kcol, vcol = 2, 3
        peak = None
        for lo in range(0, count, step):
            part = nt(kv(lo, lo + step, kcol), query) + mask[lo : lo + step, :]
            scores[lo : lo + step, :] = part
            top = jnp.max(part, axis=0, keepdims=True)
            peak = top if peak is None else jnp.maximum(peak, top)
        total = jnp.zeros((1, rows), F32)
        for lo in range(0, count, step):
            part = jnp.exp(scores[lo : lo + step, :] - peak)
            total = total + jnp.sum(part, axis=0, keepdims=True)
            probs[lo : lo + step, :] = part.astype(BF16)
        out = tn(kv(0, count, vcol), probs[0:count, :]) * (1.0 / total)
        outs.append(out)
        totals.append(peak + jnp.log(total))
    cat = jnp.concatenate(
        [jnp.zeros((HD, rows), F32), outs[2][:HD], outs[0][:HD], outs[1][HD:]], axis=0
    )
    return cat.T.astype(BF16), totals


def attend_back(queries, kv, out_grad, mask, totals, probs, grads, count, put):
    rows = queries.shape[0]
    step = 256
    wide = out_grad.astype(F32)
    second = keep(swap(wide[:, :WIN]), True).astype(BF16)
    query_parts = []
    heads = []
    for h in range(3):
        if h < 2:
            query = keep(queries[:, :WIN], h == 0)
            given = keep(out_grad[:, WIN:], h == 0)
            kcol, vcol = 0, 1
        else:
            query, given = queries[:, WIN:], second
            kcol, vcol = 2, 3
        heads.append((query, given))
        delta = jnp.zeros((1, rows), F32)
        for lo in range(0, count, step):
            part = nt(kv(lo, lo + step, kcol), query) + mask[lo : lo + step, :]
            weights = jnp.exp(part - totals[h])
            weight_grad = nt(kv(lo, lo + step, vcol), given)
            delta = delta + jnp.sum(weights * weight_grad, axis=0, keepdims=True)
            probs[h, lo : lo + step, :] = weights
            grads[h, lo : lo + step, :] = weight_grad
        query_part = jnp.zeros((rows, WIN), F32)
        for lo in range(0, count, step):
            part = probs[h, lo : lo + step, :]
            score_grad = (part * (grads[h, lo : lo + step, :] - delta)).astype(BF16)
            grads[h, lo : lo + step, :] = score_grad.astype(F32)
            query_part = query_part + tn(score_grad, kv(lo, lo + step, kcol))
        query_parts.append(query_part * 0.125)
    for lo in range(0, count, step):
        hi = lo + step
        prob = [probs[h, lo:hi, :].astype(BF16) for h in range(3)]
        grad = [grads[h, lo:hi, :].astype(BF16) for h in range(3)]
        put(
            lo,
            hi,
            nn(grad[0], heads[0][0]) + nn(grad[1], heads[1][0]),
            nn(prob[0], heads[0][1]) + nn(prob[1], heads[1][1]),
            nn(grad[2], heads[2][0]),
            nn(prob[2], heads[2][1]),
        )
    pair = jnp.where(lanes(rows, True), query_parts[0], query_parts[1])
    third = keep(swap(query_parts[2]), True)
    return pair, third


def self_mask(scal, mask, rows, splits):
    query = clip_of(
        frame_position(lax.broadcasted_iota(jnp.int32, (1, rows), 1), 0, rows, splits, scal), scal
    )
    for block in range(splits):
        key = clip_of(
            frame_position(
                lax.broadcasted_iota(jnp.int32, (rows, 1), 0), block, rows, splits, scal
            ),
            scal,
        )
        mask[block * rows : (block + 1) * rows, :] = jnp.where(key == query, 0.0, NEG)


def cross_mask(scal, mask, rows, splits, clips):
    query = clip_of(
        frame_position(lax.broadcasted_iota(jnp.int32, (1, rows), 1), 0, rows, splits, scal), scal
    )
    slot = lax.broadcasted_iota(jnp.int32, (TXT, 1), 0)
    for c in range(clips):
        allowed = (query == c) & (slot < scal[S_TOK + c])
        mask[c * TXT : (c + 1) * TXT, :] = jnp.where(allowed, 0.0, NEG)


def own_clip(scal, rows, splits, block=0):
    return clip_of(
        frame_position(lax.broadcasted_iota(jnp.int32, (rows, 1), 0), block, rows, splits, scal),
        scal,
    )


def own_clip_row(scal, rows, splits, block=0):
    return clip_of(
        frame_position(lax.broadcasted_iota(jnp.int32, (1, rows), 1), block, rows, splits, scal),
        scal,
    )


def shard_index(scal, z, splits):
    return lax.rem(scal[S_Z] - z + splits, splits)


def self_forward(n_p, splits, *refs):
    scal = refs[0]
    frames = refs[1 : 1 + splits]
    mod, bias, out_bias = refs[1 + splits : 4 + splits]
    pieces = refs[4 + splits : 4 + splits + n_p]
    hidden, kv_out, q_out, att_out, lse, branch_out, after = refs[
        4 + splits + n_p : 11 + splits + n_p
    ]
    weights, mask, scores, probs, sems = refs[11 + splits + n_p :]
    rows = frames[0].shape[0]
    count = rows * splits
    copies = load_start(pieces, weights, sems, scal, 0)
    self_mask(scal, mask, rows, splits)
    for block in range(splits):
        clip = own_clip(scal, rows, splits, block)
        normed, _ = normalize(frames[block][...].astype(F32))
        value = normed * (1.0 + per_row(mod, 1, clip)) + per_row(mod, 0, clip)
        hidden[block * rows : (block + 1) * rows, :] = value.astype(BF16)
    branch_out[...] = jnp.broadcast_to(out_bias[...], branch_out.shape)
    for copy in copies:
        copy.wait()

    def one(z, carry):
        bias_row = bias[shard_index(scal, z, splits)]
        for block in range(splits):
            span = slice(block * rows, (block + 1) * rows)
            part = nn(hidden[span, :], weights[z, :, WIN : 5 * WIN]) + bias_row[:, WIN : 5 * WIN]
            kv_out[z, span, :] = part.astype(BF16)
            if block == 0:
                third = keep(swap(part[:, 2 * WIN : 3 * WIN].astype(BF16).astype(F32)), False)
        pair = nn(hidden[0:rows, :], weights[z, :, 0:WIN]) + bias_row[:, 0:WIN]
        queries = (
            jnp.concatenate([pair.astype(BF16).astype(F32), third], axis=1) * 0.125
        ).astype(BF16)
        q_out[z] = queries

        def kv(lo, hi, col):
            return kv_out[z, lo:hi, col * WIN : (col + 1) * WIN]

        attended, totals = attend(queries, kv, mask, scores, probs, count)
        att_out[z] = attended
        for h in range(3):
            lse[z, h : h + 1, :] = totals[h]
        branch_out[...] += nt(attended, weights[z, :, 4 * WIN :])
        return carry

    lax.fori_loop(0, splits, one, 0)
    clip = own_clip(scal, rows, splits)
    after[...] = frames[0][...].astype(F32) + per_row(mod, 2, clip) * branch_out[...]


def cross_forward(n_p, splits, *refs):
    scal, after_self, text, gain, bias, out_bias = refs[:6]
    pieces = refs[6 : 6 + n_p]
    kv_out, q_out, att_out, lse, after = refs[6 + n_p : 11 + n_p]
    weights, mask, scores, probs, sems = refs[11 + n_p :]
    rows = after_self.shape[0]
    count = text.shape[0]
    copies = load_start(pieces, weights, sems, scal, 0)
    cross_mask(scal, mask, rows, splits, count // TXT)
    normed, _ = normalize(after_self[...])
    hidden = (normed * gain[...]).astype(BF16)
    after[...] = after_self[...] + out_bias[...]
    for copy in copies:
        copy.wait()

    def one(z, carry):
        bias_row = bias[shard_index(scal, z, splits)]
        for lo in range(0, count, 256):
            part = nn(text[lo : lo + 256, :], weights[z, :, WIN : 5 * WIN])
            kv_out[z, lo : lo + 256, :] = (part + bias_row[:, WIN : 5 * WIN]).astype(BF16)
        pair = nn(hidden, weights[z, :, 0:WIN]) + bias_row[:, 0:WIN]
        third = nn(hidden, weights[z, :, 3 * WIN : 4 * WIN]) + bias_row[:, 3 * WIN : 4 * WIN]
        third = keep(swap(third.astype(BF16).astype(F32)), False)
        queries = (
            jnp.concatenate([pair.astype(BF16).astype(F32), third], axis=1) * 0.125
        ).astype(BF16)
        q_out[z] = queries

        def kv(lo, hi, col):
            return kv_out[z, lo:hi, col * WIN : (col + 1) * WIN]

        attended, totals = attend(queries, kv, mask, scores, probs, count)
        att_out[z] = attended
        for h in range(3):
            lse[z, h : h + 1, :] = totals[h]
        after[...] += nt(attended, weights[z, :, 4 * WIN :])
        return carry

    lax.fori_loop(0, splits, one, 0)


def feed_forward(n_p, splits, *refs):
    scal, after_cross, upstream, mod, in_bias, out_bias = refs[:6]
    in_pieces = refs[6 : 6 + n_p]
    out_pieces = refs[6 + n_p : 6 + 2 * n_p]
    rest = refs[6 + 2 * n_p :]
    n_o = 2 if n_p > 1 else 1
    layer_out, d_after = rest[:2]
    in_grads = rest[2 : 2 + n_o]
    out_grads = rest[2 + n_o : 2 + 2 * n_o]
    in_bias_grad, out_bias_grad, sums = rest[2 + 2 * n_o : 5 + 2 * n_o]
    w_in, w_out, g_in, g_out, mlp, back, load_sems, store_sems = rest[5 + 2 * n_o :]
    rows = after_cross.shape[0]
    copies = load_start(in_pieces, w_in, load_sems, scal, 0)
    copies += load_start(out_pieces, w_out, load_sems, scal, n_p)
    clip = own_clip(scal, rows, splits)
    normed, inverse = normalize(after_cross[...])
    scale = 1.0 + per_row(mod, 4, clip)
    hidden = (normed * scale + per_row(mod, 3, clip)).astype(BF16)
    gate = per_row(mod, 5, clip)
    given = upstream[...].astype(F32)
    low = (given * gate).astype(BF16)
    low_wide = low.astype(F32)
    out_bias_grad[...] = jnp.sum(low_wide, axis=0, keepdims=True)
    hidden_t = hidden.astype(F32).T.astype(BF16)
    low_t = low_wide.T.astype(BF16)
    mlp[...] = jnp.broadcast_to(out_bias[...], mlp.shape)
    back[...] = jnp.zeros_like(back)
    for copy in copies:
        copy.wait()

    def one(z, carry):
        place = shard_index(scal, z, splits)
        pre = nn(hidden, w_in[z]) + in_bias[place]
        inner = 0.7978845608028654 * (pre + 0.044715 * (pre * pre * pre))
        curve = jnp.tanh(inner)
        half = 0.5 * (1.0 + curve)
        active = (pre * half).astype(BF16)
        slope = half + 0.5 * pre * (1.0 - curve * curve) * 0.7978845608028654 * (
            1.0 + 3.0 * 0.044715 * pre * pre
        )
        pre_grad = (slope * nn(low, w_out[z])).astype(BF16)
        in_bias_grad[place] = jnp.sum(pre_grad.astype(F32), axis=0, keepdims=True)
        mlp[...] += nt(active, w_out[z])
        back[...] += nt(pre_grad, w_in[z])
        g_in[z] = nn(hidden_t, pre_grad).astype(BF16)
        for copy in store_copies(g_in, z, in_grads, store_sems, scal, 0):
            copy.start()
        g_out[z] = nn(low_t, active).astype(BF16)
        for copy in store_copies(g_out, z, out_grads, store_sems, scal, n_p):
            copy.start()
        return carry

    lax.fori_loop(0, splits, one, 0)
    branch = mlp[...]
    layer_out[...] = (after_cross[...] + gate * branch).astype(BF16)
    hidden_grad = back[...]
    d_after[...] = given + normalize_back(hidden_grad * scale, normed, inverse)
    clip_row = own_clip_row(scal, rows, splits)
    sums[:, 0:D] = clip_sums(clip_row, hidden_grad)
    sums[:, D : 2 * D] = clip_sums(clip_row, hidden_grad * normed)
    sums[:, 2 * D :] = clip_sums(clip_row, given * branch)
    for z in range(splits):
        for copy in store_copies(g_in, z, in_grads, store_sems, scal, 0):
            copy.wait()
        for copy in store_copies(g_out, z, out_grads, store_sems, scal, n_p):
            copy.wait()


def cross_backward(n_p, splits, *refs):
    scal, d_cross, after_self, text, gain, mod, branch, kv_in, q_in, att_in, lse = refs[:11]
    pieces = refs[11 : 11 + n_p]
    rest = refs[11 + n_p :]
    n_o = 2 if n_p > 1 else 1
    grads = rest[:n_o]
    d_after, d_attn = rest[n_o : n_o + 2]
    text_own = rest[n_o + 2]
    text_parts = rest[n_o + 3 : n_o + 2 + splits]
    bias_grad, row_grads, sums = rest[n_o + 2 + splits : n_o + 5 + splits]
    weights, gbuf, mask, probs, dscore, key_grad, back, text_back, text_t, load_sems, store_sems = (
        rest[n_o + 5 + splits :]
    )
    rows = after_self.shape[0]
    count = text.shape[0]
    copies = load_start(pieces, weights, load_sems, scal, 0)
    cross_mask(scal, mask, rows, splits, count // TXT)
    normed, inverse = normalize(after_self[...])
    hidden = (normed * gain[...]).astype(BF16)
    hidden_t = hidden.astype(F32).T.astype(BF16)
    given = d_cross[...].astype(BF16)
    given_wide = given.astype(F32)
    given_t = given_wide.T.astype(BF16)
    for lo in range(0, count, 256):
        text_t[:, lo : lo + 256] = text[lo : lo + 256, :].astype(F32).T.astype(BF16)
    back[...] = jnp.zeros_like(back)
    text_back[...] = jnp.zeros_like(text_back)
    row_grads[...] = jnp.zeros_like(row_grads)
    row_grads[0:1, :] = jnp.sum(given_wide, axis=0, keepdims=True)
    for copy in copies:
        copy.wait()

    def one(z, carry):
        place = shard_index(scal, z, splits)

        def kv(lo, hi, col):
            return kv_in[z, lo:hi, col * WIN : (col + 1) * WIN]

        def put(lo, hi, k01, v01, k2, v2):
            key_grad[lo:hi, 0:WIN] = k01.astype(BF16)
            key_grad[lo:hi, WIN : 2 * WIN] = v01.astype(BF16)
            key_grad[lo:hi, 2 * WIN : 3 * WIN] = k2.astype(BF16)
            key_grad[lo:hi, 3 * WIN : 4 * WIN] = v2.astype(BF16)

        head_grad = nn(given, weights[z, :, 4 * WIN :]).astype(BF16)
        totals = [lse[z, h : h + 1, :] for h in range(3)]
        pair, third = attend_back(
            q_in[z], kv, head_grad, mask, totals, probs, dscore, count, put
        )
        pair, third = pair.astype(BF16), third.astype(BF16)
        part = nn(text_t[...], key_grad[...])
        out_part = nn(given_t, att_in[z])
        gbuf[z, :, 0:WIN] = nn(hidden_t, pair).astype(BF16)
        gbuf[z, :, WIN : 3 * WIN] = part[:, 0 : 2 * WIN].astype(BF16)
        gbuf[z, :, 3 * WIN : 4 * WIN] = (
            part[:, 2 * WIN : 3 * WIN] + nn(hidden_t, third)
        ).astype(BF16)
        gbuf[z, :, 4 * WIN : 5 * WIN] = (part[:, 3 * WIN :] + out_part[:, 0:WIN]).astype(BF16)
        gbuf[z, :, 5 * WIN :] = out_part[:, WIN:].astype(BF16)
        for copy in store_copies(gbuf, z, grads, store_sems, scal, 0):
            copy.start()
        back[...] += nt(pair, weights[z, :, 0:WIN]) + nt(third, weights[z, :, 3 * WIN : 4 * WIN])
        for lo in range(0, count, 256):
            text_back[lo : lo + 256, :] += nt(
                key_grad[lo : lo + 256, :], weights[z, :, WIN : 5 * WIN]
            )
        key_sums = jnp.sum(key_grad[...].astype(F32), axis=0, keepdims=True)
        bias_grad[place, :, 0:WIN] = jnp.sum(pair.astype(F32), axis=0, keepdims=True)
        bias_grad[place, :, WIN : 3 * WIN] = key_sums[:, 0 : 2 * WIN]
        bias_grad[place, :, 3 * WIN : 4 * WIN] = key_sums[:, 2 * WIN : 3 * WIN] + jnp.sum(
            third.astype(F32), axis=0, keepdims=True
        )
        bias_grad[place, :, 4 * WIN : 5 * WIN] = key_sums[:, 3 * WIN :]
        bias_grad[place, :, 5 * WIN :] = jnp.zeros((1, WIN), F32)
        return carry

    lax.fori_loop(0, splits, one, 0)
    hidden_grad = back[...]
    row_grads[1:2, :] = jnp.sum(hidden_grad * normed, axis=0, keepdims=True)
    total = d_cross[...] + normalize_back(hidden_grad * gain[...], normed, inverse)
    d_after[...] = total
    clip = own_clip(scal, rows, splits)
    d_attn[...] = (total * per_row(mod, 2, clip)).astype(BF16)
    sums[...] = clip_sums(own_clip_row(scal, rows, splits), total * branch[...])
    height = count // splits
    for k in range(splits):
        start = pl.multiple_of(shard_index(scal, k, splits) * height, 64)
        block = text_back[pl.ds(start, height), :]
        if k == 0:
            text_own[...] = block
        else:
            text_parts[k - 1][...] = block.astype(BF16)
    for z in range(splits):
        for copy in store_copies(gbuf, z, grads, store_sems, scal, 0):
            copy.wait()


def self_backward(n_p, splits, *refs):
    scal = refs[0]
    frames = refs[1 : 1 + splits]
    given_ref, hidden, kv_in, q_in, att_in, lse = refs[1 + splits : 7 + splits]
    pieces = refs[7 + splits : 7 + splits + n_p]
    rest = refs[7 + splits + n_p :]
    n_o = 2 if n_p > 1 else 1
    grads = rest[:n_o]
    own = rest[n_o]
    parts = rest[n_o + 1 : n_o + splits]
    bias_grad, row_grads, sums = rest[n_o + splits : n_o + 3 + splits]
    weights, gbuf, mask, probs, dscore, key_grad, back, hidden_t, load_sems, store_sems = rest[
        n_o + 3 + splits :
    ]
    rows = frames[0].shape[0]
    count = rows * splits
    copies = load_start(pieces, weights, load_sems, scal, 0)
    self_mask(scal, mask, rows, splits)
    given = given_ref[...]
    given_wide = given.astype(F32)
    given_t = given_wide.T.astype(BF16)
    for lo in range(0, count, 256):
        hidden_t[:, lo : lo + 256] = hidden[lo : lo + 256, :].astype(F32).T.astype(BF16)
    back[...] = jnp.zeros_like(back)
    row_grads[...] = jnp.zeros_like(row_grads)
    row_grads[0:1, :] = jnp.sum(given_wide, axis=0, keepdims=True)
    for copy in copies:
        copy.wait()

    def one(z, carry):
        place = shard_index(scal, z, splits)

        def kv(lo, hi, col):
            return kv_in[z, lo:hi, col * WIN : (col + 1) * WIN]

        def put(lo, hi, k01, v01, k2, v2):
            key_grad[lo:hi, 0:WIN] = k01.astype(BF16)
            key_grad[lo:hi, WIN : 2 * WIN] = v01.astype(BF16)
            key_grad[lo:hi, 2 * WIN : 3 * WIN] = k2.astype(BF16)
            key_grad[lo:hi, 3 * WIN : 4 * WIN] = v2.astype(BF16)

        head_grad = nn(given, weights[z, :, 4 * WIN :]).astype(BF16)
        totals = [lse[z, h : h + 1, :] for h in range(3)]
        pair, third = attend_back(
            q_in[z], kv, head_grad, mask, totals, probs, dscore, count, put
        )
        pair = pair.astype(BF16)
        key_grad[0:rows, 2 * WIN : 3 * WIN] = (
            key_grad[0:rows, 2 * WIN : 3 * WIN].astype(F32) + third
        ).astype(BF16)
        part = nn(hidden_t[...], key_grad[...])
        out_part = nn(given_t, att_in[z])
        gbuf[z, :, 0:WIN] = nn(hidden_t[:, 0:rows], pair).astype(BF16)
        gbuf[z, :, WIN : 4 * WIN] = part[:, 0 : 3 * WIN].astype(BF16)
        gbuf[z, :, 4 * WIN : 5 * WIN] = (part[:, 3 * WIN :] + out_part[:, 0:WIN]).astype(BF16)
        gbuf[z, :, 5 * WIN :] = out_part[:, WIN:].astype(BF16)
        for copy in store_copies(gbuf, z, grads, store_sems, scal, 0):
            copy.start()
        for lo in range(0, count, 256):
            back[lo : lo + 256, :] += nt(
                key_grad[lo : lo + 256, :], weights[z, :, WIN : 5 * WIN]
            )
        back[0:rows, :] += nt(pair, weights[z, :, 0:WIN])
        key_sums = jnp.sum(key_grad[...].astype(F32), axis=0, keepdims=True)
        bias_grad[place, :, 0:WIN] = jnp.sum(pair.astype(F32), axis=0, keepdims=True)
        bias_grad[place, :, WIN : 5 * WIN] = key_sums
        bias_grad[place, :, 5 * WIN :] = jnp.zeros((1, WIN), F32)
        return carry

    lax.fori_loop(0, splits, one, 0)
    shift = jnp.zeros((8, D), F32)
    scale = jnp.zeros((8, D), F32)
    for block in range(splits):
        value = back[block * rows : (block + 1) * rows, :]
        if block == 0:
            own[...] = value
        else:
            parts[block - 1][...] = value.astype(BF16)
        normed, _ = normalize(frames[block][...].astype(F32))
        clip_row = own_clip_row(scal, rows, splits, block)
        shift = shift + clip_sums(clip_row, value)
        scale = scale + clip_sums(clip_row, value * normed)
    sums[:, 0:D] = shift
    sums[:, D:] = scale
    for z in range(splits):
        for copy in store_copies(gbuf, z, grads, store_sems, scal, 0):
            copy.wait()


def finish(splits, *refs):
    scal, frames, mod, d_after, own = refs[:5]
    parts = refs[5 : 4 + splits]
    out = refs[4 + splits]
    rows = frames.shape[0]
    value = own[...]
    for part in parts:
        value = value + part[...].astype(F32)
    normed, inverse = normalize(frames[...].astype(F32))
    scale = 1.0 + per_row(mod, 1, own_clip(scal, rows, splits))
    out[...] = d_after[...] + normalize_back(value * scale, normed, inverse)


MEMORY = {"v": pltpu.VMEM, "s": pltpu.SMEM, "a": pl.ANY}


def call(body, inputs, outs, scratch, flops, name):
    moved = sum(a.size * a.dtype.itemsize for _, a in inputs)
    moved += sum(_size(s, t) for _, s, t in outs)
    return pl.pallas_call(
        body,
        out_shape=tuple(jax.ShapeDtypeStruct(s, t) for _, s, t in outs),
        in_specs=[pl.BlockSpec(memory_space=MEMORY[m]) for m, _ in inputs],
        out_specs=tuple(pl.BlockSpec(memory_space=MEMORY[m]) for m, _, _ in outs),
        scratch_shapes=scratch,
        compiler_params=pltpu.CompilerParams(vmem_limit_bytes=58 * 1024 * 1024),
        cost_estimate=pl.CostEstimate(flops=int(flops), bytes_accessed=int(moved), transcendentals=0),
        name=name,
    )(*[a for _, a in inputs])


def _size(shape, kind):
    total = jnp.dtype(kind).itemsize
    for s in shape:
        total *= s
    return total


class Ring:
    def __init__(self):
        self.n_dp = lax.axis_size("dp")
        self.splits = lax.axis_size("head")
        self.square = self.n_dp == 8
        if self.square:
            self.core = [(i, i ^ 1) for i in range(8)]
            self.first = [(i, i ^ (4 if i & 1 else 2)) for i in range(8)]
            self.second = [(i, i ^ (2 if i & 1 else 4)) for i in range(8)]

    def offsets(self):
        if not self.square:
            return [jnp.int32(0)]
        me = lax.axis_index("dp")
        rows = D // 8

        def kept(d):
            odd = d & 1
            return [d, d ^ (2 + 2 * odd), d ^ (4 - 2 * odd), d ^ 6]

        return [place * rows for place in kept(me) + kept(me ^ 1)]

    def z_pieces(self, value):
        n = self.splits
        return [value] + [
            lax.ppermute(value, "head", [(s, (s + k) % n) for s in range(n)]) for k in range(1, n)
        ]

    def z_back(self, parts):
        n = self.splits
        return [
            lax.ppermute(parts[k - 1], "head", [(s, (s - k) % n) for s in range(n)])
            for k in range(1, n)
        ]

    def gather(self, shard):
        mine = jnp.stack(self.z_pieces(shard))
        if not self.square:
            return [lax.all_gather(mine, "dp", axis=1, tiled=True)]
        one = lax.ppermute(mine, "dp", self.first)
        two = lax.ppermute(mine, "dp", self.second)
        three = lax.ppermute(one, "dp", self.second)
        kept = [mine, one, two, three]
        return kept + [lax.ppermute(k, "dp", self.core) for k in kept]

    def reduce(self, grads):
        if not self.square:
            mine = lax.psum_scatter(grads[0][0], "dp", scatter_dimension=1, tiled=True)
        else:
            other = lax.ppermute(grads[1], "dp", self.core)

            def added(i):
                return grads[0][i].astype(F32) + other[i].astype(F32)

            corner = lax.ppermute(added(3).astype(BF16), "dp", self.second)
            two = lax.ppermute(added(2).astype(BF16), "dp", self.second)
            one = lax.ppermute((added(1) + corner.astype(F32)).astype(BF16), "dp", self.first)
            mine = added(0) + one.astype(F32) + two.astype(F32)
        mine = mine.astype(F32)
        arrived = self.z_back([mine[k].astype(BF16) for k in range(1, self.splits)])
        total = mine[0]
        for part in arrived:
            total = total + part.astype(F32)
        return total


def to_layout(q, k, v, o):
    return jnp.concatenate(
        [
            q[:, :WIN],
            k[:, :WIN],
            v[:, :WIN],
            q[:, WIN:],
            k[:, WIN:],
            v[:, WIN:],
            o[:, WIN:],
            o[:, :WIN],
        ],
        axis=1,
    )


def from_layout(value):
    def pick(pair, third):
        return jnp.concatenate(
            [value[:, pair : pair + WIN], value[:, third : third + HD]], axis=1
        )

    return pick(0, 3 * WIN), pick(WIN, 3 * WIN + HD), pick(2 * WIN, 4 * WIN), pick(
        5 * WIN, 4 * WIN + HD
    )


def on_device(
    frames_in,
    step_embed,
    text_feats,
    clip_frames,
    text_tokens,
    out_grad,
    ada_weight,
    ada_bias,
    qkv_weight,
    qv_bias,
    attn_out_weight,
    attn_out_bias,
    cross_gain,
    cross_q_weight,
    cross_q_bias,
    cross_kv_weight,
    cross_v_bias,
    cross_out_weight,
    cross_out_bias,
    mlp_in_weight,
    mlp_in_bias,
    mlp_out_weight,
    mlp_out_bias,
):
    both = ("dp", "head")
    ring = Ring()
    n_dp, splits = ring.n_dp, ring.splits
    z_index = lax.axis_index("head")
    rows = frames_in.shape[0]
    count = rows * splits
    text_count = text_feats.shape[0]
    clips = clip_frames.shape[1]
    width = D // splits
    shard_rows = D // n_dp
    ends = jnp.cumsum(clip_frames[0])
    offs = ring.offsets()
    n_p = len(offs)
    scal = jnp.stack(
        [z_index, ends[0], ends[1], text_tokens[0, 0], text_tokens[0, 1], text_tokens[0, 2]]
        + [jnp.int32(0)] * 2
        + [o.astype(jnp.int32) for o in offs]
        + [jnp.int32(0)] * (S_LEN - S_OFF - n_p)
    ).astype(jnp.int32)

    shard_self = to_layout(
        qkv_weight[:, 0], qkv_weight[:, 1], qkv_weight[:, 2], attn_out_weight.T
    )
    shard_cross = to_layout(
        cross_q_weight, cross_kv_weight[:, 0], cross_kv_weight[:, 1], cross_out_weight.T
    )

    biases = [
        ada_bias,
        qv_bias.reshape(-1),
        attn_out_bias,
        cross_gain,
        cross_q_bias.reshape(-1),
        cross_v_bias.reshape(-1),
        cross_out_bias,
        mlp_in_bias.reshape(-1),
        mlp_out_bias,
    ]
    flat = jnp.concatenate(biases)
    cols = step_embed.reshape(clips, n_dp, shard_rows).transpose(1, 0, 2).reshape(n_dp, -1)
    sent = jnp.concatenate(
        [
            jnp.broadcast_to(flat[None, None], (n_dp, splits, flat.shape[0])),
            jnp.broadcast_to(cols[:, None], (n_dp, splits, cols.shape[1])),
        ],
        axis=2,
    ).reshape(n_dp * splits, -1)
    got = lax.all_to_all(sent, both, 0, 0, tiled=True).reshape(n_dp, splits, -1)
    step_cols = got[:, 0, flat.shape[0] :].reshape(n_dp * clips, shard_rows).astype(F32)
    silu_cols = jax.nn.silu(step_cols).astype(BF16)
    spots = []
    place = 0
    for b in biases:
        spots.append(got[:, :, place : place + b.shape[0]].astype(F32))
        place += b.shape[0]

    def over_dp(value):
        return value[:, 0].reshape(1, -1)

    def by_head(value, lead=1):
        n = value.shape[2] // (lead * 3)
        v = value.reshape(n_dp, splits, lead, 3, n).transpose(1, 2, 3, 0, 4)
        return v.reshape(splits, lead, 3 * n_dp * n)

    all_ada_bias = over_dp(spots[0])
    qv = by_head(spots[1], 2)
    nothing = jnp.zeros((splits, width), F32)
    bias_self = to_layout(qv[:, 0], nothing, qv[:, 1], nothing)[:, None]
    all_attn_bias = over_dp(spots[2])
    all_gain = over_dp(spots[3])
    bias_cross = to_layout(
        by_head(spots[4])[:, 0], nothing, by_head(spots[5])[:, 0], nothing
    )[:, None]
    all_cross_bias = over_dp(spots[6])
    all_in_bias = by_head(spots[7])
    all_out_bias = over_dp(spots[8])

    mod_part = jnp.dot(silu_cols, ada_weight, preferred_element_type=F32)
    mod_got = lax.all_to_all(mod_part.reshape(n_dp, clips, -1), "dp", 0, 0, tiled=True)
    mod = jnp.sum(mod_got, axis=0) + all_ada_bias

    frame_blocks = ring.z_pieces(frames_in)
    pieces_self = ring.gather(shard_self)
    pieces_cross = ring.gather(shard_cross)
    pieces_in = ring.gather(mlp_in_weight)
    pieces_out = ring.gather(mlp_out_weight.T)

    def dma(n):
        return pltpu.SemaphoreType.DMA(n)

    def any_of(arrays):
        return [("a", a) for a in arrays]

    def vmem_of(arrays):
        return [("v", a) for a in arrays]

    piece_rows = D // n_p
    kept_out = [("a", (max(n_p // 2, 1), splits, piece_rows, D), BF16)] * (2 if n_p > 1 else 1)
    n_o = len(kept_out)
    shard_type = pltpu.VMEM((splits, D, D), BF16)

    hidden_one, self_kv, self_q, self_att, self_lse, attn_branch, after_self = call(
        partial(self_forward, n_p, splits),
        [("s", scal)]
        + vmem_of(frame_blocks)
        + vmem_of([mod, bias_self, all_attn_bias])
        + any_of(pieces_self),
        [
            ("v", (count, D), BF16),
            ("v", (splits, count, 4 * WIN), BF16),
            ("v", (splits, rows, 2 * WIN), BF16),
            ("v", (splits, rows, 2 * WIN), BF16),
            ("v", (splits, 8, rows), F32),
            ("v", (rows, D), F32),
            ("v", (rows, D), F32),
        ],
        [
            shard_type,
            pltpu.VMEM((count, rows), F32),
            pltpu.VMEM((count, rows), F32),
            pltpu.VMEM((count, rows), BF16),
            dma((n_p,)),
        ],
        6e9,
        "self_forward",
    )
    cross_kv, cross_q, cross_att, cross_lse, after_cross = call(
        partial(cross_forward, n_p, splits),
        [("s", scal)]
        + vmem_of([after_self, text_feats, all_gain, bias_cross, all_cross_bias])
        + any_of(pieces_cross),
        [
            ("v", (splits, text_count, 4 * WIN), BF16),
            ("v", (splits, rows, 2 * WIN), BF16),
            ("v", (splits, rows, 2 * WIN), BF16),
            ("v", (splits, 8, rows), F32),
            ("v", (rows, D), F32),
        ],
        [
            shard_type,
            pltpu.VMEM((text_count, rows), F32),
            pltpu.VMEM((text_count, rows), F32),
            pltpu.VMEM((text_count, rows), BF16),
            dma((n_p,)),
        ],
        5e9,
        "cross_forward",
    )
    results = call(
        partial(feed_forward, n_p, splits),
        [("s", scal)]
        + vmem_of([after_cross, out_grad, mod, all_in_bias, all_out_bias])
        + any_of(pieces_in)
        + any_of(pieces_out),
        [("v", (rows, D), BF16), ("v", (rows, D), F32)]
        + kept_out
        + kept_out
        + [
            ("v", (splits, 1, D), F32),
            ("v", (1, D), F32),
            ("v", (8, 3 * D), F32),
        ],
        [
            shard_type,
            shard_type,
            shard_type,
            shard_type,
            pltpu.VMEM((rows, D), F32),
            pltpu.VMEM((rows, D), F32),
            dma((2 * n_p,)),
            dma((2 * n_p, splits)),
        ],
        8e9,
        "feed_forward",
    )
    layer_out, d_after_cross = results[:2]
    grads_in = results[2 : 2 + n_o]
    grads_out = results[2 + n_o : 2 + 2 * n_o]
    in_bias_grad, out_bias_grad, sums_two = results[2 + 2 * n_o :]
    height = text_count // splits
    results = call(
        partial(cross_backward, n_p, splits),
        [("s", scal)]
        + vmem_of(
            [
                d_after_cross,
                after_self,
                text_feats,
                all_gain,
                mod,
                attn_branch,
                cross_kv,
                cross_q,
                cross_att,
                cross_lse,
            ]
        )
        + any_of(pieces_cross),
        kept_out
        + [("v", (rows, D), F32), ("v", (rows, D), BF16), ("v", (height, D), F32)]
        + [("v", (height, D), BF16)] * (splits - 1)
        + [("v", (splits, 1, D), F32), ("v", (8, D), F32), ("v", (8, D), F32)],
        [
            shard_type,
            shard_type,
            pltpu.VMEM((text_count, rows), F32),
            pltpu.VMEM((3, text_count, rows), F32),
            pltpu.VMEM((3, text_count, rows), F32),
            pltpu.VMEM((text_count, 4 * WIN), BF16),
            pltpu.VMEM((rows, D), F32),
            pltpu.VMEM((text_count, D), F32),
            pltpu.VMEM((D, text_count), BF16),
            dma((n_p,)),
            dma((n_p, splits)),
        ],
        9e9,
        "cross_backward",
    )
    grads_cross = results[:n_o]
    d_after_self, d_attn, text_own = results[n_o : n_o + 3]
    text_parts = results[n_o + 3 : n_o + 2 + splits]
    cross_bias_grad, cross_rows, gate_sums = results[n_o + 2 + splits :]
    results = call(
        partial(self_backward, n_p, splits),
        [("s", scal)]
        + vmem_of(frame_blocks)
        + vmem_of([d_attn, hidden_one, self_kv, self_q, self_att, self_lse])
        + any_of(pieces_self),
        kept_out
        + [("v", (rows, D), F32)]
        + [("v", (rows, D), BF16)] * (splits - 1)
        + [("v", (splits, 1, D), F32), ("v", (8, D), F32), ("v", (8, 2 * D), F32)],
        [
            shard_type,
            shard_type,
            pltpu.VMEM((count, rows), F32),
            pltpu.VMEM((3, count, rows), F32),
            pltpu.VMEM((3, count, rows), F32),
            pltpu.VMEM((count, 4 * WIN), BF16),
            pltpu.VMEM((count, D), F32),
            pltpu.VMEM((D, count), BF16),
            dma((n_p,)),
            dma((n_p, splits)),
        ],
        12e9,
        "self_backward",
    )
    grads_self = results[:n_o]
    own_part = results[n_o]
    parts = results[n_o + 1 : n_o + splits]
    self_bias_grad, self_rows, sums_one = results[n_o + splits :]

    arrived = ring.z_back(parts)
    (frames_grad,) = call(
        partial(finish, splits),
        [("s", scal)] + vmem_of([frames_in, mod, d_after_self, own_part]) + vmem_of(arrived),
        [("v", (rows, D), F32)],
        [],
        1e8,
        "finish",
    )
    text_grad = text_own
    for part in ring.z_back(text_parts):
        text_grad = text_grad + part.astype(F32)

    mod_partial = jnp.concatenate([sums_one, gate_sums, sums_two], axis=1)[:clips]
    mod_sum = mod_partial
    for part in ring.z_back([mod_partial] * (splits - 1)):
        mod_sum = mod_sum + part
    mod_low = mod_sum.astype(BF16)
    mod_all = lax.all_to_all(
        jnp.broadcast_to(mod_low[None], (n_dp,) + mod_low.shape), "dp", 0, 0, tiled=True
    ).reshape(n_dp * clips, -1)
    grad_ada = lax.dot_general(
        silu_cols, mod_all, (((0,), (0,)), ((), ())), preferred_element_type=F32
    )
    dp_index = lax.axis_index("dp")
    bias_width = ada_bias.shape[0]
    grad_ada_bias = jnp.sum(
        lax.dynamic_slice_in_dim(mod_all, dp_index * bias_width, bias_width, 1).astype(F32), axis=0
    )
    step_part = lax.dot_general(
        mod_all, ada_weight, (((1,), (1,)), ((), ())), preferred_element_type=F32
    )
    step_got = lax.all_to_all(step_part.reshape(n_dp, clips, shard_rows), "dp", 0, 0, tiled=True)
    step_value = step_embed.astype(F32)
    _, silu_pull = jax.vjp(jax.nn.silu, step_value)
    step_grad = silu_pull(step_got.transpose(1, 0, 2).reshape(clips, D))[0]

    def spread(value):
        v = value.reshape(n_dp, 1, D // n_dp)
        return jnp.broadcast_to(v, (n_dp, splits, D // n_dp))

    def heads_out(value):
        n = value.shape[1] // (3 * n_dp)
        return value.reshape(splits, 3, n_dp, n).transpose(2, 0, 1, 3).reshape(n_dp, splits, 3 * n)

    sq, _, sv, _ = from_layout(self_bias_grad[:, 0])
    cq, _, cv, _ = from_layout(cross_bias_grad[:, 0])
    entries = [
        heads_out(sq),
        heads_out(sv),
        spread(self_rows[0]),
        spread(cross_rows[1]),
        heads_out(cq),
        heads_out(cv),
        spread(cross_rows[0]),
        heads_out(in_bias_grad[:, 0]),
        spread(out_bias_grad[0]),
    ]
    packed = jnp.concatenate(entries, axis=2).reshape(n_dp * splits, -1)
    bias_sum = jnp.sum(lax.all_to_all(packed, both, 0, 0, tiled=True), axis=0)
    bias_out = []
    place = 0
    for e in entries:
        bias_out.append(bias_sum[place : place + e.shape[2]])
        place += e.shape[2]

    total_in = ring.reduce(grads_in)
    total_out = ring.reduce(grads_out)
    total_cross = ring.reduce(grads_cross)
    total_self = ring.reduce(grads_self)
    gq, gk, gv, go = from_layout(total_self)
    hq, hk, hv, ho = from_layout(total_cross)
    return (
        layer_out,
        frames_grad,
        step_grad,
        text_grad,
        grad_ada,
        grad_ada_bias,
        jnp.stack([gq, gk, gv], axis=1),
        jnp.stack([bias_out[0], bias_out[1]]).reshape(qv_bias.shape),
        go.T,
        bias_out[2],
        bias_out[3],
        hq,
        bias_out[4].reshape(cross_q_bias.shape),
        jnp.stack([hk, hv], axis=1),
        bias_out[5].reshape(cross_v_bias.shape),
        ho.T,
        bias_out[6],
        total_in,
        bias_out[7].reshape(mlp_in_bias.shape),
        total_out.T,
        bias_out[8],
    )


def solution(mesh):
    rows_all, by_dp = P(("dp", "head"), None), P("dp", None)
    head_dp, dp_head = P("head", "dp"), P("dp", "head")
    dp_three, vector = P("dp", None, "head"), P("dp")
    params = (
        by_dp,
        vector,
        dp_three,
        P(None, "head", "dp"),
        head_dp,
        vector,
        vector,
        dp_head,
        head_dp,
        dp_three,
        head_dp,
        head_dp,
        vector,
        dp_head,
        head_dp,
        head_dp,
        vector,
    )
    return jax.shard_map(
        on_device,
        mesh=mesh,
        in_specs=(rows_all, by_dp, by_dp, by_dp, by_dp, rows_all) + params,
        out_specs=(rows_all, rows_all, by_dp, rows_all) + params,
        check_vma=False,
    )
```

time: 1010 us -> 505 us (0.50)
  waiting for transfers between devices: 505 us -> 184 us
  blocking collectives: 174 us -> 0 us
  matrix products: 150 us -> 3.19 us
  Pallas kernels: 0 us -> 120 us
  starting transfers between devices: 1.07 us -> 119 us
  other arithmetic: 86.6 us -> 31.7 us
  local copies, waits for them, and re-layouts: 62.5 us -> 37.8 us
  between operations: 18.2 us -> 2.73 us
    reduce_scatter x9 -> x0, waiting for transfers between devices: 256 us -> none  [the longest x1 46.4 us: on_device(): lax.psum_scatter(grad_qkv, 'dp', scatter_dimension=0, tiled=True)]
    ppermute x0 -> x80, waiting for transfers between devices: none -> 183 us  [the longest x21 52.1 us: z_back(): lax.ppermute(parts[k - 1], 'head', [(s, (s - k) % n) for s in range(n)])]
    dot_general x50 -> x3, matrix products: 142 us -> 3.19 us  [the longest x1 2.62 us: on_device(): lax.dot_general(silu_cols, mod_all, (((0,), (0,)), ((), ())), preferred_e...]
    pallas_call x0 -> x6, Pallas kernels: none -> 120 us  [call(): pl.pallas_call(body, out_shape=tuple((jax.ShapeDtypeStruct(s, t) for _, s...]
    all_gather x11 -> x0, blocking collectives: 107 us -> none  [the longest x1 12.7 us: on_device(): lax.all_gather(qkv_weight, 'dp', axis=0, tiled=True)]
    all_gather x7 -> x0, waiting for transfers between devices: 104 us -> none  [the longest x1 36.1 us: on_device(): lax.all_gather(cross_grad_rows.astype(jnp.bfloat16), 'head', axis=0, tile...]
    ppermute x0 -> x80, starting transfers between devices: none -> 102 us  [the longest x15 41.4 us: z_pieces(): lax.ppermute(value, 'head', [(s, (s + k) % n) for s in range(n)])]
    psum x2 -> x0, waiting for transfers between devices: 80.5 us -> none  [the longest x1 58 us: on_device(): lax.psum(matmul(cross_attended, whole_cross_out).astype(jnp.bfloat16), 'h...]
  transfers between devices with their start and end apart: 22 -> 85, of which waited for: 17 -> 30; matrix products, arithmetic and copies ran while one was open for 21% -> 12% of each run, Pallas kernels for 0% -> 9%
where the time goes in v1:
time: 505 us; the launch traced here: 499 us
  waiting for transfers between devices  184 us (36%)
  Pallas kernels  120 us (24%)
  starting transfers between devices  119 us (24%)
  local copies, waits for them, and re-layouts  37.8 us (7%)
  other arithmetic  31.7 us (6%)
    pallas_call x6, Pallas kernels, call(): pl.pallas_call(body, out_shape=tuple((jax.ShapeDtypeStruct(s, t) for _, s...  120 us
    ppermute x21, waiting for transfers between devices, z_back(): lax.ppermute(parts[k - 1], 'head', [(s, (s - k) % n) for s in range(n)])  52.1 us
    ppermute x15, starting transfers between devices, z_pieces(): lax.ppermute(value, 'head', [(s, (s + k) % n) for s in range(n)])  41.4 us
    ppermute x4, waiting for transfers between devices, reduce(): corner = lax.ppermute(added(3).astype(BF16), 'dp', self.second)  33.6 us
    ppermute x15, waiting for transfers between devices, z_pieces(): lax.ppermute(value, 'head', [(s, (s + k) % n) for s in range(n)])  32.4 us
    ppermute x21, starting transfers between devices, z_back(): lax.ppermute(parts[k - 1], 'head', [(s, (s - k) % n) for s in range(n)])  30 us
    ppermute x4, waiting for transfers between devices, gather(): two = lax.ppermute(mine, 'dp', self.second)  27.7 us
    ppermute x4, waiting for transfers between devices, reduce(): lax.ppermute((added(1) + corner.astype(F32)).astype(BF16), 'dp', self.first)  17.1 us
  transfers between devices with their start and end apart: 85, of which 30 were waited for; matrix products, arithmetic and copies ran while one was open for 12% of the time, Pallas kernels for 9%

profile of v1, /device:TPU:0, one launch (start us, length us, event | category | flops | bytes accessed | tf_op | source)
XLA Modules:
  0.0 498.7 jit_solution(18144172112495770698)
XLA Ops:
  16.7 11.7 %collective-permute-done.4 = bf16[96,768]{1,0:T(8,128)(2,1)S(1)} collective-permute-done((bf16[96,768]{1,0:T(8,128)(2,1)S(1)}, bf16[96,768]{1,0:T(8,128)(2,1)S(1)}, u32[]{:S(2)}, u32[]{:S(2)}) %collective-permute-start.4) | collective-permute-done | bytes 147488 | tf_op jit(solution)/shard_map/ppermute | solution.py:643
  41.3 9.1 %collective-permute-start.2 = (bf16[256,768]{1,0:T(8,128)(2,1)S(1)}, bf16[256,768]{1,0:T(8,128)(2,1)}, u32[]{:S(2)}, u32[]{:S(2)}) collective-permute-start(bf16[256,768]{1,0:T(8,128)(2,1)S(1)} %copy-done.8), channel_id=1, source_target_pairs={{0,3},{1,0},{2,1},{3,2},{4,7},{5,4},{6,5},{7,6},{8,11},{9,8},{10,9... | collective-permute-start | bytes 1179656 | tf_op jit(solution)/shard_map/ppermute | solution.py:643
  56.1 9.1 %collective-permute-start.24 = (bf16[96,768]{1,0:T(8,128)(2,1)S(1)}, bf16[96,768]{1,0:T(8,128)(2,1)S(1)}, u32[]{:S(2)}, u32[]{:S(2)}) collective-permute-start(bf16[96,768]{1,0:T(8,128)(2,1)S(1)} %copy-done.15), channel_id=1, source_target_pairs={{0,2},{1,3},{2,0},{3,1},{4,6},{5,7},{6,4},{7,5},{8,10},{9,11},{10,... | collective-permute-start | bytes 442376 | tf_op jit(solution)/shard_map/ppermute | solution.py:643
  82.1 15.4 %collective-permute-done.1.refs_3_ = bf16[256,768]{1,0:T(8,128)(2,1)} collective-permute-done((bf16[256,768]{1,0:T(8,128)(2,1)S(1)}, bf16[256,768]{1,0:T(8,128)(2,1)}, u32[]{:S(2)}, u32[]{:S(2)}) %collective-permute-start.1) | collective-permute-done | bytes 393248 | tf_op jit(solution)/shard_map/ppermute | solution.py:643
  108.3 5.5 %collective-permute-done.27.refs_8_ = bf16[4,96,768]{2,1,0:T(8,128)(2,1)} collective-permute-done((bf16[4,96,768]{2,1,0:T(8,128)(2,1)}, bf16[4,96,768]{2,1,0:T(8,128)(2,1)}, u32[]{:S(2)}, u32[]{:S(2)}) %collective-permute-start.27) | collective-permute-done | bytes 589856 | tf_op jit(solution)/shard_map/ppermute | solution.py:658
  116.8 12.0 %collective-permute-done.37.refs_16_ = bf16[4,96,768]{2,1,0:T(8,128)(2,1)} collective-permute-done((bf16[4,96,768]{2,1,0:T(8,128)(2,1)S(1)}, bf16[4,96,768]{2,1,0:T(8,128)(2,1)}, u32[]{:S(2)}, u32[]{:S(2)}) %collective-permute-start.37) | collective-permute-done | bytes 589856 | tf_op jit(solution)/shard_map/ppermute | solution.py:658
  135.1 10.2 %collective-permute-done.7.refs_10_.refs_13_ = bf16[4,96,768]{2,1,0:T(8,128)(2,1)S(1)} collective-permute-done((bf16[4,96,768]{2,1,0:T(8,128)(2,1)S(1)}, bf16[4,96,768]{2,1,0:T(8,128)(2,1)S(1)}, u32[]{:S(2)}, u32[]{:S(2)}) %collective-permute-start.7) | collective-permute-done | bytes 589856 | tf_op jit(solution)/shard_map/ppermute | solution.py:658
  158.3 6.3 %collective-permute-done.8.refs_11_.refs_14_ = bf16[4,96,768]{2,1,0:T(8,128)(2,1)} collective-permute-done((bf16[4,96,768]{2,1,0:T(8,128)(2,1)}, bf16[4,96,768]{2,1,0:T(8,128)(2,1)}, u32[]{:S(2)}, u32[]{:S(2)}) %collective-permute-start.8) | collective-permute-done | bytes 589856 | tf_op jit(solution)/shard_map/ppermute | solution.py:659
  165.2 5.6 %collective-permute-done.38.refs_17_ = bf16[4,96,768]{2,1,0:T(8,128)(2,1)S(1)} collective-permute-done((bf16[4,96,768]{2,1,0:T(8,128)(2,1)}, bf16[4,96,768]{2,1,0:T(8,128)(2,1)S(1)}, u32[]{:S(2)}, u32[]{:S(2)}) %collective-permute-start.38) | collective-permute-done | bytes 589856 | tf_op jit(solution)/shard_map/ppermute | solution.py:659
  172.7 21.9 %self_forward.1 = (bf16[1024,768]{1,0:T(8,128)(2,1)}, bf16[4,1024,512]{2,1,0:T(8,128)(2,1)}, bf16[4,256,256]{2,1,0:T(8,128)(2,1)}, bf16[4,256,256]{2,1,0:T(8,128...) custom-call(s32[16]{0:T(128)} %stack.129.refs_0_, bf16[256,768]{1,0:T(8,128)(2,1)} %refs_1_.5, ...), custom_call_target="tpu_custom_call" | custom-call | flops 6000000000 | bytes 14783552 | tf_op jit(solution)/shard_map/self_forward/pallas_call | solution.py:599
  194.6 17.1 %cross_forward.1 = (bf16[4,768,512]{2,1,0:T(8,128)(2,1)}, bf16[4,256,256]{2,1,0:T(8,128)(2,1)}, bf16[4,256,256]{2,1,0:T(8,128)(2,1)}, f32[4,8,256]{2,1,0:T(8,128)}, f32[256,768]{1,0:T(8,128)}) custom-call(s32[16]{0:T(128)} %stack.129.refs_0_, f32[256,768]{1,0:T(8,128)} %get-tuple-element.62.refs_1_.refs_2_, bf16[768,768]{1,0:T(8,128)(2,1)} %refs_3_.1, ...), custom_call_target="tpu_custom_call" | custom-call | flops 5000000000 | bytes 11716672 | tf_op jit(solution)/shard_map/cross_forward/pallas_call | solution.py:599
  212.6 17.2 %feed_forward.1 = (bf16[256,768]{1,0:T(8,128)(2,1)}, f32[256,768]{1,0:T(8,128)}, bf16[4,4,96,768]{3,2,1,0:T(8,128)(2,1)}, bf16[4,4,96,768]{3,2,1,0:T(8,128)(2,1)...) custom-call(s32[16]{0:T(128)} %stack.129.refs_0_, ...), custom_call_target="tpu_custom_call" | custom-call | flops 8000000000 | bytes 21393472 | tf_op jit(solution)/shard_map/feed_forward/pallas_call | solution.py:599
  229.8 27.6 %cross_backward.1 = (bf16[4,4,96,768]{3,2,1,0:T(8,128)(2,1)}, bf16[4,4,96,768]{3,2,1,0:T(8,128)(2,1)}, f32[256,768]{1,0:T(8,128)}, bf16[256,768]{1,0:T(8,128)(2,...) custom-call(s32[16]{0:T(128)} %stack.129.refs_0_, ...), custom_call_target="tpu_custom_call" | custom-call | flops 8999999488 | bytes 19977280 | tf_op jit(solution)/shard_map/cross_backward/pallas_call | solution.py:599
  257.5 33.0 %self_backward.1 = (bf16[4,4,96,768]{3,2,1,0:T(8,128)(2,1)}, bf16[4,4,96,768]{3,2,1,0:T(8,128)(2,1)}, f32[256,768]{1,0:T(8,128)}, bf16[256,768]{1,0:T(8,128)(2,1...) custom-call(s32[16]{0:T(128)} %stack.129.refs_0_, ...), custom_call_target="tpu_custom_call" | custom-call | flops 12000000000 | bytes 20303936 | tf_op jit(solution)/shard_map/self_backward/pallas_call | solution.py:599
  317.3 11.4 %collective-permute-done.50 = bf16[192,768]{1,0:T(8,128)(2,1)} collective-permute-done((bf16[192,768]{1,0:T(8,128)(2,1)}, bf16[192,768]{1,0:T(8,128)(2,1)}, u32[]{:S(2)}, u32[]{:S(2)}) %collective-permute-start.50) | collective-permute-done | bytes 294944 | tf_op jit(solution)/shard_map/ppermute | solution.py:649
  333.3 6.4 %collective-permute-done.43.refs_5_ = bf16[256,768]{1,0:T(8,128)(2,1)} collective-permute-done((bf16[256,768]{1,0:T(8,128)(2,1)}, bf16[256,768]{1,0:T(8,128)(2,1)}, u32[]{:S(2)}, u32[]{:S(2)}) %collective-permute-start.43) | collective-permute-done | bytes 393248 | tf_op jit(solution)/shard_map/ppermute | solution.py:649
  350.9 8.1 %collective-permute-done.44.refs_6_ = bf16[256,768]{1,0:T(8,128)(2,1)} collective-permute-done((bf16[256,768]{1,0:T(8,128)(2,1)}, bf16[256,768]{1,0:T(8,128)(2,1)}, u32[]{:S(2)}, u32[]{:S(2)}) %collective-permute-start.44) | collective-permute-done | bytes 393248 | tf_op jit(solution)/shard_map/ppermute | solution.py:649
  362.5 9.5 %collective-permute-done.45.refs_7_ = bf16[256,768]{1,0:T(8,128)(2,1)S(1)} collective-permute-done((bf16[256,768]{1,0:T(8,128)(2,1)}, bf16[256,768]{1,0:T(8,128)(2,1)S(1)}, u32[]{:S(2)}, u32[]{:S(2)}) %collective-permute-start.45) | collective-permute-done | bytes 393248 | tf_op jit(solution)/shard_map/ppermute | solution.py:649
  390.2 10.6 %collective-permute-done.60 = bf16[4,96,768]{2,1,0:T(8,128)(2,1)S(1)} collective-permute-done((bf16[4,96,768]{2,1,0:T(8,128)(2,1)S(1)}, bf16[4,96,768]{2,1,0:T(8,128)(2,1)S(1)}, u32[]{:S(2)}, u32[]{:S(2)}) %collective-permute-start.60) | collective-permute-done | bytes 589856 | tf_op jit(solution)/shard_map/ppermute | solution.py:672
  402.9 16.8 %collective-permute-done.67 = bf16[4,96,768]{2,1,0:T(8,128)(2,1)S(1)} collective-permute-done((bf16[4,96,768]{2,1,0:T(8,128)(2,1)S(1)}, bf16[4,96,768]{2,1,0:T(8,128)(2,1)S(1)}, u32[]{:S(2)}, u32[]{:S(2)}) %collective-permute-start.67) | collective-permute-done | bytes 589856 | tf_op jit(solution)/shard_map/ppermute | solution.py:672
  433.7 8.6 %collective-permute-done.61 = bf16[4,96,768]{2,1,0:T(8,128)(2,1)S(1)} collective-permute-done((bf16[4,96,768]{2,1,0:T(8,128)(2,1)S(1)}, bf16[4,96,768]{2,1,0:T(8,128)(2,1)S(1)}, u32[]{:S(2)}, u32[]{:S(2)}) %collective-permute-start.61) | collective-permute-done | bytes 589856 | tf_op jit(solution)/shard_map/ppermute | solution.py:674
  463.6 6.8 %collective-permute-start.77 = (bf16[96,768]{1,0:T(8,128)(2,1)S(1)}, bf16[96,768]{1,0:T(8,128)(2,1)S(1)}, u32[]{:S(2)}, u32[]{:S(2)}) collective-permute-start(bf16[96,768]{1,0:T(8,128)(2,1)S(1)} %get-tuple-element.251), channel_id=1, source_target_pairs={{0,3},{1,0},{2,1},{3,2},{4,7},{5,4},{6,5},{7,6},{8,11},{9,8},{10,9... | collective-permute-start | bytes 442376 | tf_op jit(solution)/shard_map/ppermute | solution.py:649
  470.4 6.6 %collective-permute-done.64 = bf16[96,768]{1,0:T(8,128)(2,1)S(1)} collective-permute-done((bf16[96,768]{1,0:T(8,128)(2,1)S(1)}, bf16[96,768]{1,0:T(8,128)(2,1)S(1)}, u32[]{:S(2)}, u32[]{:S(2)}) %collective-permute-start.64) | collective-permute-done | bytes 147488 | tf_op jit(solution)/shard_map/ppermute | solution.py:649
  482.2 8.0 %collective-permute-done.71 = bf16[96,768]{1,0:T(8,128)(2,1)S(1)} collective-permute-done((bf16[96,768]{1,0:T(8,128)(2,1)S(1)}, bf16[96,768]{1,0:T(8,128)(2,1)S(1)}, u32[]{:S(2)}, u32[]{:S(2)}) %collective-permute-start.71) | collective-permute-done | bytes 147488 | tf_op jit(solution)/shard_map/ppermute | solution.py:649
  (476 shorter events, 201.4 us)
Async XLA Ops:
  29.1 37.3 %collective-permute-start.35 = (bf16[96,768]{1,0:T(8,128)(2,1)S(1)}, bf16[96,768]{1,0:T(8,128)(2,1)S(1)}, u32[]{:S(2)}, u32[]{:S(2)}) collective-permute-start(bf16[96,768]{1,0:T(8,128)(2,1)S(1)} %bitcast.263), channel_id=1, source_target_pairs={{0,3},{1,0},{2,1},{3,2},{4,7},{5,4},{6,5},{7,6},{8,11},{9,8},{10,9... | collective-permute-start | bytes 442376 | tf_op jit(solution)/shard_map/ppermute | solution.py:643
  33.9 32.6 %collective-permute-start.23 = (bf16[96,768]{1,0:T(8,128)(2,1)S(1)}, bf16[96,768]{1,0:T(8,128)(2,1)S(1)}, u32[]{:S(2)}, u32[]{:S(2)}) collective-permute-start(bf16[96,768]{1,0:T(8,128)(2,1)S(1)} %copy-done.15), channel_id=1, source_target_pairs={{0,1},{1,2},{2,3},{3,0},{4,5},{5,6},{6,7},{7,4},{8,9},{9,10},{10,1... | collective-permute-start | bytes 442376 | tf_op jit(solution)/shard_map/ppermute | solution.py:643
  38.2 30.0 %collective-permute-start.25 = (bf16[96,768]{1,0:T(8,128)(2,1)S(1)}, bf16[96,768]{1,0:T(8,128)(2,1)}, u32[]{:S(2)}, u32[]{:S(2)}) collective-permute-start(bf16[96,768]{1,0:T(8,128)(2,1)S(1)} %copy-done.15), channel_id=1, source_target_pairs={{0,3},{1,0},{2,1},{3,2},{4,7},{5,4},{6,5},{7,6},{8,11},{9,8},{10,9... | collective-permute-start | bytes 442376 | tf_op jit(solution)/shard_map/ppermute | solution.py:643
  41.3 30.1 %collective-permute-start.2 = (bf16[256,768]{1,0:T(8,128)(2,1)S(1)}, bf16[256,768]{1,0:T(8,128)(2,1)}, u32[]{:S(2)}, u32[]{:S(2)}) collective-permute-start(bf16[256,768]{1,0:T(8,128)(2,1)S(1)} %copy-done.8), channel_id=1, source_target_pairs={{0,3},{1,0},{2,1},{3,2},{4,7},{5,4},{6,5},{7,6},{8,11},{9,8},{10,9... | collective-permute-start | bytes 1179656 | tf_op jit(solution)/shard_map/ppermute | solution.py:643
  66.4 31.6 %collective-permute-start.19 = (bf16[4,96,768]{2,1,0:T(8,128)(2,1)S(1)}, bf16[4,96,768]{2,1,0:T(8,128)(2,1)}, u32[]{:S(2)}, u32[]{:S(2)}) collective-permute-start(bf16[4,96,768]{2,1,0:T(8,128)(2,1)S(1)} %pad_maximum_fusion.1.refs_6_.refs_11_), channel_id=1, source_target_pairs={{0,4},{4,0},{8,12},{12,8},{16,20},{20,16},{24,28},{28,24},{1,5},{5... | collective-permute-start | bytes 1769480 | tf_op jit(solution)/shard_map/ppermute | solution.py:661
  66.5 33.6 %collective-permute-start.17 = (bf16[4,96,768]{2,1,0:T(8,128)(2,1)S(1)}, bf16[4,96,768]{2,1,0:T(8,128)(2,1)}, u32[]{:S(2)}, u32[]{:S(2)}) collective-permute-start(bf16[4,96,768]{2,1,0:T(8,128)(2,1)S(1)} %pad_maximum_fusion.1.refs_6_.refs_11_), channel_id=1, source_target_pairs={{0,16},{4,12},{8,24},{12,4},{16,0},{20,28},{24,8},{28,20},{1,17},{... | collective-permute-start | bytes 1769480 | tf_op jit(solution)/shard_map/ppermute | solution.py:658
  68.2 31.9 %collective-permute-start.16 = (bf16[4,96,768]{2,1,0:T(8,128)(2,1)S(1)}, bf16[4,96,768]{2,1,0:T(8,128)(2,1)}, u32[]{:S(2)}, u32[]{:S(2)}) collective-permute-start(bf16[4,96,768]{2,1,0:T(8,128)(2,1)S(1)} %pad_maximum_fusion.1.refs_6_.refs_11_), channel_id=1, source_target_pairs={{0,8},{4,20},{8,0},{12,28},{16,24},{20,4},{24,16},{28,12},{1,9},{5... | collective-permute-start | bytes 1769480 | tf_op jit(solution)/shard_map/ppermute | solution.py:657
  102.3 52.4 %all-to-all-start.1 = ((f32[8,3,4608]{2,1,0:T(4,128)}), f32[8,3,4608]{2,1,0:T(4,128)S(1)}, u32[]{:S(2)}, u32[]{:S(2)}) async-start(f32[8,3,4608]{2,1,0:T(4,128)} %copy.176), calls=%async_computation.1 | async-start | bytes 1179648 | tf_op jit(solution)/shard_map/all_to_all | solution.py:814
  114.7 30.6 %collective-permute-start.7 = (bf16[4,96,768]{2,1,0:T(8,128)(2,1)S(1)}, bf16[4,96,768]{2,1,0:T(8,128)(2,1)S(1)}, u32[]{:S(2)}, u32[]{:S(2)}) collective-permute-start(bf16[4,96,768]{2,1,0:T(8,128)(2,1)S(1)} %pad_maximum_fusion.refs_8_.refs_11_), channel_id=1, source_target_pairs={{0,16},{4,12},{8,24},{12,4},{16,0},{20,28},{24,8},{28,20},{1,17},{... | collective-permute-start | bytes 1769480 | tf_op jit(solution)/shard_map/ppermute | solution.py:658
  116.1 30.2 %collective-permute-start.6 = (bf16[4,96,768]{2,1,0:T(8,128)(2,1)S(1)}, bf16[4,96,768]{2,1,0:T(8,128)(2,1)}, u32[]{:S(2)}, u32[]{:S(2)}) collective-permute-start(bf16[4,96,768]{2,1,0:T(8,128)(2,1)S(1)} %pad_maximum_fusion.refs_8_.refs_11_), channel_id=1, source_target_pairs={{0,8},{4,20},{8,0},{12,28},{16,24},{20,4},{24,16},{28,12},{1,9},{5... | collective-permute-start | bytes 1769480 | tf_op jit(solution)/shard_map/ppermute | solution.py:657
  170.8 40.9 %collective-permute-start.30 = (bf16[4,96,768]{2,1,0:T(8,128)(2,1)}, bf16[4,96,768]{2,1,0:T(8,128)(2,1)}, u32[]{:S(2)}, u32[]{:S(2)}) collective-permute-start(bf16[4,96,768]{2,1,0:T(8,128)(2,1)} %collective-permute-done.26.refs_7_), channel_id=1, source_target_pairs={{0,4},{4,0},{8,12},{12,8},{16,20},{20,16},{24,28},{28,24},{1,5},{5... | collective-permute-start | bytes 1769480 | tf_op jit(solution)/shard_map/ppermute | solution.py:661
  170.8 40.9 %collective-permute-start.40 = (bf16[4,96,768]{2,1,0:T(8,128)(2,1)S(1)}, bf16[4,96,768]{2,1,0:T(8,128)(2,1)S(1)}, u32[]{:S(2)}, u32[]{:S(2)}) collective-permute-start(bf16[4,96,768]{2,1,0:T(8,128)(2,1)S(1)} %copy-done.50), channel_id=1, source_target_pairs={{0,4},{4,0},{8,12},{12,8},{16,20},{20,16},{24,28},{28,24},{1,5},{5... | collective-permute-start | bytes 1769480 | tf_op jit(solution)/shard_map/ppermute | solution.py:661
  171.4 40.4 %collective-permute-start.41 = (bf16[4,96,768]{2,1,0:T(8,128)(2,1)}, bf16[4,96,768]{2,1,0:T(8,128)(2,1)}, u32[]{:S(2)}, u32[]{:S(2)}) collective-permute-start(bf16[4,96,768]{2,1,0:T(8,128)(2,1)} %collective-permute-done.37.refs_16_), channel_id=1, source_target_pairs={{0,4},{4,0},{8,12},{12,8},{16,20},{20,16},{24,28},{28,24},{1,5},{5... | collective-permute-start | bytes 1769480 | tf_op jit(solution)/shard_map/ppermute | solution.py:661
  171.5 40.3 %collective-permute-start.32 = (bf16[4,96,768]{2,1,0:T(8,128)(2,1)}, bf16[4,96,768]{2,1,0:T(8,128)(2,1)}, u32[]{:S(2)}, u32[]{:S(2)}) collective-permute-start(bf16[4,96,768]{2,1,0:T(8,128)(2,1)} %collective-permute-done.28.refs_9_), channel_id=1, source_target_pairs={{0,4},{4,0},{8,12},{12,8},{16,20},{20,16},{24,28},{28,24},{1,5},{5... | collective-permute-start | bytes 1769480 | tf_op jit(solution)/shard_map/ppermute | solution.py:661
  171.9 39.9 %collective-permute-start.42 = (bf16[4,96,768]{2,1,0:T(8,128)(2,1)S(1)}, bf16[4,96,768]{2,1,0:T(8,128)(2,1)}, u32[]{:S(2)}, u32[]{:S(2)}) collective-permute-start(bf16[4,96,768]{2,1,0:T(8,128)(2,1)S(1)} %collective-permute-done.38.refs_17_), channel_id=1, source_target_pairs={{0,4},{4,0},{8,12},{12,8},{16,20},{20,16},{24,28},{28,24},{1,5},{5... | collective-permute-start | bytes 1769480 | tf_op jit(solution)/shard_map/ppermute | solution.py:661
  308.4 68.1 %collective-permute-start.52 = (bf16[4,4,96,768]{3,2,1,0:T(8,128)(2,1)}, bf16[4,4,96,768]{3,2,1,0:T(8,128)(2,1)}, u32[]{:S(2)}, u32[]{:S(2)}) collective-permute-start(bf16[4,4,96,768]{3,2,1,0:T(8,128)(2,1)} %get-tuple-element.90), channel_id=1, source_target_pairs={{0,4},{4,0},{8,12},{12,8},{16,20},{20,16},{24,28},{28,24},{1,5},{5... | collective-permute-start | bytes 7077896 | tf_op jit(solution)/shard_map/ppermute | solution.py:667
  308.4 71.9 %collective-permute-start.59 = (bf16[4,4,96,768]{3,2,1,0:T(8,128)(2,1)}, bf16[4,4,96,768]{3,2,1,0:T(8,128)(2,1)}, u32[]{:S(2)}, u32[]{:S(2)}) collective-permute-start(bf16[4,4,96,768]{3,2,1,0:T(8,128)(2,1)} %get-tuple-element.98), channel_id=1, source_target_pairs={{0,4},{4,0},{8,12},{12,8},{16,20},{20,16},{24,28},{28,24},{1,5},{5... | collective-permute-start | bytes 7077896 | tf_op jit(solution)/shard_map/ppermute | solution.py:667
  309.7 73.1 %collective-permute-start.66 = (bf16[4,4,96,768]{3,2,1,0:T(8,128)(2,1)}, bf16[4,4,96,768]{3,2,1,0:T(8,128)(2,1)S(1)}, u32[]{:S(2)}, u32[]{:S(2)}) collective-permute-start(bf16[4,4,96,768]{3,2,1,0:T(8,128)(2,1)} %get-tuple-element.100), channel_id=1, source_target_pairs={{0,4},{4,0},{8,12},{12,8},{16,20},{20,16},{24,28},{28,24},{1,5},{5... | collective-permute-start | bytes 7077896 | tf_op jit(solution)/shard_map/ppermute | solution.py:667
  328.7 55.7 %collective-permute-start.73 = (bf16[4,4,96,768]{3,2,1,0:T(8,128)(2,1)}, bf16[4,4,96,768]{3,2,1,0:T(8,128)(2,1)}, u32[]{:S(2)}, u32[]{:S(2)}) collective-permute-start(bf16[4,4,96,768]{3,2,1,0:T(8,128)(2,1)} %get-tuple-element.102), channel_id=1, source_target_pairs={{0,4},{4,0},{8,12},{12,8},{16,20},{20,16},{24,28},{28,24},{1,5},{5... | collective-permute-start | bytes 7077896 | tf_op jit(solution)/shard_map/ppermute | solution.py:667
  379.0 49.2 %collective-permute-start.55 = (bf16[4,96,768]{2,1,0:T(8,128)(2,1)S(1)}, bf16[4,96,768]{2,1,0:T(8,128)(2,1)S(1)}, u32[]{:S(2)}, u32[]{:S(2)}) collective-permute-start(bf16[4,96,768]{2,1,0:T(8,128)(2,1)S(1)} %get-tuple-element.250), channel_id=1, source_target_pairs={{0,16},{4,12},{8,24},{12,4},{16,0},{20,28},{24,8},{28,20},{1,17},{... | collective-permute-start | bytes 1769480 | tf_op jit(solution)/shard_map/ppermute | solution.py:673
  382.8 48.8 %collective-permute-start.62 = (bf16[4,96,768]{2,1,0:T(8,128)(2,1)S(1)}, bf16[4,96,768]{2,1,0:T(8,128)(2,1)S(1)}, u32[]{:S(2)}, u32[]{:S(2)}) collective-permute-start(bf16[4,96,768]{2,1,0:T(8,128)(2,1)S(1)} %get-tuple-element.248), channel_id=1, source_target_pairs={{0,16},{4,12},{8,24},{12,4},{16,0},{20,28},{24,8},{28,20},{1,17},{... | collective-permute-start | bytes 1769480 | tf_op jit(solution)/shard_map/ppermute | solution.py:673
  384.4 35.3 %collective-permute-start.67 = (bf16[4,96,768]{2,1,0:T(8,128)(2,1)S(1)}, bf16[4,96,768]{2,1,0:T(8,128)(2,1)S(1)}, u32[]{:S(2)}, u32[]{:S(2)}) collective-permute-start(bf16[4,96,768]{2,1,0:T(8,128)(2,1)S(1)} %get-tuple-element.245), channel_id=1, source_target_pairs={{0,16},{4,12},{8,24},{12,4},{16,0},{20,28},{24,8},{28,20},{1,17},{... | collective-permute-start | bytes 1769480 | tf_op jit(solution)/shard_map/ppermute | solution.py:672
  388.1 37.9 %collective-permute-start.74 = (bf16[4,96,768]{2,1,0:T(8,128)(2,1)S(1)}, bf16[4,96,768]{2,1,0:T(8,128)(2,1)S(1)}, u32[]{:S(2)}, u32[]{:S(2)}) collective-permute-start(bf16[4,96,768]{2,1,0:T(8,128)(2,1)S(1)} %get-tuple-element.243), channel_id=1, source_target_pairs={{0,16},{4,12},{8,24},{12,4},{16,0},{20,28},{24,8},{28,20},{1,17},{... | collective-permute-start | bytes 1769480 | tf_op jit(solution)/shard_map/ppermute | solution.py:672
  463.6 31.1 %collective-permute-start.77 = (bf16[96,768]{1,0:T(8,128)(2,1)S(1)}, bf16[96,768]{1,0:T(8,128)(2,1)S(1)}, u32[]{:S(2)}, u32[]{:S(2)}) collective-permute-start(bf16[96,768]{1,0:T(8,128)(2,1)S(1)} %get-tuple-element.251), channel_id=1, source_target_pairs={{0,3},{1,0},{2,1},{3,2},{4,7},{5,4},{6,5},{7,6},{8,11},{9,8},{10,9... | collective-permute-start | bytes 442376 | tf_op jit(solution)/shard_map/ppermute | solution.py:649
  (125 other events, 2295.4 us)

commit v2 on v1

--- a/solution.py
+++ b/solution.py
@@ -18,6 +18,7 @@
 HIGH = lax.Precision.HIGHEST
 S_Z, S_END, S_TOK, S_OFF = 0, 1, 3, 8
 S_LEN = 16
+US = 1.15e9
 
 
 def nn(a, b):
@@ -83,18 +84,23 @@
     return pltpu.roll(value, HD, 1)
 
 
-def load_start(pieces, buffer, sems, scal, first):
+def load_start(pieces, buffer, sems, scal, col=0, low=0):
+    count, _, width = buffer.shape
     copies = []
     for j, piece in enumerate(pieces):
         rows = piece.shape[1]
         start = pl.multiple_of(scal[S_OFF + j], 32)
-        copy = pltpu.make_async_copy(piece, buffer.at[:, pl.ds(start, rows), :], sems.at[first + j])
+        copy = pltpu.make_async_copy(
+            piece.at[low : low + count, :, col : col + width],
+            buffer.at[:, pl.ds(start, rows), :],
+            sems.at[j],
+        )
         copy.start()
         copies.append(copy)
     return copies
 
 
-def store_copies(buffer, z, outs, sems, scal, first):
+def store_copies(buffer, z, outs, sems, scal, col=0, first=0):
     copies = []
     j = 0
     for out in outs:
@@ -103,7 +109,9 @@
             start = pl.multiple_of(scal[S_OFF + j], 32)
             copies.append(
                 pltpu.make_async_copy(
-                    buffer.at[z, pl.ds(start, rows), :], out.at[i, z], sems.at[first + j, z]
+                    buffer.at[z, pl.ds(start, rows), col : col + out.shape[3]],
+                    out.at[i, z],
+                    sems.at[first + j, z],
                 )
             )
             j += 1
@@ -242,7 +250,7 @@
     weights, mask, scores, probs, sems = refs[11 + splits + n_p :]
     rows = frames[0].shape[0]
     count = rows * splits
-    copies = load_start(pieces, weights, sems, scal, 0)
+    copies = load_start(pieces, weights, sems, scal)
     self_mask(scal, mask, rows, splits)
     for block in range(splits):
         clip = own_clip(scal, rows, splits, block)
@@ -289,7 +297,7 @@
     weights, mask, scores, probs, sems = refs[11 + n_p :]
     rows = after_self.shape[0]
     count = text.shape[0]
-    copies = load_start(pieces, weights, sems, scal, 0)
+    copies = load_start(pieces, weights, sems, scal, D)
     cross_mask(scal, mask, rows, splits, count // TXT)
     normed, _ = normalize(after_self[...])
     hidden = (normed * gain[...]).astype(BF16)
@@ -325,18 +333,15 @@
 
 def feed_forward(n_p, splits, *refs):
     scal, after_cross, upstream, mod, in_bias, out_bias = refs[:6]
-    in_pieces = refs[6 : 6 + n_p]
-    out_pieces = refs[6 + n_p : 6 + 2 * n_p]
-    rest = refs[6 + 2 * n_p :]
+    pieces = refs[6 : 6 + n_p]
+    rest = refs[6 + n_p :]
     n_o = 2 if n_p > 1 else 1
     layer_out, d_after = rest[:2]
-    in_grads = rest[2 : 2 + n_o]
-    out_grads = rest[2 + n_o : 2 + 2 * n_o]
+    grads_in, grads_out = rest[2 : 2 + n_o], rest[2 + n_o : 2 + 2 * n_o]
     in_bias_grad, out_bias_grad, sums = rest[2 + 2 * n_o : 5 + 2 * n_o]
-    w_in, w_out, g_in, g_out, mlp, back, load_sems, store_sems = rest[5 + 2 * n_o :]
+    weights, gbuf, mlp, back, load_sems, store_sems = rest[5 + 2 * n_o :]
     rows = after_cross.shape[0]
-    copies = load_start(in_pieces, w_in, load_sems, scal, 0)
-    copies += load_start(out_pieces, w_out, load_sems, scal, n_p)
+    copies = load_start(pieces, weights, load_sems, scal)
     clip = own_clip(scal, rows, splits)
     normed, inverse = normalize(after_cross[...])
     scale = 1.0 + per_row(mod, 4, clip)
@@ -353,9 +358,14 @@
     for copy in copies:
         copy.wait()
 
+    def stores(z):
+        return store_copies(gbuf, z, grads_in, store_sems, scal) + store_copies(
+            gbuf, z, grads_out, store_sems, scal, D, n_p
+        )
+
     def one(z, carry):
         place = shard_index(scal, z, splits)
-        pre = nn(hidden, w_in[z]) + in_bias[place]
+        pre = nn(hidden, weights[z, :, 0:D]) + in_bias[place]
         inner = 0.7978845608028654 * (pre + 0.044715 * (pre * pre * pre))
         curve = jnp.tanh(inner)
         half = 0.5 * (1.0 + curve)
@@ -363,15 +373,13 @@
         slope = half + 0.5 * pre * (1.0 - curve * curve) * 0.7978845608028654 * (
             1.0 + 3.0 * 0.044715 * pre * pre
         )
-        pre_grad = (slope * nn(low, w_out[z])).astype(BF16)
+        pre_grad = (slope * nn(low, weights[z, :, D:])).astype(BF16)
         in_bias_grad[place] = jnp.sum(pre_grad.astype(F32), axis=0, keepdims=True)
-        mlp[...] += nt(active, w_out[z])
-        back[...] += nt(pre_grad, w_in[z])
-        g_in[z] = nn(hidden_t, pre_grad).astype(BF16)
-        for copy in store_copies(g_in, z, in_grads, store_sems, scal, 0):
-            copy.start()
-        g_out[z] = nn(low_t, active).astype(BF16)
-        for copy in store_copies(g_out, z, out_grads, store_sems, scal, n_p):
+        mlp[...] += nt(active, weights[z, :, D:])
+        back[...] += nt(pre_grad, weights[z, :, 0:D])
+        gbuf[z, :, 0:D] = nn(hidden_t, pre_grad).astype(BF16)
+        gbuf[z, :, D:] = nn(low_t, active).astype(BF16)
+        for copy in stores(z):
             copy.start()
         return carry
 
@@ -385,28 +393,32 @@
     sums[:, D : 2 * D] = clip_sums(clip_row, hidden_grad * normed)
     sums[:, 2 * D :] = clip_sums(clip_row, given * branch)
     for z in range(splits):
-        for copy in store_copies(g_in, z, in_grads, store_sems, scal, 0):
+        for copy in stores(z):
             copy.wait()
-        for copy in store_copies(g_out, z, out_grads, store_sems, scal, n_p):
-            copy.wait()
-
-
-def cross_backward(n_p, splits, *refs):
+
+
+def cross_backward(n_p, splits, low, high, *refs):
     scal, d_cross, after_self, text, gain, mod, branch, kv_in, q_in, att_in, lse = refs[:11]
     pieces = refs[11 : 11 + n_p]
     rest = refs[11 + n_p :]
+    first, last = low == 0, high == splits
+    if not first:
+        back_in, text_in, bias_in = rest[:3]
+        rest = rest[3:]
     n_o = 2 if n_p > 1 else 1
     grads = rest[:n_o]
-    d_after, d_attn = rest[n_o : n_o + 2]
-    text_own = rest[n_o + 2]
-    text_parts = rest[n_o + 3 : n_o + 2 + splits]
-    bias_grad, row_grads, sums = rest[n_o + 2 + splits : n_o + 5 + splits]
-    weights, gbuf, mask, probs, dscore, key_grad, back, text_back, text_t, load_sems, store_sems = (
-        rest[n_o + 5 + splits :]
-    )
+    bias_grad = rest[n_o]
+    rest = rest[n_o + 1 :]
+    if last:
+        d_after, d_attn, text_out, row_grads, sums, back, text_back = rest[:7]
+        rest = rest[7:]
+    else:
+        back, text_back = rest[:2]
+        rest = rest[2:]
+    weights, gbuf, mask, probs, dscore, key_grad, text_t, load_sems, store_sems = rest
     rows = after_self.shape[0]
     count = text.shape[0]
-    copies = load_start(pieces, weights, load_sems, scal, 0)
+    copies = load_start(pieces, weights, load_sems, scal, D, low)
     cross_mask(scal, mask, rows, splits, count // TXT)
     normed, inverse = normalize(after_self[...])
     hidden = (normed * gain[...]).astype(BF16)
@@ -416,14 +428,19 @@
     given_t = given_wide.T.astype(BF16)
     for lo in range(0, count, 256):
         text_t[:, lo : lo + 256] = text[lo : lo + 256, :].astype(F32).T.astype(BF16)
-    back[...] = jnp.zeros_like(back)
-    text_back[...] = jnp.zeros_like(text_back)
-    row_grads[...] = jnp.zeros_like(row_grads)
-    row_grads[0:1, :] = jnp.sum(given_wide, axis=0, keepdims=True)
+    if first:
+        back[...] = jnp.zeros_like(back)
+        text_back[...] = jnp.zeros_like(text_back)
+        bias_grad[...] = jnp.zeros_like(bias_grad)
+    else:
+        back[...] = back_in[...]
+        text_back[...] = text_in[...]
+        bias_grad[...] = bias_in[...]
     for copy in copies:
         copy.wait()
 
-    def one(z, carry):
+    def one(i, carry):
+        z = i + low
         place = shard_index(scal, z, splits)
 
         def kv(lo, hi, col):
@@ -435,7 +452,7 @@
             key_grad[lo:hi, 2 * WIN : 3 * WIN] = k2.astype(BF16)
             key_grad[lo:hi, 3 * WIN : 4 * WIN] = v2.astype(BF16)
 
-        head_grad = nn(given, weights[z, :, 4 * WIN :]).astype(BF16)
+        head_grad = nn(given, weights[i, :, 4 * WIN :]).astype(BF16)
         totals = [lse[z, h : h + 1, :] for h in range(3)]
         pair, third = attend_back(
             q_in[z], kv, head_grad, mask, totals, probs, dscore, count, put
@@ -443,19 +460,19 @@
         pair, third = pair.astype(BF16), third.astype(BF16)
         part = nn(text_t[...], key_grad[...])
         out_part = nn(given_t, att_in[z])
-        gbuf[z, :, 0:WIN] = nn(hidden_t, pair).astype(BF16)
-        gbuf[z, :, WIN : 3 * WIN] = part[:, 0 : 2 * WIN].astype(BF16)
-        gbuf[z, :, 3 * WIN : 4 * WIN] = (
+        gbuf[i, :, 0:WIN] = nn(hidden_t, pair).astype(BF16)
+        gbuf[i, :, WIN : 3 * WIN] = part[:, 0 : 2 * WIN].astype(BF16)
+        gbuf[i, :, 3 * WIN : 4 * WIN] = (
             part[:, 2 * WIN : 3 * WIN] + nn(hidden_t, third)
         ).astype(BF16)
-        gbuf[z, :, 4 * WIN : 5 * WIN] = (part[:, 3 * WIN :] + out_part[:, 0:WIN]).astype(BF16)
-        gbuf[z, :, 5 * WIN :] = out_part[:, WIN:].astype(BF16)
-        for copy in store_copies(gbuf, z, grads, store_sems, scal, 0):
+        gbuf[i, :, 4 * WIN : 5 * WIN] = (part[:, 3 * WIN :] + out_part[:, 0:WIN]).astype(BF16)
+        gbuf[i, :, 5 * WIN :] = out_part[:, WIN:].astype(BF16)
+        for copy in store_copies(gbuf, i, grads, store_sems, scal):
             copy.start()
-        back[...] += nt(pair, weights[z, :, 0:WIN]) + nt(third, weights[z, :, 3 * WIN : 4 * WIN])
+        back[...] += nt(pair, weights[i, :, 0:WIN]) + nt(third, weights[i, :, 3 * WIN : 4 * WIN])
         for lo in range(0, count, 256):
             text_back[lo : lo + 256, :] += nt(
-                key_grad[lo : lo + 256, :], weights[z, :, WIN : 5 * WIN]
+                key_grad[lo : lo + 256, :], weights[i, :, WIN : 5 * WIN]
             )
         key_sums = jnp.sum(key_grad[...].astype(F32), axis=0, keepdims=True)
         bias_grad[place, :, 0:WIN] = jnp.sum(pair.astype(F32), axis=0, keepdims=True)
@@ -467,7 +484,14 @@
         bias_grad[place, :, 5 * WIN :] = jnp.zeros((1, WIN), F32)
         return carry
 
-    lax.fori_loop(0, splits, one, 0)
+    lax.fori_loop(0, high - low, one, 0)
+    for i in range(high - low):
+        for copy in store_copies(gbuf, i, grads, store_sems, scal):
+            copy.wait()
+    if not last:
+        return
+    row_grads[...] = jnp.zeros_like(row_grads)
+    row_grads[0:1, :] = jnp.sum(given_wide, axis=0, keepdims=True)
     hidden_grad = back[...]
     row_grads[1:2, :] = jnp.sum(hidden_grad * normed, axis=0, keepdims=True)
     total = d_cross[...] + normalize_back(hidden_grad * gain[...], normed, inverse)
@@ -475,49 +499,52 @@
     clip = own_clip(scal, rows, splits)
     d_attn[...] = (total * per_row(mod, 2, clip)).astype(BF16)
     sums[...] = clip_sums(own_clip_row(scal, rows, splits), total * branch[...])
-    height = count // splits
-    for k in range(splits):
-        start = pl.multiple_of(shard_index(scal, k, splits) * height, 64)
-        block = text_back[pl.ds(start, height), :]
-        if k == 0:
-            text_own[...] = block
-        else:
-            text_parts[k - 1][...] = block.astype(BF16)
-    for z in range(splits):
-        for copy in store_copies(gbuf, z, grads, store_sems, scal, 0):
-            copy.wait()
-
-
-def self_backward(n_p, splits, *refs):
+    text_out[...] = text_back[...].astype(BF16)
+
+
+def self_backward(n_p, splits, low, high, *refs):
     scal = refs[0]
     frames = refs[1 : 1 + splits]
     given_ref, hidden, kv_in, q_in, att_in, lse = refs[1 + splits : 7 + splits]
     pieces = refs[7 + splits : 7 + splits + n_p]
     rest = refs[7 + splits + n_p :]
+    first, last = low == 0, high == splits
+    if not first:
+        back_in, bias_in = rest[:2]
+        rest = rest[2:]
     n_o = 2 if n_p > 1 else 1
     grads = rest[:n_o]
-    own = rest[n_o]
-    parts = rest[n_o + 1 : n_o + splits]
-    bias_grad, row_grads, sums = rest[n_o + splits : n_o + 3 + splits]
-    weights, gbuf, mask, probs, dscore, key_grad, back, hidden_t, load_sems, store_sems = rest[
-        n_o + 3 + splits :
-    ]
+    bias_grad = rest[n_o]
+    rest = rest[n_o + 1 :]
+    if last:
+        own = rest[0]
+        parts = rest[1:splits]
+        row_grads, sums, back = rest[splits : splits + 3]
+        rest = rest[splits + 3 :]
+    else:
+        back = rest[0]
+        rest = rest[1:]
+    weights, gbuf, mask, probs, dscore, key_grad, hidden_t, load_sems, store_sems = rest
     rows = frames[0].shape[0]
     count = rows * splits
-    copies = load_start(pieces, weights, load_sems, scal, 0)
+    copies = load_start(pieces, weights, load_sems, scal, 0, low)
     self_mask(scal, mask, rows, splits)
     given = given_ref[...]
     given_wide = given.astype(F32)
     given_t = given_wide.T.astype(BF16)
     for lo in range(0, count, 256):
         hidden_t[:, lo : lo + 256] = hidden[lo : lo + 256, :].astype(F32).T.astype(BF16)
-    back[...] = jnp.zeros_like(back)
-    row_grads[...] = jnp.zeros_like(row_grads)
-    row_grads[0:1, :] = jnp.sum(given_wide, axis=0, keepdims=True)
+    if first:
+        back[...] = jnp.zeros_like(back)
+        bias_grad[...] = jnp.zeros_like(bias_grad)
+    else:
+        back[...] = back_in[...]
+        bias_grad[...] = bias_in[...]
     for copy in copies:
         copy.wait()
 
-    def one(z, carry):
+    def one(i, carry):
+        z = i + low
         place = shard_index(scal, z, splits)
 
         def kv(lo, hi, col):
@@ -529,7 +556,7 @@
             key_grad[lo:hi, 2 * WIN : 3 * WIN] = k2.astype(BF16)
             key_grad[lo:hi, 3 * WIN : 4 * WIN] = v2.astype(BF16)
 
-        head_grad = nn(given, weights[z, :, 4 * WIN :]).astype(BF16)
+        head_grad = nn(given, weights[i, :, 4 * WIN :]).astype(BF16)
         totals = [lse[z, h : h + 1, :] for h in range(3)]
         pair, third = attend_back(
             q_in[z], kv, head_grad, mask, totals, probs, dscore, count, put
@@ -540,24 +567,31 @@
         ).astype(BF16)
         part = nn(hidden_t[...], key_grad[...])
         out_part = nn(given_t, att_in[z])
-        gbuf[z, :, 0:WIN] = nn(hidden_t[:, 0:rows], pair).astype(BF16)
-        gbuf[z, :, WIN : 4 * WIN] = part[:, 0 : 3 * WIN].astype(BF16)
-        gbuf[z, :, 4 * WIN : 5 * WIN] = (part[:, 3 * WIN :] + out_part[:, 0:WIN]).astype(BF16)
-        gbuf[z, :, 5 * WIN :] = out_part[:, WIN:].astype(BF16)
-        for copy in store_copies(gbuf, z, grads, store_sems, scal, 0):
+        gbuf[i, :, 0:WIN] = nn(hidden_t[:, 0:rows], pair).astype(BF16)
+        gbuf[i, :, WIN : 4 * WIN] = part[:, 0 : 3 * WIN].astype(BF16)
+        gbuf[i, :, 4 * WIN : 5 * WIN] = (part[:, 3 * WIN :] + out_part[:, 0:WIN]).astype(BF16)
+        gbuf[i, :, 5 * WIN :] = out_part[:, WIN:].astype(BF16)
+        for copy in store_copies(gbuf, i, grads, store_sems, scal):
             copy.start()
         for lo in range(0, count, 256):
             back[lo : lo + 256, :] += nt(
-                key_grad[lo : lo + 256, :], weights[z, :, WIN : 5 * WIN]
+                key_grad[lo : lo + 256, :], weights[i, :, WIN : 5 * WIN]
             )
-        back[0:rows, :] += nt(pair, weights[z, :, 0:WIN])
+        back[0:rows, :] += nt(pair, weights[i, :, 0:WIN])
         key_sums = jnp.sum(key_grad[...].astype(F32), axis=0, keepdims=True)
         bias_grad[place, :, 0:WIN] = jnp.sum(pair.astype(F32), axis=0, keepdims=True)
         bias_grad[place, :, WIN : 5 * WIN] = key_sums
         bias_grad[place, :, 5 * WIN :] = jnp.zeros((1, WIN), F32)
         return carry
 
-    lax.fori_loop(0, splits, one, 0)
+    lax.fori_loop(0, high - low, one, 0)
+    for i in range(high - low):
+        for copy in store_copies(gbuf, i, grads, store_sems, scal):
+            copy.wait()
+    if not last:
+        return
+    row_grads[...] = jnp.zeros_like(row_grads)
+    row_grads[0:1, :] = jnp.sum(given_wide, axis=0, keepdims=True)
     shift = jnp.zeros((8, D), F32)
     scale = jnp.zeros((8, D), F32)
     for block in range(splits):
@@ -572,9 +606,6 @@
         scale = scale + clip_sums(clip_row, value * normed)
     sums[:, 0:D] = shift
     sums[:, D:] = scale
-    for z in range(splits):
-        for copy in store_copies(gbuf, z, grads, store_sems, scal, 0):
-            copy.wait()
 
 
 def finish(splits, *refs):
@@ -650,35 +681,44 @@
             for k in range(1, n)
         ]
 
-    def gather(self, shard):
-        mine = jnp.stack(self.z_pieces(shard))
+    def gather_z(self, shard):
+        return jnp.stack(self.z_pieces(shard))
+
+    def across(self, value, how):
+        return lax.ppermute(value, "dp", how)
+
+    def gather(self, mine):
         if not self.square:
             return [lax.all_gather(mine, "dp", axis=1, tiled=True)]
-        one = lax.ppermute(mine, "dp", self.first)
-        two = lax.ppermute(mine, "dp", self.second)
-        three = lax.ppermute(one, "dp", self.second)
+        one = self.across(mine, self.first)
+        two = self.across(mine, self.second)
+        three = self.across(one, self.second)
         kept = [mine, one, two, three]
-        return kept + [lax.ppermute(k, "dp", self.core) for k in kept]
-
-    def reduce(self, grads):
-        if not self.square:
-            mine = lax.psum_scatter(grads[0][0], "dp", scatter_dimension=1, tiled=True)
-        else:
-            other = lax.ppermute(grads[1], "dp", self.core)
-
-            def added(i):
-                return grads[0][i].astype(F32) + other[i].astype(F32)
-
-            corner = lax.ppermute(added(3).astype(BF16), "dp", self.second)
-            two = lax.ppermute(added(2).astype(BF16), "dp", self.second)
-            one = lax.ppermute((added(1) + corner.astype(F32)).astype(BF16), "dp", self.first)
-            mine = added(0) + one.astype(F32) + two.astype(F32)
-        mine = mine.astype(F32)
+        return kept + [self.across(k, self.core) for k in kept]
+
+    def send_second(self, blocks):
+        return self.across(blocks[2:4].astype(BF16), self.second)
+
+    def send_first(self, blocks):
+        return self.across(blocks[1].astype(BF16), self.first)
+
+    def reduce_z(self, mine):
         arrived = self.z_back([mine[k].astype(BF16) for k in range(1, self.splits)])
         total = mine[0]
         for part in arrived:
             total = total + part.astype(F32)
         return total
+
+    def reduce_other(self, grads):
+        return lax.psum_scatter(grads[0][0], "dp", scatter_dimension=1, tiled=True).astype(F32)
+
+
+def wide_sum(a, b):
+    return a.astype(F32) + b.astype(F32)
+
+
+def tie(value, *others):
+    return lax.optimization_barrier((value,) + others)[0]
 
 
 def to_layout(q, k, v, o):
@@ -815,10 +855,15 @@
     mod = jnp.sum(mod_got, axis=0) + all_ada_bias
 
     frame_blocks = ring.z_pieces(frames_in)
-    pieces_self = ring.gather(shard_self)
-    pieces_cross = ring.gather(shard_cross)
-    pieces_in = ring.gather(mlp_in_weight)
-    pieces_out = ring.gather(mlp_out_weight.T)
+    pieces_attn = ring.gather(
+        ring.gather_z(jnp.concatenate([shard_self, shard_cross], axis=1))
+    )
+    mlp_mine = ring.gather_z(jnp.concatenate([mlp_in_weight, mlp_out_weight.T], axis=1))
+    if ring.square:
+        mlp_one = ring.across(mlp_mine, ring.first)
+        mlp_two = ring.across(mlp_mine, ring.second)
+    else:
+        pieces_mlp = ring.gather(mlp_mine)
 
     def dma(n):
         return pltpu.SemaphoreType.DMA(n)
@@ -839,7 +884,7 @@
         [("s", scal)]
         + vmem_of(frame_blocks)
         + vmem_of([mod, bias_self, all_attn_bias])
-        + any_of(pieces_self),
+        + any_of(pieces_attn),
         [
             ("v", (count, D), BF16),
             ("v", (splits, count, 4 * WIN), BF16),
@@ -856,14 +901,19 @@
             pltpu.VMEM((count, rows), BF16),
             dma((n_p,)),
         ],
-        6e9,
+        22 * US,
         "self_forward",
     )
+    if ring.square:
+        mlp_mine, mlp_one, mlp_two = (tie(v, after_self) for v in (mlp_mine, mlp_one, mlp_two))
+        after_self = tie(after_self, mlp_one, mlp_two)
+        mlp_three = ring.across(mlp_one, ring.second)
+        mlp_other = [ring.across(v, ring.core) for v in (mlp_mine, mlp_one, mlp_two)]
     cross_kv, cross_q, cross_att, cross_lse, after_cross = call(
         partial(cross_forward, n_p, splits),
         [("s", scal)]
         + vmem_of([after_self, text_feats, all_gain, bias_cross, all_cross_bias])
-        + any_of(pieces_cross),
+        + any_of(pieces_attn),
         [
             ("v", (splits, text_count, 4 * WIN), BF16),
             ("v", (splits, rows, 2 * WIN), BF16),
@@ -878,15 +928,19 @@
             pltpu.VMEM((text_count, rows), BF16),
             dma((n_p,)),
         ],
-        5e9,
+        17 * US,
         "cross_forward",
     )
+    if ring.square:
+        mlp_three = tie(mlp_three, after_cross)
+        after_cross = tie(after_cross, mlp_three)
+        pieces_mlp = [mlp_mine, mlp_one, mlp_two, mlp_three] + mlp_other
+        pieces_mlp.append(ring.across(mlp_three, ring.core))
     results = call(
         partial(feed_forward, n_p, splits),
         [("s", scal)]
         + vmem_of([after_cross, out_grad, mod, all_in_bias, all_out_bias])
-        + any_of(pieces_in)
-        + any_of(pieces_out),
+        + any_of(pieces_mlp),
         [("v", (rows, D), BF16), ("v", (rows, D), F32)]
         + kept_out
         + kept_out
@@ -896,94 +950,143 @@
             ("v", (8, 3 * D), F32),
         ],
         [
-            shard_type,
-            shard_type,
-            shard_type,
-            shard_type,
+            pltpu.VMEM((splits, D, 2 * D), BF16),
+            pltpu.VMEM((splits, D, 2 * D), BF16),
             pltpu.VMEM((rows, D), F32),
             pltpu.VMEM((rows, D), F32),
-            dma((2 * n_p,)),
+            dma((n_p,)),
             dma((2 * n_p, splits)),
         ],
-        8e9,
+        17 * US,
         "feed_forward",
     )
     layer_out, d_after_cross = results[:2]
-    grads_in = results[2 : 2 + n_o]
-    grads_out = results[2 + n_o : 2 + 2 * n_o]
+    grads_in, grads_out = results[2 : 2 + n_o], results[2 + n_o : 2 + 2 * n_o]
     in_bias_grad, out_bias_grad, sums_two = results[2 + 2 * n_o :]
-    height = text_count // splits
+    half = splits // 2
+    kept_half = [(m, (shape[0], half) + shape[2:], kind) for m, shape, kind in kept_out]
+    half_type = pltpu.VMEM((half, D, D), BF16)
+
+    def back_scratch(keys):
+        return [
+            half_type,
+            half_type,
+            pltpu.VMEM((keys, rows), F32),
+            pltpu.VMEM((3, keys, rows), F32),
+            pltpu.VMEM((3, keys, rows), F32),
+            pltpu.VMEM((keys, 4 * WIN), BF16),
+            pltpu.VMEM((D, keys), BF16),
+            dma((n_p,)),
+            dma((n_p, half)),
+        ]
+
+    if ring.square:
+        core_in = ring.across(grads_in[1], ring.core)
+        core_out = ring.across(grads_out[1], ring.core)
+    cross_args = [
+        d_after_cross,
+        after_self,
+        text_feats,
+        all_gain,
+        mod,
+        attn_branch,
+        cross_kv,
+        cross_q,
+        cross_att,
+        cross_lse,
+    ]
+    cross_state = [("v", (rows, D), F32), ("v", (text_count, D), F32)]
+    bias_type = [("v", (splits, 1, D), F32)]
     results = call(
-        partial(cross_backward, n_p, splits),
+        partial(cross_backward, n_p, splits, 0, half),
+        [("s", scal)] + vmem_of(cross_args) + any_of(pieces_attn),
+        kept_half + bias_type + cross_state,
+        back_scratch(text_count),
+        14 * US,
+        "cross_backward_first",
+    )
+    grads_cross = [results[:n_o]]
+    cross_bias_grad, cross_back, text_back = results[n_o:]
+    if ring.square:
+        core_in, core_out = tie(core_in, cross_back), tie(core_out, cross_back)
+        cross_back = tie(cross_back, core_in, core_out)
+        blocks_in = wide_sum(grads_in[0], core_in)
+        blocks_out = wide_sum(grads_out[0], core_out)
+        far_in = ring.send_second(blocks_in)
+        core_cross = [ring.across(grads_cross[0][1], ring.core)]
+    results = call(
+        partial(cross_backward, n_p, splits, half, splits),
         [("s", scal)]
-        + vmem_of(
-            [
-                d_after_cross,
-                after_self,
-                text_feats,
-                all_gain,
-                mod,
-                attn_branch,
-                cross_kv,
-                cross_q,
-                cross_att,
-                cross_lse,
-            ]
+        + vmem_of(cross_args)
+        + any_of(pieces_attn)
+        + vmem_of([cross_back, text_back, cross_bias_grad]),
+        kept_half
+        + bias_type
+        + [
+            ("v", (rows, D), F32),
+            ("v", (rows, D), BF16),
+            ("v", (text_count, D), BF16),
+            ("v", (8, D), F32),
+            ("v", (8, D), F32),
+        ],
+        [pltpu.VMEM((rows, D), F32), pltpu.VMEM((text_count, D), F32)] + back_scratch(text_count),
+        15 * US,
+        "cross_backward_last",
+    )
+    grads_cross.append(results[:n_o])
+    cross_bias_grad, d_after_self, d_attn, text_out, cross_rows, gate_sums = results[n_o:]
+    self_args = [d_attn, hidden_one, self_kv, self_q, self_att, self_lse]
+    if ring.square:
+        far_in = tie(far_in, d_attn)
+        core_cross[0] = tie(core_cross[0], d_attn)
+        d_attn = tie(d_attn, far_in, core_cross[0])
+        self_args[0] = d_attn
+        blocks_in = wide_sum(blocks_in[0:2], far_in)
+        near_in = ring.send_first(blocks_in)
+        far_out = ring.send_second(tie(blocks_out, d_attn))
+        core_cross.append(ring.across(grads_cross[1][1], ring.core))
+    results = call(
+        partial(self_backward, n_p, splits, 0, half),
+        [("s", scal)] + vmem_of(frame_blocks) + vmem_of(self_args) + any_of(pieces_attn),
+        kept_half + bias_type + [("v", (count, D), F32)],
+        back_scratch(count),
+        17 * US,
+        "self_backward_first",
+    )
+    grads_self = [results[:n_o]]
+    self_bias_grad, self_back = results[n_o:]
+    if ring.square:
+        near_in, far_out = tie(near_in, self_back), tie(far_out, self_back)
+        core_cross[1] = tie(core_cross[1], self_back)
+        self_back = tie(self_back, near_in, far_out, core_cross[1])
+        shard_in = wide_sum(blocks_in[0], near_in)
+        blocks_out = wide_sum(blocks_out[0:2], far_out)
+        near_out = ring.send_first(blocks_out)
+        blocks_cross = jnp.concatenate(
+            [wide_sum(g[0], c) for g, c in zip(grads_cross, core_cross)], axis=1
         )
-        + any_of(pieces_cross),
-        kept_out
-        + [("v", (rows, D), F32), ("v", (rows, D), BF16), ("v", (height, D), F32)]
-        + [("v", (height, D), BF16)] * (splits - 1)
-        + [("v", (splits, 1, D), F32), ("v", (8, D), F32), ("v", (8, D), F32)],
-        [
-            shard_type,
-            shard_type,
-            pltpu.VMEM((text_count, rows), F32),
-            pltpu.VMEM((3, text_count, rows), F32),
-            pltpu.VMEM((3, text_count, rows), F32),
-            pltpu.VMEM((text_count, 4 * WIN), BF16),
-            pltpu.VMEM((rows, D), F32),
-            pltpu.VMEM((text_count, D), F32),
-            pltpu.VMEM((D, text_count), BF16),
-            dma((n_p,)),
-            dma((n_p, splits)),
-        ],
-        9e9,
-        "cross_backward",
-    )
-    grads_cross = results[:n_o]
-    d_after_self, d_attn, text_own = results[n_o : n_o + 3]
-    text_parts = results[n_o + 3 : n_o + 2 + splits]
-    cross_bias_grad, cross_rows, gate_sums = results[n_o + 2 + splits :]
+        far_cross = ring.send_second(blocks_cross)
+        core_self = [ring.across(grads_self[0][1], ring.core)]
     results = call(
-        partial(self_backward, n_p, splits),
+        partial(self_backward, n_p, splits, half, splits),
         [("s", scal)]
         + vmem_of(frame_blocks)
-        + vmem_of([d_attn, hidden_one, self_kv, self_q, self_att, self_lse])
-        + any_of(pieces_self),
-        kept_out
+        + vmem_of(self_args)
+        + any_of(pieces_attn)
+        + vmem_of([self_back, self_bias_grad]),
+        kept_half
+        + bias_type
         + [("v", (rows, D), F32)]
         + [("v", (rows, D), BF16)] * (splits - 1)
-        + [("v", (splits, 1, D), F32), ("v", (8, D), F32), ("v", (8, 2 * D), F32)],
-        [
-            shard_type,
-            shard_type,
-            pltpu.VMEM((count, rows), F32),
-            pltpu.VMEM((3, count, rows), F32),
-            pltpu.VMEM((3, count, rows), F32),
-            pltpu.VMEM((count, 4 * WIN), BF16),
-            pltpu.VMEM((count, D), F32),
-            pltpu.VMEM((D, count), BF16),
-            dma((n_p,)),
-            dma((n_p, splits)),
-        ],
-        12e9,
-        "self_backward",
-    )
-    grads_self = results[:n_o]
-    own_part = results[n_o]
-    parts = results[n_o + 1 : n_o + splits]
-    self_bias_grad, self_rows, sums_one = results[n_o + splits :]
+        + [("v", (8, D), F32), ("v", (8, 2 * D), F32)],
+        [pltpu.VMEM((count, D), F32)] + back_scratch(count),
+        18 * US,
+        "self_backward_last",
+    )
+    grads_self.append(results[:n_o])
+    self_bias_grad, own_part = results[n_o : n_o + 2]
+    parts = results[n_o + 2 : n_o + 1 + splits]
+    self_rows, sums_one = results[n_o + 1 + splits :]
 
     arrived = ring.z_back(parts)
     (frames_grad,) = call(
@@ -991,12 +1094,13 @@
         [("s", scal)] + vmem_of([frames_in, mod, d_after_self, own_part]) + vmem_of(arrived),
         [("v", (rows, D), F32)],
         [],
-        1e8,
+        3 * US,
         "finish",
     )
-    text_grad = text_own
-    for part in ring.z_back(text_parts):
-        text_grad = text_grad + part.astype(F32)
+    text_got = lax.all_to_all(
+        text_out.reshape(splits, text_count // splits, D), "head", 0, 0, tiled=True
+    )
+    text_grad = jnp.sum(text_got.astype(F32), axis=0)
 
     mod_partial = jnp.concatenate([sums_one, gate_sums, sums_two], axis=1)[:clips]
     mod_sum = mod_partial
@@ -1051,10 +1155,28 @@
         bias_out.append(bias_sum[place : place + e.shape[2]])
         place += e.shape[2]
 
-    total_in = ring.reduce(grads_in)
-    total_out = ring.reduce(grads_out)
-    total_cross = ring.reduce(grads_cross)
-    total_self = ring.reduce(grads_self)
+    if ring.square:
+        total_in = ring.reduce_z(shard_in)
+        total_out = ring.reduce_z(wide_sum(blocks_out[0], near_out))
+        blocks_cross = wide_sum(blocks_cross[0:2], far_cross)
+        total_cross = ring.reduce_z(wide_sum(blocks_cross[0], ring.send_first(blocks_cross)))
+        core_self.append(ring.across(grads_self[1][1], ring.core))
+        blocks_self = jnp.concatenate(
+            [wide_sum(g[0], c) for g, c in zip(grads_self, core_self)], axis=1
+        )
+        blocks_self = wide_sum(blocks_self[0:2], ring.send_second(blocks_self))
+        total_self = ring.reduce_z(wide_sum(blocks_self[0], ring.send_first(blocks_self)))
+    else:
+
+        def joined(halves):
+            return ring.reduce_z(
+                jnp.concatenate([ring.reduce_other(h) for h in halves], axis=0)
+            )
+
+        total_in = joined([grads_in])
+        total_out = joined([grads_out])
+        total_cross = joined(grads_cross)
+        total_self = joined(grads_self)
     gq, gk, gv, go = from_layout(total_self)
     hq, hk, hv, ho = from_layout(total_cross)
     return (

time: 505 us -> 434 us (0.86)
  waiting for transfers between devices: 184 us -> 104 us
  starting transfers between devices: 119 us -> 87.8 us
  Pallas kernels: 120 us -> 134 us
  other arithmetic: 31.7 us -> 45.5 us
  local copies, waits for them, and re-layouts: 37.8 us -> 49.1 us
    ppermute x44 -> x28, waiting for transfers between devices: 98.4 us -> 26.1 us  [across(): return lax.ppermute(value, 'dp', how)]
    ppermute x21 -> x18, waiting for transfers between devices: 52.1 us -> 16.3 us  [z_back(): lax.ppermute(parts[k - 1], 'head', [(s, (s - k) % n) for s in range(n)])]
    ppermute x15 -> x9, starting transfers between devices: 41.4 us -> 12.6 us  [z_pieces(): lax.ppermute(value, 'head', [(s, (s + k) % n) for s in range(n)])]
    add x4 -> x13, other arithmetic: 3.08 us -> 23.4 us  [the longest x10 21.4 us: wide_sum(): return a.astype(F32) + b.astype(F32)]
    all_to_all x1, waiting for transfers between devices: 0.01 us -> 14.5 us  [on_device(): got = lax.all_to_all(sent, both, 0, 0, tiled=True).reshape(n_dp, splits, -1)]
    pallas_call x6 -> x8, Pallas kernels: 120 us -> 134 us  [call(): pl.pallas_call(body, out_shape=tuple((jax.ShapeDtypeStruct(s, t) for _, s...]
    ppermute x15 -> x9, waiting for transfers between devices: 32.4 us -> 44.9 us  [z_pieces(): lax.ppermute(value, 'head', [(s, (s + k) % n) for s in range(n)])]
    ppermute x44 -> x28, starting transfers between devices: 30.6 us -> 20.7 us  [across(): return lax.ppermute(value, 'dp', how)]
  transfers between devices with their start and end apart: 85 -> 61, of which waited for: 30 -> 19; matrix products, arithmetic and copies ran while one was open for 12% -> 21% of each run, Pallas kernels for 9% -> 27%
where the time goes in v2:
time: 434 us; the launch traced here: 426 us
  Pallas kernels  134 us (31%)
  waiting for transfers between devices  104 us (24%)
  starting transfers between devices  87.8 us (20%)
  local copies, waits for them, and re-layouts  49.1 us (11%)
  other arithmetic  45.5 us (10%)
    pallas_call x8, Pallas kernels, call(): pl.pallas_call(body, out_shape=tuple((jax.ShapeDtypeStruct(s, t) for _, s...  134 us
    ppermute x9, waiting for transfers between devices, z_pieces(): lax.ppermute(value, 'head', [(s, (s + k) % n) for s in range(n)])  44.9 us
    ppermute x18, starting transfers between devices, z_back(): lax.ppermute(parts[k - 1], 'head', [(s, (s - k) % n) for s in range(n)])  32.8 us
    ppermute x28, waiting for transfers between devices, across(): return lax.ppermute(value, 'dp', how)  26.1 us
    add x10, other arithmetic, wide_sum(): return a.astype(F32) + b.astype(F32)  21.4 us
    ppermute x28, starting transfers between devices, across(): return lax.ppermute(value, 'dp', how)  20.7 us
    ppermute x18, waiting for transfers between devices, z_back(): lax.ppermute(parts[k - 1], 'head', [(s, (s - k) % n) for s in range(n)])  16.3 us
    all_to_all x1, waiting for transfers between devices, on_device(): got = lax.all_to_all(sent, both, 0, 0, tiled=True).reshape(n_dp, splits, -1)  14.5 us
  transfers between devices with their start and end apart: 61, of which 19 were waited for; matrix products, arithmetic and copies ran while one was open for 21% of the time, Pallas kernels for 27%

profile of v2, /device:TPU:0, one launch (start us, length us, event | category | flops | bytes accessed | tf_op | source)
XLA Modules:
  0.0 425.6 jit_solution(11454011161343129816)
XLA Ops:
  4.1 5.1 %collective-permute-start.5 = (bf16[96,1536]{1,0:T(8,128)(2,1)S(1)}, bf16[96,1536]{1,0:T(8,128)(2,1)S(1)}, u32[]{:S(2)}, u32[]{:S(2)}) collective-permute-start(bf16[96,1536]{1,0:T(8,128)(2,1)S(1)} %concatenate.89), channel_id=1, source_target_pairs={{0,3},{1,0},{2,1},{3,2},{4,7},{5,4},{6,5},{7,6},{8,11},{9,8},{10,9... | collective-permute-start | bytes 884744 | tf_op jit(solution)/shard_map/ppermute | solution.py:674
  10.3 6.4 %collective-permute-done.5 = bf16[96,1536]{1,0:T(8,128)(2,1)S(1)} collective-permute-done((bf16[96,1536]{1,0:T(8,128)(2,1)S(1)}, bf16[96,1536]{1,0:T(8,128)(2,1)S(1)}, u32[]{:S(2)}, u32[]{:S(2)}) %collective-permute-start.5) | collective-permute-done | bytes 294944 | tf_op jit(solution)/shard_map/ppermute | solution.py:674
  16.7 17.7 %collective-permute-done.4 = bf16[96,1536]{1,0:T(8,128)(2,1)S(1)} collective-permute-done((bf16[96,1536]{1,0:T(8,128)(2,1)S(1)}, bf16[96,1536]{1,0:T(8,128)(2,1)S(1)}, u32[]{:S(2)}, u32[]{:S(2)}) %collective-permute-start.4) | collective-permute-done | bytes 294944 | tf_op jit(solution)/shard_map/ppermute | solution.py:674
  49.7 3.8 stack.99.refs_0_
  53.5 14.5 %all-to-all-done = bf16[32,2,720]{2,1,0:T(2,128)(2,1)S(1)} async-done(((bf16[32,2,720]{2,1,0:T(2,128)(2,1)}), bf16[32,2,720]{2,1,0:T(2,128)(2,1)S(1)}, u32[]{:S(2)}, u32[]{:S(2)}) %all-to-all-start) | async-done | bytes 92192 | tf_op jit(solution)/shard_map/all_to_all | solution.py:823
  82.1 8.4 %collective-permute-done.refs_2_ = bf16[256,768]{1,0:T(8,128)(2,1)} collective-permute-done((bf16[256,768]{1,0:T(8,128)(2,1)}, bf16[256,768]{1,0:T(8,128)(2,1)}, u32[]{:S(2)}, u32[]{:S(2)}) %collective-permute-start) | collective-permute-done | bytes 393248 | tf_op jit(solution)/shard_map/ppermute | solution.py:674
  91.0 10.0 %collective-permute-done.8.refs_11_.refs_9_.refs_14_ = bf16[4,96,1536]{2,1,0:T(8,128)(2,1)} collective-permute-done((bf16[4,96,1536]{2,1,0:T(8,128)(2,1)}, bf16[4,96,1536]{2,1,0:T(8,128)(2,1)}, u32[]{:S(2)}, u32[]{:S(2)}) %collective-permute-start.8) | collective-permute-done | bytes 1179680 | tf_op jit(solution)/shard_map/ppermute | solution.py:688
  107.0 10.2 %collective-permute-done.2.refs_4_ = bf16[256,768]{1,0:T(8,128)(2,1)S(1)} collective-permute-done((bf16[256,768]{1,0:T(8,128)(2,1)}, bf16[256,768]{1,0:T(8,128)(2,1)S(1)}, u32[]{:S(2)}, u32[]{:S(2)}) %collective-permute-start.2) | collective-permute-done | bytes 393248 | tf_op jit(solution)/shard_map/ppermute | solution.py:674
  120.4 19.9 %self_forward.1 = (bf16[1024,768]{1,0:T(8,128)(2,1)}, bf16[4,1024,512]{2,1,0:T(8,128)(2,1)}, bf16[4,256,256]{2,1,0:T(8,128)(2,1)}, bf16[4,256,256]{2,1,0:T(8,128...) custom-call(s32[16]{0:T(128)} %stack.99.refs_0_, bf16[256,768]{1,0:T(8,128)(2,1)} %refs_1_.7, ...), custom_call_target="tpu_custom_call" | custom-call | flops 25300000768 | bytes 19502144 | tf_op jit(solution)/shard_map/self_forward/pallas_call | solution.py:630
  140.3 6.1 %collective-permute-done.16.refs_7_ = bf16[4,96,1536]{2,1,0:T(8,128)(2,1)} collective-permute-done((bf16[4,96,1536]{2,1,0:T(8,128)(2,1)}, bf16[4,96,1536]{2,1,0:T(8,128)(2,1)}, u32[]{:S(2)}, u32[]{:S(2)}) %collective-permute-start.16) | collective-permute-done | bytes 1179680 | tf_op jit(solution)/shard_map/ppermute | solution.py:688
  147.0 17.3 %cross_forward.1 = (bf16[4,768,512]{2,1,0:T(8,128)(2,1)}, bf16[4,256,256]{2,1,0:T(8,128)(2,1)}, bf16[4,256,256]{2,1,0:T(8,128)(2,1)}, f32[4,8,256]{2,1,0:T(8,128)}, f32[256,768]{1,0:T(8,128)}) custom-call(s32[16]{0:T(128)} %stack.99.refs_0_, f32[256,768]{1,0:T(8,128)} %get-tuple-element.88.refs_1_.refs_2_, bf16[768,768]{1,0:T(8,128)(2,1)} %refs_3_.3, ...), custom_call_target="tpu_custom_call" | custom-call | flops 19549999104 | bytes 16435264 | tf_op jit(solution)/shard_map/cross_forward/pallas_call | solution.py:630
  167.6 17.1 %feed_forward.1 = (bf16[256,768]{1,0:T(8,128)(2,1)}, f32[256,768]{1,0:T(8,128)}, bf16[4,4,96,768]{3,2,1,0:T(8,128)(2,1)}, bf16[4,4,96,768]{3,2,1,0:T(8,128)(2,1)...) custom-call(s32[16]{0:T(128)} %stack.99.refs_0_, ...), custom_call_target="tpu_custom_call" | custom-call | flops 19549999104 | bytes 21393472 | tf_op jit(solution)/shard_map/feed_forward/pallas_call | solution.py:630
  186.0 16.9 %cross_backward_first.1 = (bf16[4,2,96,768]{3,2,1,0:T(8,128)(2,1)}, bf16[4,2,96,768]{3,2,1,0:T(8,128)(2,1)}, f32[4,1,768]{2,1,0:T(1,128)}, f32[256,768]{1,0:T(8,128)}, f32[768,768]{1,0:T(8,128)}) custom-call(s32[16]{0:T(128)} %stack.99.refs_0_, f32[256,768]{1,0:T(8,128)} %get-tuple-element.94.refs_1_, f32[256,768]{1,0:T(8,128)} %get-tuple-element.88.refs_1_.refs_2_, ...), custom_call_target="tpu_custom_call" | custom-call | flops 16099999744 | bytes 22778944 | tf_op jit(solution)/shard_map/cross_backward_first/pallas_call | solution.py:630
  204.2 3.8 convert_add_fusion.1
  213.4 18.3 %cross_backward_last.1 = (bf16[4,2,96,768]{3,2,1,0:T(8,128)(2,1)}, bf16[4,2,96,768]{3,2,1,0:T(8,128)(2,1)}, f32[4,1,768]{2,1,0:T(1,128)}, f32[256,768]{1,0:T(8,1...) custom-call(s32[16]{0:T(128)} %stack.99.refs_0_, ...), custom_call_target="tpu_custom_call" | custom-call | flops 17250000896 | bytes 25199680 | tf_op jit(solution)/shard_map/cross_backward_last/pallas_call | solution.py:630
  231.8 4.7 %all-to-all-start.4 = ((bf16[4,192,768]{2,1,0:T(8,128)(2,1)}), bf16[4,192,768]{2,1,0:T(8,128)(2,1)}, u32[]{:S(2)}, u32[]{:S(2)}) async-start(bf16[4,192,768]{2,1,0:T(8,128)(2,1)} %bitcast.217), calls=%async_computation.4 | async-start | bytes 2359296 | tf_op jit(solution)/shard_map/all_to_all | solution.py:1100
  251.8 18.7 %self_backward_first.1 = (bf16[4,2,96,768]{3,2,1,0:T(8,128)(2,1)}, bf16[4,2,96,768]{3,2,1,0:T(8,128)(2,1)}, f32[4,1,768]{2,1,0:T(1,128)}, f32[1024,768]{1,0:T(8,128)}) custom-call(s32[16]{0:T(128)} %stack.99.refs_0_, bf16[256,768]{1,0:T(8,128)(2,1)} %refs_1_.7, bf16[256,768]{1,0:T(8,128)(2,1)} %collective-permute-done.refs_2_, ...), custom_call_target="tpu_custom_call" | custom-call | flops 19549999104 | bytes 23769152 | tf_op jit(solution)/shard_map/self_backward_first/pallas_call | solution.py:630
  287.8 4.5 %collective-permute-done.49 = bf16[96,768]{1,0:T(8,128)(2,1)} collective-permute-done((bf16[96,768]{1,0:T(8,128)(2,1)S(1)}, bf16[96,768]{1,0:T(8,128)(2,1)}, u32[]{:S(2)}, u32[]{:S(2)}) %collective-permute-start.49) | collective-permute-done | bytes 147488 | tf_op jit(solution)/shard_map/ppermute | solution.py:680
  294.3 22.3 %self_backward_last.1 = (bf16[4,2,96,768]{3,2,1,0:T(8,128)(2,1)}, bf16[4,2,96,768]{3,2,1,0:T(8,128)(2,1)}, f32[4,1,768]{2,1,0:T(1,128)}, f32[256,768]{1,0:T(8,12...) custom-call(s32[16]{0:T(128)} %stack.99.refs_0_, ...), custom_call_target="tpu_custom_call" | custom-call | flops 20700000256 | bytes 25821248 | tf_op jit(solution)/shard_map/self_backward_last/pallas_call | solution.py:630
  317.4 3.7 collective-permute-start.35
  332.9 3.7 collective-permute-start.30
  373.2 3.6 finish.1
  392.7 5.4 %collective-permute-start.52 = (bf16[96,768]{1,0:T(8,128)(2,1)S(1)}, bf16[96,768]{1,0:T(8,128)(2,1)S(1)}, u32[]{:S(2)}, u32[]{:S(2)}) collective-permute-start(bf16[96,768]{1,0:T(8,128)(2,1)S(1)} %get-tuple-element.289), channel_id=1, source_target_pairs={{0,3},{1,0},{2,1},{3,2},{4,7},{5,4},{6,5},{7,6},{8,11},{9,8},{10,9... | collective-permute-start | bytes 442376 | tf_op jit(solution)/shard_map/ppermute | solution.py:680
  405.5 5.8 %collective-permute-done.39 = bf16[4,96,768]{2,1,0:T(8,128)(2,1)S(1)} collective-permute-done((bf16[4,96,768]{2,1,0:T(8,128)(2,1)S(1)}, bf16[4,96,768]{2,1,0:T(8,128)(2,1)S(1)}, u32[]{:S(2)}, u32[]{:S(2)}) %collective-permute-start.39) | collective-permute-done | bytes 589856 | tf_op jit(solution)/shard_map/ppermute | solution.py:688
  (397 shorter events, 175.5 us)
Async XLA Ops:
  34.7 35.4 %collective-permute-start.6 = (bf16[4,96,1536]{2,1,0:T(8,128)(2,1)S(1)}, bf16[4,96,1536]{2,1,0:T(8,128)(2,1)}, u32[]{:S(2)}, u32[]{:S(2)}) collective-permute-start(bf16[4,96,1536]{2,1,0:T(8,128)(2,1)S(1)} %pad_maximum_fusion.2.refs_8_.refs_6_.refs_11_), channel_id=1, source_target_pairs={{0,8},{4,20},{8,0},{12,28},{16,24},{20,4},{24,16},{28,12},{1,9},{5... | collective-permute-start | bytes 3538952 | tf_op jit(solution)/shard_map/ppermute | solution.py:688
  37.0 39.3 %collective-permute-start.15 = (bf16[96,1536]{1,0:T(8,128)(2,1)}, bf16[96,1536]{1,0:T(8,128)(2,1)}, u32[]{:S(2)}, u32[]{:S(2)}) collective-permute-start(bf16[96,1536]{1,0:T(8,128)(2,1)} %get-tuple-element.318), channel_id=1, source_target_pairs={{0,3},{1,0},{2,1},{3,2},{4,7},{5,4},{6,5},{7,6},{8,11},{9,8},{10,9... | collective-permute-start | bytes 884744 | tf_op jit(solution)/shard_map/ppermute | solution.py:674
  37.0 40.1 %collective-permute-start.14 = (bf16[96,1536]{1,0:T(8,128)(2,1)}, bf16[96,1536]{1,0:T(8,128)(2,1)}, u32[]{:S(2)}, u32[]{:S(2)}) collective-permute-start(bf16[96,1536]{1,0:T(8,128)(2,1)} %get-tuple-element.318), channel_id=1, source_target_pairs={{0,2},{1,3},{2,0},{3,1},{4,6},{5,7},{6,4},{7,5},{8,10},{9,11},{10,... | collective-permute-start | bytes 884744 | tf_op jit(solution)/shard_map/ppermute | solution.py:674
  39.8 42.3 %collective-permute-start.13 = (bf16[96,1536]{1,0:T(8,128)(2,1)}, bf16[96,1536]{1,0:T(8,128)(2,1)}, u32[]{:S(2)}, u32[]{:S(2)}) collective-permute-start(bf16[96,1536]{1,0:T(8,128)(2,1)} %get-tuple-element.318), channel_id=1, source_target_pairs={{0,1},{1,2},{2,3},{3,0},{4,5},{5,6},{6,7},{7,4},{8,9},{9,10},{10,1... | collective-permute-start | bytes 884744 | tf_op jit(solution)/shard_map/ppermute | solution.py:674
  70.1 31.0 %collective-permute-start.8 = (bf16[4,96,1536]{2,1,0:T(8,128)(2,1)}, bf16[4,96,1536]{2,1,0:T(8,128)(2,1)}, u32[]{:S(2)}, u32[]{:S(2)}) collective-permute-start(bf16[4,96,1536]{2,1,0:T(8,128)(2,1)} %collective-permute-done.6.refs_9_.refs_7_.refs_12_), channel_id=1, source_target_pairs={{0,16},{4,12},{8,24},{12,4},{16,0},{20,28},{24,8},{28,20},{1,17},{... | collective-permute-start | bytes 3538952 | tf_op jit(solution)/shard_map/ppermute | solution.py:688
  72.3 31.8 %all-to-all-start.1 = ((f32[8,3,4608]{2,1,0:T(4,128)}), f32[8,3,4608]{2,1,0:T(4,128)S(1)}, u32[]{:S(2)}, u32[]{:S(2)}) async-start(f32[8,3,4608]{2,1,0:T(4,128)} %copy.176), calls=%async_computation.1 | async-start | bytes 1179648 | tf_op jit(solution)/shard_map/all_to_all | solution.py:854
  77.1 29.2 %collective-permute-start.1 = (bf16[256,768]{1,0:T(8,128)(2,1)}, bf16[256,768]{1,0:T(8,128)(2,1)}, u32[]{:S(2)}, u32[]{:S(2)}) collective-permute-start(bf16[256,768]{1,0:T(8,128)(2,1)} %refs_1_.7), channel_id=1, source_target_pairs={{0,2},{1,3},{2,0},{3,1},{4,6},{5,7},{6,4},{7,5},{8,10},{9,11},{10,... | collective-permute-start | bytes 1179656 | tf_op jit(solution)/shard_map/ppermute | solution.py:674
  82.1 36.7 %collective-permute-start.9 = (bf16[4,96,1536]{2,1,0:T(8,128)(2,1)S(1)}, bf16[4,96,1536]{2,1,0:T(8,128)(2,1)}, u32[]{:S(2)}, u32[]{:S(2)}) collective-permute-start(bf16[4,96,1536]{2,1,0:T(8,128)(2,1)S(1)} %pad_maximum_fusion.2.refs_8_.refs_6_.refs_11_), channel_id=1, source_target_pairs={{0,4},{4,0},{8,12},{12,8},{16,20},{20,16},{24,28},{28,24},{1,5},{5... | collective-permute-start | bytes 3538952 | tf_op jit(solution)/shard_map/ppermute | solution.py:688
  90.5 29.8 %collective-permute-start.10 = (bf16[4,96,1536]{2,1,0:T(8,128)(2,1)}, bf16[4,96,1536]{2,1,0:T(8,128)(2,1)}, u32[]{:S(2)}, u32[]{:S(2)}) collective-permute-start(bf16[4,96,1536]{2,1,0:T(8,128)(2,1)} %collective-permute-done.6.refs_9_.refs_7_.refs_12_), channel_id=1, source_target_pairs={{0,4},{4,0},{8,12},{12,8},{16,20},{20,16},{24,28},{28,24},{1,5},{5... | collective-permute-start | bytes 3538952 | tf_op jit(solution)/shard_map/ppermute | solution.py:688
  90.5 29.8 %collective-permute-start.11 = (bf16[4,96,1536]{2,1,0:T(8,128)(2,1)}, bf16[4,96,1536]{2,1,0:T(8,128)(2,1)}, u32[]{:S(2)}, u32[]{:S(2)}) collective-permute-start(bf16[4,96,1536]{2,1,0:T(8,128)(2,1)} %collective-permute-done.7.refs_10_.refs_8_.refs_13_), channel_id=1, source_target_pairs={{0,4},{4,0},{8,12},{12,8},{16,20},{20,16},{24,28},{28,24},{1,5},{5... | collective-permute-start | bytes 3538952 | tf_op jit(solution)/shard_map/ppermute | solution.py:688
  117.2 29.1 %collective-permute-start.16 = (bf16[4,96,1536]{2,1,0:T(8,128)(2,1)}, bf16[4,96,1536]{2,1,0:T(8,128)(2,1)}, u32[]{:S(2)}, u32[]{:S(2)}) collective-permute-start(bf16[4,96,1536]{2,1,0:T(8,128)(2,1)} %pad_maximum_fusion.3.refs_6_), channel_id=1, source_target_pairs={{0,8},{4,20},{8,0},{12,28},{16,24},{20,4},{24,16},{28,12},{1,9},{5... | collective-permute-start | bytes 3538952 | tf_op jit(solution)/shard_map/ppermute | solution.py:688
  118.8 27.5 %collective-permute-start.17 = (bf16[4,96,1536]{2,1,0:T(8,128)(2,1)}, bf16[4,96,1536]{2,1,0:T(8,128)(2,1)S(1)}, u32[]{:S(2)}, u32[]{:S(2)}) collective-permute-start(bf16[4,96,1536]{2,1,0:T(8,128)(2,1)} %pad_maximum_fusion.3.refs_6_), channel_id=1, source_target_pairs={{0,16},{4,12},{8,24},{12,4},{16,0},{20,28},{24,8},{28,20},{1,17},{... | collective-permute-start | bytes 3538952 | tf_op jit(solution)/shard_map/ppermute | solution.py:688
  202.8 28.8 %collective-permute-start.26 = (bf16[4,2,96,768]{3,2,1,0:T(8,128)(2,1)}, bf16[4,2,96,768]{3,2,1,0:T(8,128)(2,1)}, u32[]{:S(2)}, u32[]{:S(2)}) collective-permute-start(bf16[4,2,96,768]{3,2,1,0:T(8,128)(2,1)} %get-tuple-element.112), channel_id=1, source_target_pairs={{0,4},{4,0},{8,12},{12,8},{16,20},{20,16},{24,28},{28,24},{1,5},{5... | collective-permute-start | bytes 3538952 | tf_op jit(solution)/shard_map/ppermute | solution.py:688
  211.4 34.0 %collective-permute-start.25 = (bf16[2,4,96,768]{3,2,1,0:T(8,128)(2,1)}, bf16[2,4,96,768]{3,2,1,0:T(8,128)(2,1)}, u32[]{:S(2)}, u32[]{:S(2)}) collective-permute-start(bf16[2,4,96,768]{3,2,1,0:T(8,128)(2,1)} %slice.739), channel_id=1, source_target_pairs={{0,16},{4,12},{8,24},{12,4},{16,0},{20,28},{24,8},{28,20},{1,17},{... | collective-permute-start | bytes 3538952 | tf_op jit(solution)/shard_map/ppermute | solution.py:688
  231.7 38.9 %collective-permute-start.29 = (bf16[4,2,96,768]{3,2,1,0:T(8,128)(2,1)}, bf16[4,2,96,768]{3,2,1,0:T(8,128)(2,1)}, u32[]{:S(2)}, u32[]{:S(2)}) collective-permute-start(bf16[4,2,96,768]{3,2,1,0:T(8,128)(2,1)} %get-tuple-element.125), channel_id=1, source_target_pairs={{0,4},{4,0},{8,12},{12,8},{16,20},{20,16},{24,28},{28,24},{1,5},{5... | collective-permute-start | bytes 3538952 | tf_op jit(solution)/shard_map/ppermute | solution.py:688
  231.8 51.3 %all-to-all-start.4 = ((bf16[4,192,768]{2,1,0:T(8,128)(2,1)}), bf16[4,192,768]{2,1,0:T(8,128)(2,1)}, u32[]{:S(2)}, u32[]{:S(2)}) async-start(bf16[4,192,768]{2,1,0:T(8,128)(2,1)} %bitcast.217), calls=%async_computation.4 | async-start | bytes 2359296 | tf_op jit(solution)/shard_map/all_to_all | solution.py:1100
  251.3 42.9 %collective-permute-start.28 = (bf16[2,4,96,768]{3,2,1,0:T(8,128)(2,1)}, bf16[2,4,96,768]{3,2,1,0:T(8,128)(2,1)}, u32[]{:S(2)}, u32[]{:S(2)}) collective-permute-start(bf16[2,4,96,768]{3,2,1,0:T(8,128)(2,1)} %slice.738), channel_id=1, source_target_pairs={{0,16},{4,12},{8,24},{12,4},{16,0},{20,28},{24,8},{28,20},{1,17},{... | collective-permute-start | bytes 3538952 | tf_op jit(solution)/shard_map/ppermute | solution.py:688
  270.6 72.7 %collective-permute-start.36 = (bf16[4,2,96,768]{3,2,1,0:T(8,128)(2,1)}, bf16[4,2,96,768]{3,2,1,0:T(8,128)(2,1)}, u32[]{:S(2)}, u32[]{:S(2)}) collective-permute-start(bf16[4,2,96,768]{3,2,1,0:T(8,128)(2,1)} %get-tuple-element.138), channel_id=1, source_target_pairs={{0,4},{4,0},{8,12},{12,8},{16,20},{20,16},{24,28},{28,24},{1,5},{5... | collective-permute-start | bytes 3538952 | tf_op jit(solution)/shard_map/ppermute | solution.py:688
  286.2 46.7 %collective-permute-start.43 = (bf16[2,4,96,768]{3,2,1,0:T(8,128)(2,1)}, bf16[2,4,96,768]{3,2,1,0:T(8,128)(2,1)}, u32[]{:S(2)}, u32[]{:S(2)}) collective-permute-start(bf16[2,4,96,768]{3,2,1,0:T(8,128)(2,1)} %fusion.4), channel_id=1, source_target_pairs={{0,16},{4,12},{8,24},{12,4},{16,0},{20,28},{24,8},{28,20},{1,17},{... | collective-permute-start | bytes 3538952 | tf_op jit(solution)/shard_map/ppermute | solution.py:688
  317.4 29.2 %collective-permute-start.35 = (f32[3,4608]{1,0:T(4,128)S(1)}, f32[3,4608]{1,0:T(4,128)S(1)}, u32[]{:S(2)}, u32[]{:S(2)}) collective-permute-start(f32[3,4608]{1,0:T(4,128)S(1)} %pad_maximum_fusion.9), channel_id=1, source_target_pairs={{0,1},{1,2},{2,3},{3,0},{4,5},{5,6},{6,7},{7,4},{8,9},{9,10},{10,1... | collective-permute-start | bytes 165896 | tf_op jit(solution)/shard_map/ppermute | solution.py:680
  332.9 38.3 %collective-permute-start.30 = (bf16[256,768]{1,0:T(8,128)(2,1)}, bf16[256,768]{1,0:T(8,128)(2,1)}, u32[]{:S(2)}, u32[]{:S(2)}) collective-permute-start(bf16[256,768]{1,0:T(8,128)(2,1)} %get-tuple-element.130), channel_id=1, source_target_pairs={{0,3},{1,0},{2,1},{3,2},{4,7},{5,4},{6,5},{7,6},{8,11},{9,8},{10,9... | collective-permute-start | bytes 1179656 | tf_op jit(solution)/shard_map/ppermute | solution.py:680
  343.2 29.9 %collective-permute-start.31 = (bf16[256,768]{1,0:T(8,128)(2,1)}, bf16[256,768]{1,0:T(8,128)(2,1)}, u32[]{:S(2)}, u32[]{:S(2)}) collective-permute-start(bf16[256,768]{1,0:T(8,128)(2,1)} %get-tuple-element.131), channel_id=1, source_target_pairs={{0,2},{1,3},{2,0},{3,1},{4,6},{5,7},{6,4},{7,5},{8,10},{9,11},{10,... | collective-permute-start | bytes 1179656 | tf_op jit(solution)/shard_map/ppermute | solution.py:680
  346.8 36.3 %collective-permute-start.37 = (bf16[4,2,96,768]{3,2,1,0:T(8,128)(2,1)}, bf16[4,2,96,768]{3,2,1,0:T(8,128)(2,1)}, u32[]{:S(2)}, u32[]{:S(2)}) collective-permute-start(bf16[4,2,96,768]{3,2,1,0:T(8,128)(2,1)} %get-tuple-element.140), channel_id=1, source_target_pairs={{0,4},{4,0},{8,12},{12,8},{16,20},{20,16},{24,28},{28,24},{1,5},{5... | collective-permute-start | bytes 3538952 | tf_op jit(solution)/shard_map/ppermute | solution.py:688
  346.8 30.0 %collective-permute-start.44 = (bf16[4,96,768]{2,1,0:T(8,128)(2,1)}, bf16[4,96,768]{2,1,0:T(8,128)(2,1)}, u32[]{:S(2)}, u32[]{:S(2)}) collective-permute-start(bf16[4,96,768]{2,1,0:T(8,128)(2,1)} %fusion.16), channel_id=1, source_target_pairs={{0,8},{4,20},{8,0},{12,28},{16,24},{20,4},{24,16},{28,12},{1,9},{5... | collective-permute-start | bytes 1769480 | tf_op jit(solution)/shard_map/ppermute | solution.py:688
  (80 other events, 1081.9 us)

commit v3 on v2

--- a/solution.py
+++ b/solution.py
@@ -2,6 +2,7 @@
 
 import jax
 import jax.numpy as jnp
+import numpy as np
 from jax import lax
 from jax.experimental import pallas as pl
 from jax.experimental.pallas import tpu as pltpu
@@ -149,10 +150,20 @@
     return cat.T.astype(BF16), totals
 
 
-def attend_back(queries, kv, out_grad, mask, totals, probs, grads, count, put):
+def attend_back(queries, kv, attended, out_grad, mask, totals, probs, dscore, count, put):
     rows = queries.shape[0]
     step = 256
     wide = out_grad.astype(F32)
+    row = lax.broadcasted_iota(jnp.int32, (8, 2 * WIN), 0)
+    part = lax.broadcasted_iota(jnp.int32, (8, 2 * WIN), 1) // HD
+    choose = ((part == row + 2) & (row < 2)) | ((part == 1) & (row == 2))
+    deltas = lax.dot_general(
+        choose.astype(F32),
+        wide * attended.astype(F32),
+        (((1,), (1,)), ((), ())),
+        precision=HIGH,
+        preferred_element_type=F32,
+    )
     second = keep(swap(wide[:, :WIN]), True).astype(BF16)
     query_parts = []
     heads = []
@@ -165,36 +176,35 @@
             query, given = queries[:, WIN:], second
             kcol, vcol = 2, 3
         heads.append((query, given))
-        delta = jnp.zeros((1, rows), F32)
+        total, delta = totals[h], deltas[h : h + 1, :]
         for lo in range(0, count, step):
-            part = nt(kv(lo, lo + step, kcol), query) + mask[lo : lo + step, :]
-            weights = jnp.exp(part - totals[h])
-            weight_grad = nt(kv(lo, lo + step, vcol), given)
-            delta = delta + jnp.sum(weights * weight_grad, axis=0, keepdims=True)
-            probs[h, lo : lo + step, :] = weights
-            grads[h, lo : lo + step, :] = weight_grad
-        query_part = jnp.zeros((rows, WIN), F32)
-        for lo in range(0, count, step):
-            part = probs[h, lo : lo + step, :]
-            score_grad = (part * (grads[h, lo : lo + step, :] - delta)).astype(BF16)
-            grads[h, lo : lo + step, :] = score_grad.astype(F32)
-            query_part = query_part + tn(score_grad, kv(lo, lo + step, kcol))
-        query_parts.append(query_part * 0.125)
+            hi = lo + step
+            weights = jnp.exp(nt(kv(lo, hi, kcol), query) + mask[lo:hi, :] - total)
+            probs[h, lo:hi, :] = weights.astype(BF16)
+            weight_grad = nt(kv(lo, hi, vcol), given)
+            dscore[h, lo:hi, :] = (weights * (weight_grad - delta)).astype(BF16)
+        query_parts.append(tn(kv(0, count, kcol), dscore[h, 0:count, :]))
     for lo in range(0, count, step):
         hi = lo + step
-        prob = [probs[h, lo:hi, :].astype(BF16) for h in range(3)]
-        grad = [grads[h, lo:hi, :].astype(BF16) for h in range(3)]
         put(
             lo,
             hi,
-            nn(grad[0], heads[0][0]) + nn(grad[1], heads[1][0]),
-            nn(prob[0], heads[0][1]) + nn(prob[1], heads[1][1]),
-            nn(grad[2], heads[2][0]),
-            nn(prob[2], heads[2][1]),
+            nn(dscore[0, lo:hi, :], heads[0][0]) + nn(dscore[1, lo:hi, :], heads[1][0]),
+            nn(probs[0, lo:hi, :], heads[0][1]) + nn(probs[1, lo:hi, :], heads[1][1]),
+            nn(dscore[2, lo:hi, :], heads[2][0]),
+            nn(probs[2, lo:hi, :], heads[2][1]),
         )
-    pair = jnp.where(lanes(rows, True), query_parts[0], query_parts[1])
-    third = keep(swap(query_parts[2]), True)
-    return pair, third
+    both = jnp.concatenate(
+        [
+            query_parts[0][:HD],
+            query_parts[1][HD:],
+            query_parts[2][HD:],
+            jnp.zeros((HD, rows), F32),
+        ],
+        axis=0,
+    )
+    both = (both * 0.125).T
+    return both[:, :WIN], both[:, WIN:]
 
 
 def self_mask(scal, mask, rows, splits):
@@ -244,10 +254,10 @@
     frames = refs[1 : 1 + splits]
     mod, bias, out_bias = refs[1 + splits : 4 + splits]
     pieces = refs[4 + splits : 4 + splits + n_p]
-    hidden, kv_out, q_out, att_out, lse, branch_out, after = refs[
+    hidden_t, kv_out, q_out, att_out, lse, branch_out, after = refs[
         4 + splits + n_p : 11 + splits + n_p
     ]
-    weights, mask, scores, probs, sems = refs[11 + splits + n_p :]
+    hidden, weights, mask, scores, probs, sems = refs[11 + splits + n_p :]
     rows = frames[0].shape[0]
     count = rows * splits
     copies = load_start(pieces, weights, sems, scal)
@@ -257,6 +267,7 @@
         normed, _ = normalize(frames[block][...].astype(F32))
         value = normed * (1.0 + per_row(mod, 1, clip)) + per_row(mod, 0, clip)
         hidden[block * rows : (block + 1) * rows, :] = value.astype(BF16)
+        hidden_t[:, block * rows : (block + 1) * rows] = value.T.astype(BF16)
     branch_out[...] = jnp.broadcast_to(out_bias[...], branch_out.shape)
     for copy in copies:
         copy.wait()
@@ -293,14 +304,18 @@
 def cross_forward(n_p, splits, *refs):
     scal, after_self, text, gain, bias, out_bias = refs[:6]
     pieces = refs[6 : 6 + n_p]
-    kv_out, q_out, att_out, lse, after = refs[6 + n_p : 11 + n_p]
-    weights, mask, scores, probs, sems = refs[11 + n_p :]
+    hidden_t, text_t, kv_out, q_out, att_out, lse, after = refs[6 + n_p : 13 + n_p]
+    weights, mask, scores, probs, sems = refs[13 + n_p :]
     rows = after_self.shape[0]
     count = text.shape[0]
     copies = load_start(pieces, weights, sems, scal, D)
     cross_mask(scal, mask, rows, splits, count // TXT)
     normed, _ = normalize(after_self[...])
-    hidden = (normed * gain[...]).astype(BF16)
+    wide = normed * gain[...]
+    hidden = wide.astype(BF16)
+    hidden_t[...] = wide.T.astype(BF16)
+    for lo in range(0, count, 256):
+        text_t[:, lo : lo + 256] = text[lo : lo + 256, :].astype(F32).T.astype(BF16)
     after[...] = after_self[...] + out_bias[...]
     for copy in copies:
         copy.wait()
@@ -331,41 +346,52 @@
     lax.fori_loop(0, splits, one, 0)
 
 
-def feed_forward(n_p, splits, *refs):
+def feed_forward(n_p, splits, low, high, *refs):
     scal, after_cross, upstream, mod, in_bias, out_bias = refs[:6]
     pieces = refs[6 : 6 + n_p]
     rest = refs[6 + n_p :]
     n_o = 2 if n_p > 1 else 1
-    layer_out, d_after = rest[:2]
-    grads_in, grads_out = rest[2 : 2 + n_o], rest[2 + n_o : 2 + 2 * n_o]
-    in_bias_grad, out_bias_grad, sums = rest[2 + 2 * n_o : 5 + 2 * n_o]
-    weights, gbuf, mlp, back, load_sems, store_sems = rest[5 + 2 * n_o :]
+    first, last = low == 0, high == splits
+    if not first:
+        mlp_in, back_in, bias_in = rest[:3]
+        rest = rest[3:]
+    grads = rest[:n_o]
+    in_bias_grad = rest[n_o]
+    rest = rest[n_o + 1 :]
+    if last:
+        layer_out, d_after, out_bias_grad, sums, mlp, back = rest[:6]
+        rest = rest[6:]
+    else:
+        mlp, back = rest[:2]
+        rest = rest[2:]
+    weights, gbuf, load_sems, store_sems = rest
     rows = after_cross.shape[0]
     copies = load_start(pieces, weights, load_sems, scal)
     clip = own_clip(scal, rows, splits)
     normed, inverse = normalize(after_cross[...])
     scale = 1.0 + per_row(mod, 4, clip)
-    hidden = (normed * scale + per_row(mod, 3, clip)).astype(BF16)
+    wide = normed * scale + per_row(mod, 3, clip)
+    hidden = wide.astype(BF16)
+    hidden_t = wide.T.astype(BF16)
     gate = per_row(mod, 5, clip)
     given = upstream[...].astype(F32)
-    low = (given * gate).astype(BF16)
-    low_wide = low.astype(F32)
-    out_bias_grad[...] = jnp.sum(low_wide, axis=0, keepdims=True)
-    hidden_t = hidden.astype(F32).T.astype(BF16)
+    low_wide = given * gate
+    lowered = low_wide.astype(BF16)
     low_t = low_wide.T.astype(BF16)
-    mlp[...] = jnp.broadcast_to(out_bias[...], mlp.shape)
-    back[...] = jnp.zeros_like(back)
+    if first:
+        mlp[...] = jnp.broadcast_to(out_bias[...], mlp.shape)
+        back[...] = jnp.zeros_like(back)
+        in_bias_grad[...] = jnp.zeros_like(in_bias_grad)
+    else:
+        mlp[...] = mlp_in[...]
+        back[...] = back_in[...]
+        in_bias_grad[...] = bias_in[...]
     for copy in copies:
         copy.wait()
 
-    def stores(z):
-        return store_copies(gbuf, z, grads_in, store_sems, scal) + store_copies(
-            gbuf, z, grads_out, store_sems, scal, D, n_p
-        )
-
-    def one(z, carry):
-        place = shard_index(scal, z, splits)
-        pre = nn(hidden, weights[z, :, 0:D]) + in_bias[place]
+    def one(i, carry):
+        place = shard_index(scal, i + low, splits)
+        pre = nn(hidden, weights[i, :, 0:D]) + in_bias[place]
         inner = 0.7978845608028654 * (pre + 0.044715 * (pre * pre * pre))
         curve = jnp.tanh(inner)
         half = 0.5 * (1.0 + curve)
@@ -373,34 +399,38 @@
         slope = half + 0.5 * pre * (1.0 - curve * curve) * 0.7978845608028654 * (
             1.0 + 3.0 * 0.044715 * pre * pre
         )
-        pre_grad = (slope * nn(low, weights[z, :, D:])).astype(BF16)
+        pre_grad = (slope * nn(lowered, weights[i, :, D:])).astype(BF16)
         in_bias_grad[place] = jnp.sum(pre_grad.astype(F32), axis=0, keepdims=True)
-        mlp[...] += nt(active, weights[z, :, D:])
-        back[...] += nt(pre_grad, weights[z, :, 0:D])
-        gbuf[z, :, 0:D] = nn(hidden_t, pre_grad).astype(BF16)
-        gbuf[z, :, D:] = nn(low_t, active).astype(BF16)
-        for copy in stores(z):
+        mlp[...] += nt(active, weights[i, :, D:])
+        back[...] += nt(pre_grad, weights[i, :, 0:D])
+        gbuf[i, :, 0:D] = nn(hidden_t, pre_grad).astype(BF16)
+        gbuf[i, :, D:] = nn(low_t, active).astype(BF16)
+        for copy in store_copies(gbuf, i, grads, store_sems, scal):
             copy.start()
         return carry
 
-    lax.fori_loop(0, splits, one, 0)
-    branch = mlp[...]
-    layer_out[...] = (after_cross[...] + gate * branch).astype(BF16)
-    hidden_grad = back[...]
-    d_after[...] = given + normalize_back(hidden_grad * scale, normed, inverse)
-    clip_row = own_clip_row(scal, rows, splits)
-    sums[:, 0:D] = clip_sums(clip_row, hidden_grad)
-    sums[:, D : 2 * D] = clip_sums(clip_row, hidden_grad * normed)
-    sums[:, 2 * D :] = clip_sums(clip_row, given * branch)
-    for z in range(splits):
-        for copy in stores(z):
+    lax.fori_loop(0, high - low, one, 0)
+    if last:
+        out_bias_grad[...] = jnp.sum(lowered.astype(F32), axis=0, keepdims=True)
+        branch = mlp[...]
+        layer_out[...] = (after_cross[...] + gate * branch).astype(BF16)
+        hidden_grad = back[...]
+        d_after[...] = given + normalize_back(hidden_grad * scale, normed, inverse)
+        clip_row = own_clip_row(scal, rows, splits)
+        sums[:, 0:D] = clip_sums(clip_row, hidden_grad)
+        sums[:, D : 2 * D] = clip_sums(clip_row, hidden_grad * normed)
+        sums[:, 2 * D :] = clip_sums(clip_row, given * branch)
+    for i in range(high - low):
+        for copy in store_copies(gbuf, i, grads, store_sems, scal):
             copy.wait()
 
 
 def cross_backward(n_p, splits, low, high, *refs):
-    scal, d_cross, after_self, text, gain, mod, branch, kv_in, q_in, att_in, lse = refs[:11]
-    pieces = refs[11 : 11 + n_p]
-    rest = refs[11 + n_p :]
+    scal, d_cross, after_self, hidden_t, text_t, gain, mod, branch, kv_in, q_in, att_in, lse = refs[
+        :12
+    ]
+    pieces = refs[12 : 12 + n_p]
+    rest = refs[12 + n_p :]
     first, last = low == 0, high == splits
     if not first:
         back_in, text_in, bias_in = rest[:3]
@@ -415,19 +445,14 @@
     else:
         back, text_back = rest[:2]
         rest = rest[2:]
-    weights, gbuf, mask, probs, dscore, key_grad, text_t, load_sems, store_sems = rest
+    weights, gbuf, mask, probs, dscore, key_grad, load_sems, store_sems = rest
     rows = after_self.shape[0]
-    count = text.shape[0]
+    count = text_t.shape[1]
     copies = load_start(pieces, weights, load_sems, scal, D, low)
     cross_mask(scal, mask, rows, splits, count // TXT)
-    normed, inverse = normalize(after_self[...])
-    hidden = (normed * gain[...]).astype(BF16)
-    hidden_t = hidden.astype(F32).T.astype(BF16)
     given = d_cross[...].astype(BF16)
     given_wide = given.astype(F32)
     given_t = given_wide.T.astype(BF16)
-    for lo in range(0, count, 256):
-        text_t[:, lo : lo + 256] = text[lo : lo + 256, :].astype(F32).T.astype(BF16)
     if first:
         back[...] = jnp.zeros_like(back)
         text_back[...] = jnp.zeros_like(text_back)
@@ -455,15 +480,15 @@
         head_grad = nn(given, weights[i, :, 4 * WIN :]).astype(BF16)
         totals = [lse[z, h : h + 1, :] for h in range(3)]
         pair, third = attend_back(
-            q_in[z], kv, head_grad, mask, totals, probs, dscore, count, put
+            q_in[z], kv, att_in[z], head_grad, mask, totals, probs, dscore, count, put
         )
         pair, third = pair.astype(BF16), third.astype(BF16)
         part = nn(text_t[...], key_grad[...])
         out_part = nn(given_t, att_in[z])
-        gbuf[i, :, 0:WIN] = nn(hidden_t, pair).astype(BF16)
+        gbuf[i, :, 0:WIN] = nn(hidden_t[...], pair).astype(BF16)
         gbuf[i, :, WIN : 3 * WIN] = part[:, 0 : 2 * WIN].astype(BF16)
         gbuf[i, :, 3 * WIN : 4 * WIN] = (
-            part[:, 2 * WIN : 3 * WIN] + nn(hidden_t, third)
+            part[:, 2 * WIN : 3 * WIN] + nn(hidden_t[...], third)
         ).astype(BF16)
         gbuf[i, :, 4 * WIN : 5 * WIN] = (part[:, 3 * WIN :] + out_part[:, 0:WIN]).astype(BF16)
         gbuf[i, :, 5 * WIN :] = out_part[:, WIN:].astype(BF16)
@@ -492,6 +517,7 @@
         return
     row_grads[...] = jnp.zeros_like(row_grads)
     row_grads[0:1, :] = jnp.sum(given_wide, axis=0, keepdims=True)
+    normed, inverse = normalize(after_self[...])
     hidden_grad = back[...]
     row_grads[1:2, :] = jnp.sum(hidden_grad * normed, axis=0, keepdims=True)
     total = d_cross[...] + normalize_back(hidden_grad * gain[...], normed, inverse)
@@ -505,7 +531,7 @@
 def self_backward(n_p, splits, low, high, *refs):
     scal = refs[0]
     frames = refs[1 : 1 + splits]
-    given_ref, hidden, kv_in, q_in, att_in, lse = refs[1 + splits : 7 + splits]
+    given_ref, hidden_t, kv_in, q_in, att_in, lse = refs[1 + splits : 7 + splits]
     pieces = refs[7 + splits : 7 + splits + n_p]
     rest = refs[7 + splits + n_p :]
     first, last = low == 0, high == splits
@@ -524,7 +550,7 @@
     else:
         back = rest[0]
         rest = rest[1:]
-    weights, gbuf, mask, probs, dscore, key_grad, hidden_t, load_sems, store_sems = rest
+    weights, gbuf, mask, probs, dscore, key_grad, load_sems, store_sems = rest
     rows = frames[0].shape[0]
     count = rows * splits
     copies = load_start(pieces, weights, load_sems, scal, 0, low)
@@ -532,8 +558,6 @@
     given = given_ref[...]
     given_wide = given.astype(F32)
     given_t = given_wide.T.astype(BF16)
-    for lo in range(0, count, 256):
-        hidden_t[:, lo : lo + 256] = hidden[lo : lo + 256, :].astype(F32).T.astype(BF16)
     if first:
         back[...] = jnp.zeros_like(back)
         bias_grad[...] = jnp.zeros_like(bias_grad)
@@ -559,7 +583,7 @@
         head_grad = nn(given, weights[i, :, 4 * WIN :]).astype(BF16)
         totals = [lse[z, h : h + 1, :] for h in range(3)]
         pair, third = attend_back(
-            q_in[z], kv, head_grad, mask, totals, probs, dscore, count, put
+            q_in[z], kv, att_in[z], head_grad, mask, totals, probs, dscore, count, put
         )
         pair = pair.astype(BF16)
         key_grad[0:rows, 2 * WIN : 3 * WIN] = (
@@ -621,6 +645,60 @@
     out[...] = d_after[...] + normalize_back(value * scale, normed, inverse)
 
 
+def pack_small(
+    table, own, cross, inner, own_rows, cross_rows, out_row, first, gate, second, packed
+):
+    n_dp = table.shape[1] // WIN
+    splits, clips = packed.shape[0], packed.shape[1] - 2
+    for z in range(splits):
+        packed[z, 0:clips, 0 : 2 * D] = first[0:clips, :]
+        packed[z, 0:clips, 2 * D : 3 * D] = gate[0:clips, :]
+        packed[z, 0:clips, 3 * D :] = second[0:clips, :]
+    packed[:, clips + 1, :] = jnp.zeros((splits, 6 * D), F32)
+    lane = lax.broadcasted_iota(jnp.int32, (D, n_dp * WIN), 0)
+
+    def moved(value, which):
+        choose = (lane == table[which : which + 1, :]).astype(F32).astype(BF16)
+        high = value.astype(BF16).astype(F32)
+        middle = (value - high).astype(BF16).astype(F32)
+        parts = jnp.concatenate([high, middle, value - high - middle], axis=0).astype(BF16)
+        found = nn(parts, choose)
+        count = value.shape[0]
+        return found[:count] + found[count : 2 * count] + found[2 * count :]
+
+    def by_shard(ref):
+        return jnp.concatenate([ref[z] for z in range(splits)], axis=0)
+
+    both = moved(jnp.concatenate([by_shard(own), by_shard(cross)], axis=0), 0)
+    heads = both[:splits] + pltpu.roll(both[splits:], 48, 1)
+    hidden = moved(by_shard(inner), 1)
+    rows = moved(
+        jnp.concatenate(
+            [own_rows[0:1, :], cross_rows[0:2, :], out_row[...]] + [jnp.zeros((4, D), F32)], axis=0
+        ),
+        2,
+    )
+    for d in range(n_dp):
+        span = slice(d * WIN, (d + 1) * WIN)
+        parts = [heads[:, span], hidden[:, span]]
+        parts += [jnp.broadcast_to(rows[r : r + 1, span], (splits, WIN)) for r in range(4)]
+        packed[:, clips + d // 6, d % 6 * D : (d % 6 + 1) * D] = jnp.concatenate(parts, axis=1)
+
+
+def bias_table(n_dp):
+    table = np.full((8, n_dp * WIN), -1, np.int32)
+    for d in range(n_dp):
+        for i in range(48):
+            part, h, r = i // 24, i % 24 // 8, i % 8
+            spot = d * 8 + r
+            start = (h * HD if h < 2 else 3 * WIN) if part == 0 else (2 + h / 2) * WIN
+            table[0, d * WIN + i] = (start if part == 0 or h < 2 else 4 * WIN) + spot
+        for i in range(96):
+            table[1, d * WIN + i] = i // 32 * 256 + d * 32 + i % 32
+            table[2, d * WIN + i] = d * 96 + i
+    return table
+
+
 MEMORY = {"v": pltpu.VMEM, "s": pltpu.SMEM, "a": pl.ANY}
 
 
@@ -668,10 +746,11 @@
 
         return [place * rows for place in kept(me) + kept(me ^ 1)]
 
-    def z_pieces(self, value):
+    def z_pieces(self, value, far=None):
         n = self.splits
         return [value] + [
-            lax.ppermute(value, "head", [(s, (s + k) % n) for s in range(n)]) for k in range(1, n)
+            lax.ppermute(value, "head", [(s, (s + k) % n) for s in range(n)])
+            for k in (range(1, n) if far is None else far)
         ]
 
     def z_back(self, parts):
@@ -681,44 +760,124 @@
             for k in range(1, n)
         ]
 
-    def gather_z(self, shard):
-        return jnp.stack(self.z_pieces(shard))
-
     def across(self, value, how):
         return lax.ppermute(value, "dp", how)
 
-    def gather(self, mine):
-        if not self.square:
-            return [lax.all_gather(mine, "dp", axis=1, tiled=True)]
-        one = self.across(mine, self.first)
-        two = self.across(mine, self.second)
-        three = self.across(one, self.second)
-        kept = [mine, one, two, three]
-        return kept + [self.across(k, self.core) for k in kept]
-
-    def send_second(self, blocks):
-        return self.across(blocks[2:4].astype(BF16), self.second)
-
-    def send_first(self, blocks):
-        return self.across(blocks[1].astype(BF16), self.first)
-
-    def reduce_z(self, mine):
-        arrived = self.z_back([mine[k].astype(BF16) for k in range(1, self.splits)])
-        total = mine[0]
-        for part in arrived:
-            total = total + part.astype(F32)
-        return total
-
-    def reduce_other(self, grads):
-        return lax.psum_scatter(grads[0][0], "dp", scatter_dimension=1, tiled=True).astype(F32)
-
-
-def wide_sum(a, b):
-    return a.astype(F32) + b.astype(F32)
-
-
-def tie(value, *others):
-    return lax.optimization_barrier((value,) + others)[0]
+    def z_move(self, value, k):
+        n = self.splits
+        return lax.ppermute(value, "head", [(s, (s - k) % n) for s in range(n)])
+
+
+class GradSum:
+    def __init__(self, ring, grads):
+        self.ring, self.grads = ring, list(grads)
+        self.moved = []
+        self.arrived = []
+        if not ring.square:
+            self.whole = lax.psum_scatter(grads[0][0], "dp", scatter_dimension=1, tiled=True)
+
+    def across(self, value, how):
+        if self.ring.square:
+            self.moved.append(self.ring.across(value.astype(BF16), how))
+
+    def block(self, i):
+        value = self.grads[0][i].astype(F32) + self.moved[0][i].astype(F32)
+        if len(self.moved) > 1:
+            value = value + self.moved[1][i].astype(F32)
+        return value
+
+    def core(self):
+        if self.ring.square:
+            self.across(self.grads[1], self.ring.core)
+
+    def second(self):
+        if self.ring.square:
+            self.across(self.block(slice(2, 4)), self.ring.second)
+
+    def first(self):
+        if self.ring.square:
+            self.across(self.block(1), self.ring.first)
+
+    def own(self, i):
+        if not self.ring.square:
+            return self.whole[i].astype(F32)
+        value = self.grads[0][0, i].astype(F32) + self.moved[2][i].astype(F32)
+        return value + self.moved[0][0, i].astype(F32) + self.moved[1][0, i].astype(F32)
+
+    def shard(self, start):
+        count = self.grads[0].shape[1]
+        for i in range(count):
+            k = i if start == 1 else start + i
+            if k > 0:
+                self.arrived.append(self.ring.z_move(self.own(i).astype(BF16), k))
+
+
+def join_second(low, high):
+    if not low.ring.square:
+        return []
+    part = slice(2, 4)
+    both = jnp.concatenate([low.block(part), high.block(part)], axis=1)
+    return [low.ring.across(both.astype(BF16), low.ring.second)]
+
+
+def join_first(low, high):
+    if not low.ring.square:
+        return []
+    both = jnp.concatenate([low.block(1), high.block(1)], axis=0)
+    return [low.ring.across(both.astype(BF16), low.ring.first)]
+
+
+def join_take(low, high, moved):
+    count = low.grads[0].shape[1]
+    for value in moved:
+        low.moved.append(value[..., :count, :, :])
+        high.moved.append(value[..., count:, :, :])
+
+
+def join_shards(pairs):
+    ring = pairs[0][0].ring
+    half = ring.splits // 2
+    return [
+        ring.z_move(
+            jnp.concatenate([pair[k // half].own(k % half) for pair in pairs], axis=1).astype(BF16),
+            k,
+        )
+        for k in range(1, ring.splits)
+    ]
+
+
+class Gather:
+    def __init__(self, ring, mine):
+        self.ring = ring
+        if ring.square:
+            self.kept, self.other = [mine], []
+        else:
+            self.kept, self.other = [lax.all_gather(mine, "dp", axis=1, tiled=True)], []
+
+    def sides(self):
+        if self.ring.square:
+            self.kept.append(self.ring.across(self.kept[0], self.ring.first))
+            self.kept.append(self.ring.across(self.kept[0], self.ring.second))
+
+    def corner(self):
+        if self.ring.square:
+            self.kept.append(self.ring.across(self.kept[1], self.ring.second))
+
+    def core(self, *which):
+        if self.ring.square:
+            for i in which:
+                self.other.append(self.ring.across(self.kept[i], self.ring.core))
+
+    def pieces(self):
+        return self.kept + self.other
+
+
+def meet(*groups):
+    flat = [v for group in groups for v in group]
+    flat = list(lax.optimization_barrier(tuple(flat)))
+    for group in groups:
+        for i in range(len(group)):
+            group[i] = flat.pop(0)
 
 
 def to_layout(q, k, v, o):
@@ -746,6 +905,17 @@
     return pick(0, 3 * WIN), pick(WIN, 3 * WIN + HD), pick(2 * WIN, 4 * WIN), pick(
         5 * WIN, 4 * WIN + HD
     )
+
+
+def mod_gradients(ring, sums, clips):
+    part = jnp.concatenate(sums, axis=1)[:clips]
+    got = lax.all_to_all(
+        jnp.broadcast_to(part[None], (ring.splits,) + part.shape), "head", 0, 0, tiled=True
+    )
+    low = jnp.sum(got, axis=0).astype(BF16)
+    return lax.all_to_all(
+        jnp.broadcast_to(low[None], (ring.n_dp,) + low.shape), "dp", 0, 0, tiled=True
+    ).reshape(ring.n_dp * clips, -1)
 
 
 def on_device(
@@ -820,7 +990,12 @@
         ],
         axis=2,
     ).reshape(n_dp * splits, -1)
-    got = lax.all_to_all(sent, both, 0, 0, tiled=True).reshape(n_dp, splits, -1)
+    got = lax.all_to_all(sent, both, 0, 0, tiled=True)
+    attn_shards = ring.z_pieces(jnp.concatenate([shard_self, shard_cross], axis=1))
+    mlp_shard = jnp.concatenate([mlp_in_weight, mlp_out_weight.T], axis=1)
+    held = [got]
+    meet(held, attn_shards)
+    got = held[0].reshape(n_dp, splits, -1)
     step_cols = got[:, 0, flat.shape[0] :].reshape(n_dp * clips, shard_rows).astype(F32)
     silu_cols = jax.nn.silu(step_cols).astype(BF16)
     spots = []
@@ -852,18 +1027,22 @@
 
     mod_part = jnp.dot(silu_cols, ada_weight, preferred_element_type=F32)
     mod_got = lax.all_to_all(mod_part.reshape(n_dp, clips, -1), "dp", 0, 0, tiled=True)
-    mod = jnp.sum(mod_got, axis=0) + all_ada_bias
-
+
+    half = splits // 2
+    attn_gather = Gather(ring, jnp.stack(attn_shards))
+    attn_gather.sides()
     frame_blocks = ring.z_pieces(frames_in)
-    pieces_attn = ring.gather(
-        ring.gather_z(jnp.concatenate([shard_self, shard_cross], axis=1))
-    )
-    mlp_mine = ring.gather_z(jnp.concatenate([mlp_in_weight, mlp_out_weight.T], axis=1))
-    if ring.square:
-        mlp_one = ring.across(mlp_mine, ring.first)
-        mlp_two = ring.across(mlp_mine, ring.second)
-    else:
-        pieces_mlp = ring.gather(mlp_mine)
+    held = [mod_got, mlp_shard]
+    meet(held, attn_gather.kept)
+    mlp_shard = held[1]
+    mod = jnp.sum(held[0], axis=0) + all_ada_bias
+    attn_gather.corner()
+    attn_gather.core(0, 1, 2, 3)
+    mlp_shards = ring.z_pieces(mlp_shard, range(1, half))
+    mlp_gathers = [Gather(ring, jnp.stack(mlp_shards))]
+    mlp_gathers[0].sides()
+    mlp_gathers[0].core(0)
+    mlp_late = ring.z_pieces(mlp_shard, range(half, splits))[1:]
 
     def dma(n):
         return pltpu.SemaphoreType.DMA(n)
@@ -879,14 +1058,14 @@
     n_o = len(kept_out)
     shard_type = pltpu.VMEM((splits, D, D), BF16)
 
-    hidden_one, self_kv, self_q, self_att, self_lse, attn_branch, after_self = call(
+    results = list(call(
         partial(self_forward, n_p, splits),
         [("s", scal)]
         + vmem_of(frame_blocks)
         + vmem_of([mod, bias_self, all_attn_bias])
-        + any_of(pieces_attn),
+        + any_of(attn_gather.pieces()),
         [
-            ("v", (count, D), BF16),
+            ("v", (D, count), BF16),
             ("v", (splits, count, 4 * WIN), BF16),
             ("v", (splits, rows, 2 * WIN), BF16),
             ("v", (splits, rows, 2 * WIN), BF16),
@@ -895,6 +1074,7 @@
             ("v", (rows, D), F32),
         ],
         [
+            pltpu.VMEM((count, D), BF16),
             shard_type,
             pltpu.VMEM((count, rows), F32),
             pltpu.VMEM((count, rows), F32),
@@ -903,18 +1083,24 @@
         ],
         22 * US,
         "self_forward",
-    )
-    if ring.square:
-        mlp_mine, mlp_one, mlp_two = (tie(v, after_self) for v in (mlp_mine, mlp_one, mlp_two))
-        after_self = tie(after_self, mlp_one, mlp_two)
-        mlp_three = ring.across(mlp_one, ring.second)
-        mlp_other = [ring.across(v, ring.core) for v in (mlp_mine, mlp_one, mlp_two)]
-    cross_kv, cross_q, cross_att, cross_lse, after_cross = call(
+    ))
+    meet(
+        results, mlp_gathers[0].kept, mlp_gathers[0].other, mlp_late, attn_gather.kept, attn_gather.other
+    )
+    hidden_one, self_kv, self_q, self_att, self_lse, attn_branch, after_self = results
+    mlp_gathers[0].corner()
+    mlp_gathers[0].core(1, 2)
+    mlp_gathers.append(Gather(ring, jnp.stack(mlp_late)))
+    mlp_gathers[1].sides()
+
+    results = list(call(
         partial(cross_forward, n_p, splits),
         [("s", scal)]
         + vmem_of([after_self, text_feats, all_gain, bias_cross, all_cross_bias])
-        + any_of(pieces_attn),
+        + any_of(attn_gather.pieces()),
         [
+            ("v", (D, rows), BF16),
+            ("v", (D, text_count), BF16),
             ("v", (splits, text_count, 4 * WIN), BF16),
             ("v", (splits, rows, 2 * WIN), BF16),
             ("v", (splits, rows, 2 * WIN), BF16),
@@ -930,41 +1116,15 @@
         ],
         17 * US,
         "cross_forward",
-    )
-    if ring.square:
-        mlp_three = tie(mlp_three, after_cross)
-        after_cross = tie(after_cross, mlp_three)
-        pieces_mlp = [mlp_mine, mlp_one, mlp_two, mlp_three] + mlp_other
-        pieces_mlp.append(ring.across(mlp_three, ring.core))
-    results = call(
-        partial(feed_forward, n_p, splits),
-        [("s", scal)]
-        + vmem_of([after_cross, out_grad, mod, all_in_bias, all_out_bias])
-        + any_of(pieces_mlp),
-        [("v", (rows, D), BF16), ("v", (rows, D), F32)]
-        + kept_out
-        + kept_out
-        + [
-            ("v", (splits, 1, D), F32),
-            ("v", (1, D), F32),
-            ("v", (8, 3 * D), F32),
-        ],
-        [
-            pltpu.VMEM((splits, D, 2 * D), BF16),
-            pltpu.VMEM((splits, D, 2 * D), BF16),
-            pltpu.VMEM((rows, D), F32),
-            pltpu.VMEM((rows, D), F32),
-            dma((n_p,)),
-            dma((2 * n_p, splits)),
-        ],
-        17 * US,
-        "feed_forward",
-    )
-    layer_out, d_after_cross = results[:2]
-    grads_in, grads_out = results[2 : 2 + n_o], results[2 + n_o : 2 + 2 * n_o]
-    in_bias_grad, out_bias_grad, sums_two = results[2 + 2 * n_o :]
-    half = splits // 2
+    ))
+    meet(results, mlp_gathers[0].kept, mlp_gathers[0].other, mlp_gathers[1].kept)
+    hidden_two_t, text_t, cross_kv, cross_q, cross_att, cross_lse, after_cross = results
+    mlp_gathers[0].core(3)
+    mlp_gathers[1].corner()
+    mlp_gathers[1].core(0, 1, 2)
+
     kept_half = [(m, (shape[0], half) + shape[2:], kind) for m, shape, kind in kept_out]
+    kept_wide = [(m, shape[:3] + (2 * D,), kind) for m, shape, kind in kept_half]
     half_type = pltpu.VMEM((half, D, D), BF16)
 
     def back_scratch(keys):
@@ -972,21 +1132,64 @@
             half_type,
             half_type,
             pltpu.VMEM((keys, rows), F32),
-            pltpu.VMEM((3, keys, rows), F32),
-            pltpu.VMEM((3, keys, rows), F32),
+            pltpu.VMEM((3, keys, rows), BF16),
+            pltpu.VMEM((3, keys, rows), BF16),
             pltpu.VMEM((keys, 4 * WIN), BF16),
-            pltpu.VMEM((D, keys), BF16),
             dma((n_p,)),
             dma((n_p, half)),
         ]
 
-    if ring.square:
-        core_in = ring.across(grads_in[1], ring.core)
-        core_out = ring.across(grads_out[1], ring.core)
+    bias_type = [("v", (splits, 1, D), F32)]
+    mlp_args = [after_cross, out_grad, mod, all_in_bias, all_out_bias]
+    mlp_scratch = [
+        pltpu.VMEM((half, D, 2 * D), BF16),
+        pltpu.VMEM((half, D, 2 * D), BF16),
+        dma((n_p,)),
+        dma((n_p, half)),
+    ]
+    results = call(
+        partial(feed_forward, n_p, splits, 0, half),
+        [("s", scal)] + vmem_of(mlp_args) + any_of(mlp_gathers[0].pieces()),
+        kept_wide + bias_type + [("v", (rows, D), F32)] * 2,
+        mlp_scratch,
+        9 * US,
+        "feed_forward_first",
+    )
+    results = list(results)
+    meet(results, mlp_gathers[1].kept, mlp_gathers[1].other)
+    mlp_gathers[1].core(3)
+    sum_mlp = [GradSum(ring, results[:n_o])]
+    in_bias_grad, mlp_state, mlp_back = results[n_o:]
+    sum_mlp[0].core()
+    results = call(
+        partial(feed_forward, n_p, splits, half, splits),
+        [("s", scal)]
+        + vmem_of(mlp_args)
+        + any_of(mlp_gathers[1].pieces())
+        + vmem_of([mlp_state, mlp_back, in_bias_grad]),
+        kept_wide
+        + bias_type
+        + [
+            ("v", (rows, D), BF16),
+            ("v", (rows, D), F32),
+            ("v", (1, D), F32),
+            ("v", (8, 3 * D), F32),
+        ],
+        [pltpu.VMEM((rows, D), F32), pltpu.VMEM((rows, D), F32)] + mlp_scratch,
+        10 * US,
+        "feed_forward_last",
+    )
+    results = list(results)
+    meet(results, sum_mlp[0].moved)
+    sum_mlp.append(GradSum(ring, results[:n_o]))
+    in_bias_grad, layer_out, d_after_cross, out_bias_grad, sums_two = results[n_o:]
+    sum_mlp[0].second()
+    sum_mlp[1].core()
     cross_args = [
         d_after_cross,
         after_self,
-        text_feats,
+        hidden_two_t,
+        text_t,
         all_gain,
         mod,
         attn_branch,
@@ -996,29 +1199,26 @@
         cross_lse,
     ]
     cross_state = [("v", (rows, D), F32), ("v", (text_count, D), F32)]
-    bias_type = [("v", (splits, 1, D), F32)]
     results = call(
         partial(cross_backward, n_p, splits, 0, half),
-        [("s", scal)] + vmem_of(cross_args) + any_of(pieces_attn),
+        [("s", scal)] + vmem_of(cross_args) + any_of(attn_gather.pieces()),
         kept_half + bias_type + cross_state,
         back_scratch(text_count),
         14 * US,
         "cross_backward_first",
     )
-    grads_cross = [results[:n_o]]
+    results = list(results)
+    meet(results, sum_mlp[0].moved, sum_mlp[1].moved)
+    sum_cross = [GradSum(ring, results[:n_o])]
     cross_bias_grad, cross_back, text_back = results[n_o:]
-    if ring.square:
-        core_in, core_out = tie(core_in, cross_back), tie(core_out, cross_back)
-        cross_back = tie(cross_back, core_in, core_out)
-        blocks_in = wide_sum(grads_in[0], core_in)
-        blocks_out = wide_sum(grads_out[0], core_out)
-        far_in = ring.send_second(blocks_in)
-        core_cross = [ring.across(grads_cross[0][1], ring.core)]
+    sum_mlp[0].first()
+    sum_mlp[1].second()
+    sum_cross[0].core()
     results = call(
         partial(cross_backward, n_p, splits, half, splits),
         [("s", scal)]
         + vmem_of(cross_args)
-        + any_of(pieces_attn)
+        + any_of(attn_gather.pieces())
         + vmem_of([cross_back, text_back, cross_bias_grad]),
         kept_half
         + bias_type
@@ -1033,46 +1233,49 @@
         15 * US,
         "cross_backward_last",
     )
-    grads_cross.append(results[:n_o])
+    results = list(results)
+    meet(results, sum_mlp[0].moved, sum_mlp[1].moved, sum_cross[0].moved)
+    sum_cross.append(GradSum(ring, results[:n_o]))
     cross_bias_grad, d_after_self, d_attn, text_out, cross_rows, gate_sums = results[n_o:]
+    sum_mlp[0].shard(1)
+    sum_mlp[1].first()
+    sum_cross[0].second()
+    sum_cross[1].core()
+    text_got = lax.all_to_all(
+        text_out.reshape(splits, text_count // splits, D), "head", 0, 0, tiled=True
+    )
     self_args = [d_attn, hidden_one, self_kv, self_q, self_att, self_lse]
-    if ring.square:
-        far_in = tie(far_in, d_attn)
-        core_cross[0] = tie(core_cross[0], d_attn)
-        d_attn = tie(d_attn, far_in, core_cross[0])
-        self_args[0] = d_attn
-        blocks_in = wide_sum(blocks_in[0:2], far_in)
-        near_in = ring.send_first(blocks_in)
-        far_out = ring.send_second(tie(blocks_out, d_attn))
-        core_cross.append(ring.across(grads_cross[1][1], ring.core))
     results = call(
         partial(self_backward, n_p, splits, 0, half),
-        [("s", scal)] + vmem_of(frame_blocks) + vmem_of(self_args) + any_of(pieces_attn),
+        [("s", scal)] + vmem_of(frame_blocks) + vmem_of(self_args) + any_of(attn_gather.pieces()),
         kept_half + bias_type + [("v", (count, D), F32)],
         back_scratch(count),
         17 * US,
         "self_backward_first",
     )
-    grads_self = [results[:n_o]]
+    results = list(results)
+    held = [text_got]
+    meet(
+        results,
+        held,
+        sum_mlp[0].arrived,
+        sum_mlp[1].moved,
+        sum_cross[0].moved,
+        sum_cross[1].moved,
+    )
+    text_got = held[0]
+    sum_self = [GradSum(ring, results[:n_o])]
     self_bias_grad, self_back = results[n_o:]
-    if ring.square:
-        near_in, far_out = tie(near_in, self_back), tie(far_out, self_back)
-        core_cross[1] = tie(core_cross[1], self_back)
-        self_back = tie(self_back, near_in, far_out, core_cross[1])
-        shard_in = wide_sum(blocks_in[0], near_in)
-        blocks_out = wide_sum(blocks_out[0:2], far_out)
-        near_out = ring.send_first(blocks_out)
-        blocks_cross = jnp.concatenate(
-            [wide_sum(g[0], c) for g, c in zip(grads_cross, core_cross)], axis=1
-        )
-        far_cross = ring.send_second(blocks_cross)
-        core_self = [ring.across(grads_self[0][1], ring.core)]
+    sum_mlp[1].shard(2)
+    sum_cross[0].first()
+    sum_cross[1].second()
+    sum_self[0].core()
     results = call(
         partial(self_backward, n_p, splits, half, splits),
         [("s", scal)]
         + vmem_of(frame_blocks)
         + vmem_of(self_args)
-        + any_of(pieces_attn)
+        + any_of(attn_gather.pieces())
         + vmem_of([self_back, self_bias_grad]),
         kept_half
         + bias_type
@@ -1083,12 +1286,67 @@
         18 * US,
         "self_backward_last",
     )
-    grads_self.append(results[:n_o])
+    results = list(results)
+    held = [in_bias_grad, out_bias_grad, cross_bias_grad, cross_rows, gate_sums, sums_two]
+    meet(
+        results,
+        held,
+        sum_mlp[1].arrived,
+        sum_cross[0].moved,
+        sum_cross[1].moved,
+        sum_self[0].moved,
+    )
+    sum_self.append(GradSum(ring, results[:n_o]))
     self_bias_grad, own_part = results[n_o : n_o + 2]
     parts = results[n_o + 2 : n_o + 1 + splits]
     self_rows, sums_one = results[n_o + 1 + splits :]
 
+    sum_self[1].core()
+    sum_cross[1].first()
     arrived = ring.z_back(parts)
+    in_bias_grad, out_bias_grad, cross_bias_grad, cross_rows, gate_sums, sums_two = held
+    small = [self_bias_grad, cross_bias_grad, in_bias_grad, self_rows, cross_rows, out_bias_grad]
+    small += [sums_one, gate_sums, sums_two]
+    far = join_second(*sum_self)
+    early, late = arrived[0::2], arrived[1::2]
+    meet(small, far, sum_cross[1].moved, early)
+    join_take(*sum_self, far)
+    near = join_first(*sum_self)
+    if ring.square:
+        (packed,) = call(
+            pack_small,
+            vmem_of([jnp.asarray(bias_table(n_dp))] + small),
+            [("v", (splits, clips + 2, 6 * D), F32)],
+            [],
+            6 * US,
+            "pack_small",
+        )
+        held = [lax.all_to_all(packed, "head", 0, 0, tiled=True)]
+        got = jnp.sum(held[0], axis=0)
+        mod_low = got[:clips].astype(BF16).astype(F32)
+        bias_low = got[clips:].reshape(-1, 1, D)[:n_dp]
+        sent = jnp.concatenate(
+            [
+                jnp.broadcast_to(mod_low[None], (n_dp,) + mod_low.shape),
+                jnp.pad(bias_low, ((0, 0), (0, 0), (0, 5 * D))),
+            ],
+            axis=1,
+        )
+        held = [lax.all_to_all(sent, "dp", 0, 0, tiled=True)]
+    meet(late, near)
+    arrived = early + late
+    join_take(*sum_self, near)
+    last = join_shards([sum_cross, sum_self])
+    self_bias_grad, cross_bias_grad, in_bias_grad, self_rows, cross_rows, out_bias_grad = small[:6]
+    if ring.square:
+        mod_all = held[0][:, :clips].reshape(n_dp * clips, -1).astype(BF16)
+        bias_sum = jnp.sum(held[0][:, clips, :D], axis=0)
+        places = [0, 24, 2 * WIN, 4 * WIN, 48, 72, 3 * WIN, WIN, 5 * WIN]
+    else:
+        mod_all = mod_gradients(ring, small[6:], clips)
+    step_part = lax.dot_general(
+        mod_all, ada_weight, (((1,), (1,)), ((), ())), preferred_element_type=F32
+    )
     (frames_grad,) = call(
         partial(finish, splits),
         [("s", scal)] + vmem_of([frames_in, mod, d_after_self, own_part]) + vmem_of(arrived),
@@ -1097,19 +1355,8 @@
         3 * US,
         "finish",
     )
-    text_got = lax.all_to_all(
-        text_out.reshape(splits, text_count // splits, D), "head", 0, 0, tiled=True
-    )
     text_grad = jnp.sum(text_got.astype(F32), axis=0)
 
-    mod_partial = jnp.concatenate([sums_one, gate_sums, sums_two], axis=1)[:clips]
-    mod_sum = mod_partial
-    for part in ring.z_back([mod_partial] * (splits - 1)):
-        mod_sum = mod_sum + part
-    mod_low = mod_sum.astype(BF16)
-    mod_all = lax.all_to_all(
-        jnp.broadcast_to(mod_low[None], (n_dp,) + mod_low.shape), "dp", 0, 0, tiled=True
-    ).reshape(n_dp * clips, -1)
     grad_ada = lax.dot_general(
         silu_cols, mod_all, (((0,), (0,)), ((), ())), preferred_element_type=F32
     )
@@ -1118,10 +1365,14 @@
     grad_ada_bias = jnp.sum(
         lax.dynamic_slice_in_dim(mod_all, dp_index * bias_width, bias_width, 1).astype(F32), axis=0
     )
-    step_part = lax.dot_general(
-        mod_all, ada_weight, (((1,), (1,)), ((), ())), preferred_element_type=F32
-    )
     step_got = lax.all_to_all(step_part.reshape(n_dp, clips, shard_rows), "dp", 0, 0, tiled=True)
+    step_got = [step_got]
+    meet(last, step_got)
+    (step_got,) = step_got
+    total_cross, total_self = (
+        pair[0].own(0) + sum(part[:, i * D : (i + 1) * D].astype(F32) for part in last)
+        for i, pair in enumerate((sum_cross, sum_self))
+    )
     step_value = step_embed.astype(F32)
     _, silu_pull = jax.vjp(jax.nn.silu, step_value)
     step_grad = silu_pull(step_got.transpose(1, 0, 2).reshape(clips, D))[0]
@@ -1147,36 +1398,17 @@
         heads_out(in_bias_grad[:, 0]),
         spread(out_bias_grad[0]),
     ]
-    packed = jnp.concatenate(entries, axis=2).reshape(n_dp * splits, -1)
-    bias_sum = jnp.sum(lax.all_to_all(packed, both, 0, 0, tiled=True), axis=0)
-    bias_out = []
-    place = 0
-    for e in entries:
-        bias_out.append(bias_sum[place : place + e.shape[2]])
-        place += e.shape[2]
-
-    if ring.square:
-        total_in = ring.reduce_z(shard_in)
-        total_out = ring.reduce_z(wide_sum(blocks_out[0], near_out))
-        blocks_cross = wide_sum(blocks_cross[0:2], far_cross)
-        total_cross = ring.reduce_z(wide_sum(blocks_cross[0], ring.send_first(blocks_cross)))
-        core_self.append(ring.across(grads_self[1][1], ring.core))
-        blocks_self = jnp.concatenate(
-            [wide_sum(g[0], c) for g, c in zip(grads_self, core_self)], axis=1
+    if not ring.square:
+        packed = jnp.concatenate(entries, axis=2)
+        places = [sum(e.shape[2] for e in entries[:i]) for i in range(len(entries))]
+        bias_sum = jnp.sum(
+            lax.all_to_all(packed.reshape(n_dp * splits, -1), both, 0, 0, tiled=True), axis=0
         )
-        blocks_self = wide_sum(blocks_self[0:2], ring.send_second(blocks_self))
-        total_self = ring.reduce_z(wide_sum(blocks_self[0], ring.send_first(blocks_self)))
-    else:
-
-        def joined(halves):
-            return ring.reduce_z(
-                jnp.concatenate([ring.reduce_other(h) for h in halves], axis=0)
-            )
-
-        total_in = joined([grads_in])
-        total_out = joined([grads_out])
-        total_cross = joined(grads_cross)
-        total_self = joined(grads_self)
+    bias_out = [bias_sum[p : p + e.shape[2]] for p, e in zip(places, entries)]
+
+    total_mlp = sum_mlp[0].own(0) + sum(
+        part.astype(F32) for part in sum_mlp[0].arrived + sum_mlp[1].arrived
+    )
     gq, gk, gv, go = from_layout(total_self)
     hq, hk, hv, ho = from_layout(total_cross)
     return (
@@ -1197,9 +1429,9 @@
         bias_out[5].reshape(cross_v_bias.shape),
         ho.T,
         bias_out[6],
-        total_in,
+        total_mlp[:, :D],
         bias_out[7].reshape(mlp_in_bias.shape),
-        total_out.T,
+        total_mlp[:, D:].T,
         bias_out[8],
     )
 

time: 434 us -> 400 us (0.922)
  waiting for transfers between devices: 104 us -> 70.7 us
  blocking collectives: 0 us -> 24.9 us
  local copies, waits for them, and re-layouts: 49.1 us -> 35 us
  other arithmetic: 45.5 us -> 35.6 us
  starting transfers between devices: 87.8 us -> 82.6 us
    ppermute x9, waiting for transfers between devices: 44.9 us -> 5.67 us  [z_pieces(): lax.ppermute(value, 'head', [(s, (s + k) % n) for s in range(n)])]
    ppermute x18 -> x3, starting transfers between devices: 32.8 us -> 4.94 us  [z_back(): lax.ppermute(parts[k - 1], 'head', [(s, (s - k) % n) for s in range(n)])]
    all_to_all x0 -> x1, blocking collectives: none -> 24.9 us  [on_device(): got = lax.all_to_all(sent, both, 0, 0, tiled=True)]
    add x15 -> x5, other arithmetic: 24.1 us -> 5.4 us  [the longest x1 1.77 us: on_device(): pair[0].own(0)]
    all_to_all x1, waiting for transfers between devices: 0.73 us -> 18 us  [on_device(): lax.all_to_all(mod_part.reshape(n_dp, clips, -1), 'dp', 0, 0, tiled=True)]
    ppermute x0 -> x6, starting transfers between devices: none -> 15.8 us  [z_move(): return lax.ppermute(value, 'head', [(s, (s - k) % n) for s in range(n)])]
    ppermute x28 -> x37, waiting for transfers between devices: 26.1 us -> 10.5 us  [across(): return lax.ppermute(value, 'dp', how)]
    convert_element_type x1 -> x11, other arithmetic: 0.96 us -> 13.7 us  [the longest x8 9.62 us: across(): self.moved.append(self.ring.across(value.astype(BF16), how))]
  transfers between devices with their start and end apart: 61 -> 60, of which waited for: 19 -> 11; matrix products, arithmetic and copies ran while one was open for 21% -> 13% of each run, Pallas kernels for 27% -> 35%
where the time goes in v3:
time: 400 us; the launch traced here: 392 us
  Pallas kernels  138 us (34%)
  starting transfers between devices  82.6 us (21%)
  waiting for transfers between devices  70.7 us (18%)
  other arithmetic  35.6 us (9%)
  local copies, waits for them, and re-layouts  35 us (9%)
  blocking collectives  24.9 us (6%)
    pallas_call x10, Pallas kernels, call(): pl.pallas_call(body, out_shape=tuple((jax.ShapeDtypeStruct(s, t) for _, s...  138 us
    all_to_all x1, blocking collectives, on_device(): got = lax.all_to_all(sent, both, 0, 0, tiled=True)  24.9 us
    ppermute x37, starting transfers between devices, across(): return lax.ppermute(value, 'dp', how)  22.7 us
    all_to_all x1, waiting for transfers between devices, on_device(): lax.all_to_all(mod_part.reshape(n_dp, clips, -1), 'dp', 0, 0, tiled=True)  18 us
    ppermute x6, starting transfers between devices, z_move(): return lax.ppermute(value, 'head', [(s, (s - k) % n) for s in range(n)])  15.8 us
    ppermute x9, starting transfers between devices, z_pieces(): lax.ppermute(value, 'head', [(s, (s + k) % n) for s in range(n)])  15.1 us
    ppermute x3, waiting for transfers between devices, z_back(): lax.ppermute(parts[k - 1], 'head', [(s, (s - k) % n) for s in range(n)])  14 us
    unnamed x142, local copies, waits for them, and re-layouts  13.1 us
  transfers between devices with their start and end apart: 60, of which 11 were waited for; matrix products, arithmetic and copies ran while one was open for 13% of the time, Pallas kernels for 35%

profile of v3, /device:TPU:0, one launch (start us, length us, event | category | flops | bytes accessed | tf_op | source)
XLA Modules:
  0.0 391.8 jit_solution(16246918802303283749)
XLA Ops:
  4.1 5.1 %collective-permute-start.5 = (bf16[96,1536]{1,0:T(8,128)(2,1)S(1)}, bf16[96,1536]{1,0:T(8,128)(2,1)S(1)}, u32[]{:S(2)}, u32[]{:S(2)}) collective-permute-start(bf16[96,1536]{1,0:T(8,128)(2,1)S(1)} %concatenate.68), channel_id=1, source_target_pairs={{0,3},{1,0},{2,1},{3,2},{4,7},{5,4},{6,5},{7,6},{8,11},{9,8},{10,9... | collective-permute-start | bytes 884744 | tf_op jit(solution)/shard_map/ppermute | solution.py:752
  12.9 24.9 %all_to_all.38 = bf16[32,2,720]{2,1,0:T(2,128)(2,1)S(1)} all-to-all(bf16[32,2,720]{2,1,0:T(2,128)(2,1)S(1)} %reshape.420), channel_id=1, replica_groups=mesh['dp'=8,'head'=4] {'dp','head'}, dimensions={0} | all-to-all | bytes 184320 | tf_op jit(solution)/shard_map/all_to_all | solution.py:993
  39.6 3.9 %collective-permute-start.2 = (bf16[256,768]{1,0:T(8,128)(2,1)}, bf16[256,768]{1,0:T(8,128)(2,1)}, u32[]{:S(2)}, u32[]{:S(2)}) collective-permute-start(bf16[256,768]{1,0:T(8,128)(2,1)} %refs_1_.7), channel_id=1, source_target_pairs={{0,3},{1,0},{2,1},{3,2},{4,7},{5,4},{6,5},{7,6},{8,11},{9,8},{10,9... | collective-permute-start | bytes 1179656 | tf_op jit(solution)/shard_map/ppermute | solution.py:752
  51.0 3.9 stack.102.refs_0_
  55.0 18.0 %all-to-all-done.1 = f32[8,3,4608]{2,1,0:T(4,128)S(1)} async-done(((f32[8,3,4608]{2,1,0:T(4,128)}), f32[8,3,4608]{2,1,0:T(4,128)S(1)}, u32[]{:S(2)}, u32[]{:S(2)}) %all-to-all-start.1) | async-done | bytes 442400 | tf_op jit(solution)/shard_map/all_to_all | solution.py:1029
  79.7 5.7 %collective-permute-done.13 = bf16[96,1536]{1,0:T(8,128)(2,1)} collective-permute-done((bf16[96,1536]{1,0:T(8,128)(2,1)S(1)}, bf16[96,1536]{1,0:T(8,128)(2,1)}, u32[]{:S(2)}, u32[]{:S(2)}) %collective-permute-start.13) | collective-permute-done | bytes 294944 | tf_op jit(solution)/shard_map/ppermute | solution.py:752
  85.3 4.2 %collective-permute-done.8.refs_11_.refs_9_.refs_15_.refs_14_ = bf16[4,96,1536]{2,1,0:T(8,128)(2,1)} collective-permute-done((bf16[4,96,1536]{2,1,0:T(8,128)(2,1)}, bf16[4,96,1536]{2,1,0:T(8,128)(2,1)}, u32[]{:S(2)}, u32[]{:S(2)}) %collective-permute-start.8) | collective-permute-done | bytes 1179680 | tf_op jit(solution)/shard_map/ppermute | solution.py:764
  91.2 3.8 collective-permute-start.18
  98.4 19.1 %self_forward.1 = (bf16[768,1024]{1,0:T(8,128)(2,1)}, bf16[4,1024,512]{2,1,0:T(8,128)(2,1)}, bf16[4,256,256]{2,1,0:T(8,128)(2,1)}, bf16[4,256,256]{2,1,0:T(8,128...) custom-call(s32[16]{0:T(128)} %stack.102.refs_0_, bf16[256,768]{1,0:T(8,128)(2,1)} %refs_1_.7, ...), custom_call_target="tpu_custom_call" | custom-call | flops 25300000768 | bytes 19502144 | tf_op jit(solution)/shard_map/self_forward/pallas_call | solution.py:708
  121.2 17.4 %cross_forward.1 = (bf16[768,256]{1,0:T(8,128)(2,1)}, bf16[768,768]{1,0:T(8,128)(2,1)}, bf16[4,768,512]{2,1,0:T(8,128)(2,1)}, bf16[4,256,256]{2,1,0:T(8,128)(2,1...) custom-call(s32[16]{0:T(128)} %stack.102.refs_0_, ...), custom_call_target="tpu_custom_call" | custom-call | flops 19549999104 | bytes 18008128 | tf_op jit(solution)/shard_map/cross_forward/pallas_call | solution.py:708
  144.4 11.0 %feed_forward_first.1 = (bf16[4,2,96,1536]{3,2,1,0:T(8,128)(2,1)}, bf16[4,2,96,1536]{3,2,1,0:T(8,128)(2,1)}, f32[4,1,768]{2,1,0:T(1,128)}, f32[256,768]{1,0:T(8,128)}, f32[256,768]{1,0:T(8,128)}) custom-call(s32[16]{0:T(128)} %stack.102.refs_0_, f32[256,768]{1,0:T(8,128)} %get-tuple-element.258.refs_1_, bf16[256,768]{1,0:T(8,128)(2,1)} %refs_2_.5, ...), custom_call_target="tpu_custom_call" | custom-call | flops 10350000128 | bytes 12272704 | tf_op jit(solution)/shard_map/feed_forward_first/pallas_call | solution.py:708
  157.4 5.1 %collective-permute-done.29.refs_13_ = bf16[2,96,1536]{2,1,0:T(8,128)(2,1)S(1)} collective-permute-done((bf16[2,96,1536]{2,1,0:T(8,128)(2,1)}, bf16[2,96,1536]{2,1,0:T(8,128)(2,1)S(1)}, u32[]{:S(2)}, u32[]{:S(2)}) %collective-permute-start.29) | collective-permute-done | bytes 589856 | tf_op jit(solution)/shard_map/ppermute | solution.py:764
  163.3 11.9 %feed_forward_last.1 = (bf16[4,2,96,1536]{3,2,1,0:T(8,128)(2,1)}, bf16[4,2,96,1536]{3,2,1,0:T(8,128)(2,1)}, f32[4,1,768]{2,1,0:T(1,128)}, bf16[256,768]{1,0:T(8,...) custom-call(s32[16]{0:T(128)} %stack.102.refs_0_, f32[256,768]{1,0:T(8,128)} %get-tuple-element.258.refs_1_, ...), custom_call_target="tpu_custom_call" | custom-call | flops 11500000256 | bytes 13541440 | tf_op jit(solution)/shard_map/feed_forward_last/pallas_call | solution.py:708
  177.8 15.9 %cross_backward_first.1 = (bf16[4,2,96,768]{3,2,1,0:T(8,128)(2,1)}, bf16[4,2,96,768]{3,2,1,0:T(8,128)(2,1)}, f32[4,1,768]{2,1,0:T(1,128)}, f32[256,768]{1,0:T(8,128)}, f32[768,768]{1,0:T(8,128)}) custom-call(s32[16]{0:T(128)} %stack.102.refs_0_, f32[256,768]{1,0:T(8,128)} %get-tuple-element.293.refs_1_, f32[256,768]{1,0:T(8,128)} %get-tuple-element.236.refs_1_.refs_2_, ...), custom_call_target="tpu_custom_call" | custom-call | flops 16099999744 | bytes 23172160 | tf_op jit(solution)/shard_map/cross_backward_first/pallas_call | solution.py:708
  199.9 18.0 %cross_backward_last.1 = (bf16[4,2,96,768]{3,2,1,0:T(8,128)(2,1)}, bf16[4,2,96,768]{3,2,1,0:T(8,128)(2,1)}, f32[4,1,768]{2,1,0:T(1,128)}, f32[256,768]{1,0:T(8,1...) custom-call(s32[16]{0:T(128)} %stack.102.refs_0_, ...), custom_call_target="tpu_custom_call" | custom-call | flops 17250000896 | bytes 25592896 | tf_op jit(solution)/shard_map/cross_backward_last/pallas_call | solution.py:708
  219.0 4.1 %all-to-all-start.2 = ((bf16[4,192,768]{2,1,0:T(8,128)(2,1)}), bf16[4,192,768]{2,1,0:T(8,128)(2,1)S(1)}, u32[]{:S(2)}, u32[]{:S(2)}) async-start(bf16[4,192,768]{2,1,0:T(8,128)(2,1)} %bitcast.266), calls=%async_computation.2 | async-start | bytes 2359296 | tf_op jit(solution)/shard_map/all_to_all | solution.py:1244
  224.6 3.9 collective-permute-start.36
  232.0 17.5 %self_backward_first.1 = (bf16[4,2,96,768]{3,2,1,0:T(8,128)(2,1)}, bf16[4,2,96,768]{3,2,1,0:T(8,128)(2,1)}, f32[4,1,768]{2,1,0:T(1,128)}, f32[1024,768]{1,0:T(8,128)}) custom-call(s32[16]{0:T(128)} %stack.102.refs_0_, bf16[256,768]{1,0:T(8,128)(2,1)} %refs_1_.7, bf16[256,768]{1,0:T(8,128)(2,1)} %collective-permute-done.refs_2_, ...), custom_call_target="tpu_custom_call" | custom-call | flops 19549999104 | bytes 23769152 | tf_op jit(solution)/shard_map/self_backward_first/pallas_call | solution.py:708
  257.1 8.5 %collective-permute-start.41 = (bf16[96,1536]{1,0:T(8,128)(2,1)S(1)}, bf16[96,1536]{1,0:T(8,128)(2,1)S(1)}, u32[]{:S(2)}, u32[]{:S(2)}) collective-permute-start(bf16[96,1536]{1,0:T(8,128)(2,1)S(1)} %get-tuple-element.547), channel_id=1, source_target_pairs={{0,1},{1,2},{2,3},{3,0},{4,5},{5,6},{6,7},{7,4},{8,9},{9,10},{10,1... | collective-permute-start | bytes 884744 | tf_op jit(solution)/shard_map/ppermute | solution.py:768
  267.2 20.9 %self_backward_last.1 = (bf16[4,2,96,768]{3,2,1,0:T(8,128)(2,1)}, bf16[4,2,96,768]{3,2,1,0:T(8,128)(2,1)}, f32[4,1,768]{2,1,0:T(1,128)}, f32[256,768]{1,0:T(8,12...) custom-call(s32[16]{0:T(128)} %stack.102.refs_0_, ...), custom_call_target="tpu_custom_call" | custom-call | flops 20700000256 | bytes 25821248 | tf_op jit(solution)/shard_map/self_backward_last/pallas_call | solution.py:708
  310.0 11.0 %collective-permute-done.49.refs_6_ = bf16[256,768]{1,0:T(8,128)(2,1)} collective-permute-done((bf16[256,768]{1,0:T(8,128)(2,1)S(1)}, bf16[256,768]{1,0:T(8,128)(2,1)}, u32[]{:S(2)}, u32[]{:S(2)}) %collective-permute-start.49) | collective-permute-done | bytes 393248 | tf_op jit(solution)/shard_map/ppermute | solution.py:759
  323.7 9.4 %all-to-all-start.3 = ((f32[4,5,4608]{2,1,0:T(8,128)}), f32[4,5,4608]{2,1,0:T(8,128)S(1)}, u32[]{:S(2)}, u32[]{:S(2)}) async-start(f32[4,5,4608]{2,1,0:T(8,128)} %pack_small.1), calls=%async_computation.3 | async-start | bytes 1179648 | tf_op jit(solution)/shard_map/all_to_all | solution.py:1324
  337.2 10.4 %all-to-all-done.3 = f32[4,5,4608]{2,1,0:T(8,128)S(1)} async-done(((f32[4,5,4608]{2,1,0:T(8,128)}), f32[4,5,4608]{2,1,0:T(8,128)S(1)}, u32[]{:S(2)}, u32[]{:S(2)}) %all-to-all-start.3) | async-done | bytes 368672 | tf_op jit(solution)/shard_map/all_to_all | solution.py:1324
  375.7 8.7 %collective-permute-done.53 = bf16[96,1536]{1,0:T(8,128)(2,1)} collective-permute-done((bf16[96,1536]{1,0:T(8,128)(2,1)S(1)}, bf16[96,1536]{1,0:T(8,128)(2,1)}, u32[]{:S(2)}, u32[]{:S(2)}) %collective-permute-start.53) | collective-permute-done | bytes 294944 | tf_op jit(solution)/shard_map/ppermute | solution.py:768
  (410 shorter events, 126.6 us)
Async XLA Ops:
  4.1 34.0 %collective-permute-start.5 = (bf16[96,1536]{1,0:T(8,128)(2,1)S(1)}, bf16[96,1536]{1,0:T(8,128)(2,1)S(1)}, u32[]{:S(2)}, u32[]{:S(2)}) collective-permute-start(bf16[96,1536]{1,0:T(8,128)(2,1)S(1)} %concatenate.68), channel_id=1, source_target_pairs={{0,3},{1,0},{2,1},{3,2},{4,7},{5,4},{6,5},{7,6},{8,11},{9,8},{10,9... | collective-permute-start | bytes 884744 | tf_op jit(solution)/shard_map/ppermute | solution.py:752
  9.2 28.9 %collective-permute-start.4 = (bf16[96,1536]{1,0:T(8,128)(2,1)S(1)}, bf16[96,1536]{1,0:T(8,128)(2,1)S(1)}, u32[]{:S(2)}, u32[]{:S(2)}) collective-permute-start(bf16[96,1536]{1,0:T(8,128)(2,1)S(1)} %concatenate.68), channel_id=1, source_target_pairs={{0,2},{1,3},{2,0},{3,1},{4,6},{5,7},{6,4},{7,5},{8,10},{9,11},{10,... | collective-permute-start | bytes 884744 | tf_op jit(solution)/shard_map/ppermute | solution.py:752
  9.2 28.9 %collective-permute-start.3 = (bf16[96,1536]{1,0:T(8,128)(2,1)S(1)}, bf16[96,1536]{1,0:T(8,128)(2,1)S(1)}, u32[]{:S(2)}, u32[]{:S(2)}) collective-permute-start(bf16[96,1536]{1,0:T(8,128)(2,1)S(1)} %concatenate.68), channel_id=1, source_target_pairs={{0,1},{1,2},{2,3},{3,0},{4,5},{5,6},{6,7},{7,4},{8,9},{9,10},{10,1... | collective-permute-start | bytes 884744 | tf_op jit(solution)/shard_map/ppermute | solution.py:752
  38.2 34.8 %collective-permute-start.7 = (bf16[4,96,1536]{2,1,0:T(8,128)(2,1)S(1)}, bf16[4,96,1536]{2,1,0:T(8,128)(2,1)}, u32[]{:S(2)}, u32[]{:S(2)}) collective-permute-start(bf16[4,96,1536]{2,1,0:T(8,128)(2,1)S(1)} %pad_maximum_fusion.refs_8_.refs_6_.refs_12_.refs_11_), channel_id=1, source_target_pairs={{0,16},{4,12},{8,24},{12,4},{16,0},{20,28},{24,8},{28,20},{1,17},{... | collective-permute-start | bytes 3538952 | tf_op jit(solution)/shard_map/ppermute | solution.py:764
  39.0 34.0 %collective-permute-start.6 = (bf16[4,96,1536]{2,1,0:T(8,128)(2,1)S(1)}, bf16[4,96,1536]{2,1,0:T(8,128)(2,1)}, u32[]{:S(2)}, u32[]{:S(2)}) collective-permute-start(bf16[4,96,1536]{2,1,0:T(8,128)(2,1)S(1)} %pad_maximum_fusion.refs_8_.refs_6_.refs_12_.refs_11_), channel_id=1, source_target_pairs={{0,8},{4,20},{8,0},{12,28},{16,24},{20,4},{24,16},{28,12},{1,9},{5... | collective-permute-start | bytes 3538952 | tf_op jit(solution)/shard_map/ppermute | solution.py:764
  39.6 39.5 %collective-permute-start.2 = (bf16[256,768]{1,0:T(8,128)(2,1)}, bf16[256,768]{1,0:T(8,128)(2,1)}, u32[]{:S(2)}, u32[]{:S(2)}) collective-permute-start(bf16[256,768]{1,0:T(8,128)(2,1)} %refs_1_.7), channel_id=1, source_target_pairs={{0,3},{1,0},{2,1},{3,2},{4,7},{5,4},{6,5},{7,6},{8,11},{9,8},{10,9... | collective-permute-start | bytes 1179656 | tf_op jit(solution)/shard_map/ppermute | solution.py:752
  43.5 35.6 %collective-permute-start.1 = (bf16[256,768]{1,0:T(8,128)(2,1)}, bf16[256,768]{1,0:T(8,128)(2,1)}, u32[]{:S(2)}, u32[]{:S(2)}) collective-permute-start(bf16[256,768]{1,0:T(8,128)(2,1)} %refs_1_.7), channel_id=1, source_target_pairs={{0,2},{1,3},{2,0},{3,1},{4,6},{5,7},{6,4},{7,5},{8,10},{9,11},{10,... | collective-permute-start | bytes 1179656 | tf_op jit(solution)/shard_map/ppermute | solution.py:752
  43.5 47.7 %collective-permute-start = (bf16[256,768]{1,0:T(8,128)(2,1)}, bf16[256,768]{1,0:T(8,128)(2,1)}, u32[]{:S(2)}, u32[]{:S(2)}) collective-permute-start(bf16[256,768]{1,0:T(8,128)(2,1)} %refs_1_.7), channel_id=1, source_target_pairs={{0,1},{1,2},{2,3},{3,0},{4,5},{5,6},{6,7},{7,4},{8,9},{9,10},{10,1... | collective-permute-start | bytes 1179656 | tf_op jit(solution)/shard_map/ppermute | solution.py:752
  46.2 26.8 %all-to-all-start.1 = ((f32[8,3,4608]{2,1,0:T(4,128)}), f32[8,3,4608]{2,1,0:T(4,128)S(1)}, u32[]{:S(2)}, u32[]{:S(2)}) async-start(f32[8,3,4608]{2,1,0:T(4,128)} %copy.163), calls=%async_computation.1 | async-start | bytes 1179648 | tf_op jit(solution)/shard_map/all_to_all | solution.py:1029
  91.2 26.3 %collective-permute-start.18 = (bf16[96,1536]{1,0:T(8,128)(2,1)S(1)}, bf16[96,1536]{1,0:T(8,128)(2,1)S(1)}, u32[]{:S(2)}, u32[]{:S(2)}) collective-permute-start(bf16[96,1536]{1,0:T(8,128)(2,1)S(1)} %pad_maximum_fusion.5), channel_id=1, source_target_pairs={{0,3},{1,0},{2,1},{3,2},{4,7},{5,4},{6,5},{7,6},{8,11},{9,8},{10,9... | collective-permute-start | bytes 884744 | tf_op jit(solution)/shard_map/ppermute | solution.py:752
  95.1 22.5 %collective-permute-start.17 = (bf16[96,1536]{1,0:T(8,128)(2,1)S(1)}, bf16[96,1536]{1,0:T(8,128)(2,1)S(1)}, u32[]{:S(2)}, u32[]{:S(2)}) collective-permute-start(bf16[96,1536]{1,0:T(8,128)(2,1)S(1)} %pad_maximum_fusion.5), channel_id=1, source_target_pairs={{0,2},{1,3},{2,0},{3,1},{4,6},{5,7},{6,4},{7,5},{8,10},{9,11},{10,... | collective-permute-start | bytes 884744 | tf_op jit(solution)/shard_map/ppermute | solution.py:752
  95.1 22.4 %collective-permute-start.16 = (bf16[2,96,1536]{2,1,0:T(8,128)(2,1)S(1)}, bf16[2,96,1536]{2,1,0:T(8,128)(2,1)S(1)}, u32[]{:S(2)}, u32[]{:S(2)}) collective-permute-start(bf16[2,96,1536]{2,1,0:T(8,128)(2,1)S(1)} %pad_maximum_fusion.2.refs_6_), channel_id=1, source_target_pairs={{0,4},{4,0},{8,12},{12,8},{16,20},{20,16},{24,28},{28,24},{1,5},{5... | collective-permute-start | bytes 1769480 | tf_op jit(solution)/shard_map/ppermute | solution.py:764
  95.4 22.2 %collective-permute-start.15 = (bf16[2,96,1536]{2,1,0:T(8,128)(2,1)S(1)}, bf16[2,96,1536]{2,1,0:T(8,128)(2,1)}, u32[]{:S(2)}, u32[]{:S(2)}) collective-permute-start(bf16[2,96,1536]{2,1,0:T(8,128)(2,1)S(1)} %pad_maximum_fusion.2.refs_6_), channel_id=1, source_target_pairs={{0,16},{4,12},{8,24},{12,4},{16,0},{20,28},{24,8},{28,20},{1,17},{... | collective-permute-start | bytes 1769480 | tf_op jit(solution)/shard_map/ppermute | solution.py:764
  219.0 34.0 %all-to-all-start.2 = ((bf16[4,192,768]{2,1,0:T(8,128)(2,1)}), bf16[4,192,768]{2,1,0:T(8,128)(2,1)S(1)}, u32[]{:S(2)}, u32[]{:S(2)}) async-start(bf16[4,192,768]{2,1,0:T(8,128)(2,1)} %bitcast.266), calls=%async_computation.2 | async-start | bytes 2359296 | tf_op jit(solution)/shard_map/all_to_all | solution.py:1244
  224.6 25.0 %collective-permute-start.36 = (bf16[96,1536]{1,0:T(8,128)(2,1)S(1)}, bf16[96,1536]{1,0:T(8,128)(2,1)S(1)}, u32[]{:S(2)}, u32[]{:S(2)}) collective-permute-start(bf16[96,1536]{1,0:T(8,128)(2,1)S(1)} %fusion.9), channel_id=1, source_target_pairs={{0,3},{1,0},{2,1},{3,2},{4,7},{5,4},{6,5},{7,6},{8,11},{9,8},{10,9... | collective-permute-start | bytes 884744 | tf_op jit(solution)/shard_map/ppermute | solution.py:768
  254.4 33.7 %collective-permute-start.42 = (bf16[2,96,768]{2,1,0:T(8,128)(2,1)S(1)}, bf16[2,96,768]{2,1,0:T(8,128)(2,1)}, u32[]{:S(2)}, u32[]{:S(2)}) collective-permute-start(bf16[2,96,768]{2,1,0:T(8,128)(2,1)S(1)} %fusion.10), channel_id=1, source_target_pairs={{0,8},{4,20},{8,0},{12,28},{16,24},{20,4},{24,16},{28,12},{1,9},{5... | collective-permute-start | bytes 884744 | tf_op jit(solution)/shard_map/ppermute | solution.py:764
  257.1 31.0 %collective-permute-start.41 = (bf16[96,1536]{1,0:T(8,128)(2,1)S(1)}, bf16[96,1536]{1,0:T(8,128)(2,1)S(1)}, u32[]{:S(2)}, u32[]{:S(2)}) collective-permute-start(bf16[96,1536]{1,0:T(8,128)(2,1)S(1)} %get-tuple-element.547), channel_id=1, source_target_pairs={{0,1},{1,2},{2,3},{3,0},{4,5},{5,6},{6,7},{7,4},{8,9},{9,10},{10,1... | collective-permute-start | bytes 884744 | tf_op jit(solution)/shard_map/ppermute | solution.py:768
  265.6 22.5 %collective-permute-start.40 = (bf16[96,1536]{1,0:T(8,128)(2,1)S(1)}, bf16[96,1536]{1,0:T(8,128)(2,1)S(1)}, u32[]{:S(2)}, u32[]{:S(2)}) collective-permute-start(bf16[96,1536]{1,0:T(8,128)(2,1)S(1)} %get-tuple-element.548), channel_id=1, source_target_pairs={{0,2},{1,3},{2,0},{3,1},{4,6},{5,7},{6,4},{7,5},{8,10},{9,11},{10,... | collective-permute-start | bytes 884744 | tf_op jit(solution)/shard_map/ppermute | solution.py:768
  265.8 22.4 %collective-permute-start.43 = (bf16[2,2,96,768]{3,2,1,0:T(8,128)(2,1)S(1)}, bf16[2,2,96,768]{3,2,1,0:T(8,128)(2,1)S(1)}, u32[]{:S(2)}, u32[]{:S(2)}) collective-permute-start(bf16[2,2,96,768]{3,2,1,0:T(8,128)(2,1)S(1)} %add_convert_fusion.4), channel_id=1, source_target_pairs={{0,16},{4,12},{8,24},{12,4},{16,0},{20,28},{24,8},{28,20},{1,17},{... | collective-permute-start | bytes 1769480 | tf_op jit(solution)/shard_map/ppermute | solution.py:764
  294.8 26.2 %collective-permute-start.46 = (bf16[2,4,96,768]{3,2,1,0:T(8,128)(2,1)S(1)}, bf16[2,4,96,768]{3,2,1,0:T(8,128)(2,1)}, u32[]{:S(2)}, u32[]{:S(2)}) collective-permute-start(bf16[2,4,96,768]{3,2,1,0:T(8,128)(2,1)S(1)} %pad_maximum_fusion.1), channel_id=1, source_target_pairs={{0,16},{4,12},{8,24},{12,4},{16,0},{20,28},{24,8},{28,20},{1,17},{... | collective-permute-start | bytes 3538952 | tf_op jit(solution)/shard_map/ppermute | solution.py:764
  300.4 54.4 %collective-permute-start.50 = (bf16[256,768]{1,0:T(8,128)(2,1)}, bf16[256,768]{1,0:T(8,128)(2,1)}, u32[]{:S(2)}, u32[]{:S(2)}) collective-permute-start(bf16[256,768]{1,0:T(8,128)(2,1)} %get-tuple-element.390), channel_id=1, source_target_pairs={{0,2},{1,3},{2,0},{3,1},{4,6},{5,7},{6,4},{7,5},{8,10},{9,11},{10,... | collective-permute-start | bytes 1179656 | tf_op jit(solution)/shard_map/ppermute | solution.py:759
  323.7 23.8 %all-to-all-start.3 = ((f32[4,5,4608]{2,1,0:T(8,128)}), f32[4,5,4608]{2,1,0:T(8,128)S(1)}, u32[]{:S(2)}, u32[]{:S(2)}) async-start(f32[4,5,4608]{2,1,0:T(8,128)} %pack_small.1), calls=%async_computation.3 | async-start | bytes 1179648 | tf_op jit(solution)/shard_map/all_to_all | solution.py:1324
  359.3 25.1 %collective-permute-start.53 = (bf16[96,1536]{1,0:T(8,128)(2,1)S(1)}, bf16[96,1536]{1,0:T(8,128)(2,1)}, u32[]{:S(2)}, u32[]{:S(2)}) collective-permute-start(bf16[96,1536]{1,0:T(8,128)(2,1)S(1)} %pad_maximum_fusion.7), channel_id=1, source_target_pairs={{0,2},{1,3},{2,0},{3,1},{4,6},{5,7},{6,4},{7,5},{8,10},{9,11},{10,... | collective-permute-start | bytes 884744 | tf_op jit(solution)/shard_map/ppermute | solution.py:768
  359.5 25.0 %collective-permute-start.54 = (bf16[96,1536]{1,0:T(8,128)(2,1)S(1)}, bf16[96,1536]{1,0:T(8,128)(2,1)}, u32[]{:S(2)}, u32[]{:S(2)}) collective-permute-start(bf16[96,1536]{1,0:T(8,128)(2,1)S(1)} %pad_maximum_fusion.8), channel_id=1, source_target_pairs={{0,1},{1,2},{2,3},{3,0},{4,5},{5,6},{6,7},{7,4},{8,9},{9,10},{10,1... | collective-permute-start | bytes 884744 | tf_op jit(solution)/shard_map/ppermute | solution.py:768
  (103 other events, 1096.4 us)

commit v4 on v3

--- a/solution.py
+++ b/solution.py
@@ -510,10 +510,14 @@
         return carry
 
     lax.fori_loop(0, high - low, one, 0)
-    for i in range(high - low):
-        for copy in store_copies(gbuf, i, grads, store_sems, scal):
-            copy.wait()
+
+    def finish_stores():
+        for i in range(high - low):
+            for copy in store_copies(gbuf, i, grads, store_sems, scal):
+                copy.wait()
+
     if not last:
+        finish_stores()
         return
     row_grads[...] = jnp.zeros_like(row_grads)
     row_grads[0:1, :] = jnp.sum(given_wide, axis=0, keepdims=True)
@@ -526,9 +530,50 @@
     d_attn[...] = (total * per_row(mod, 2, clip)).astype(BF16)
     sums[...] = clip_sums(own_clip_row(scal, rows, splits), total * branch[...])
     text_out[...] = text_back[...].astype(BF16)
-
-
-def self_backward(n_p, splits, low, high, *refs):
+    finish_stores()
+
+
+def pack_small(table, own, cross, inner, given_sum, cross_rows, out_row, first, gate, second, out):
+    n_dp = table.shape[1] // WIN
+    splits, clips = out.shape[0], 3
+    lane = lax.broadcasted_iota(jnp.int32, (D, n_dp * WIN), 0)
+
+    def moved(value, which):
+        choose = (lane == table[which : which + 1, :]).astype(F32).astype(BF16)
+        high = value.astype(BF16).astype(F32)
+        middle = (value - high).astype(BF16).astype(F32)
+        parts = jnp.concatenate([high, middle, value - high - middle], axis=0).astype(BF16)
+        found = nn(parts, choose)
+        count = value.shape[0]
+        return found[:count] + found[count : 2 * count] + found[2 * count :]
+
+    def by_shard(ref):
+        return jnp.concatenate([ref[z] for z in range(splits)], axis=0)
+
+    both = moved(jnp.concatenate([by_shard(own), by_shard(cross)], axis=0), 0)
+    heads = both[:splits] + pltpu.roll(both[splits:], 48, 1)
+    hidden = moved(by_shard(inner), 1)
+    rows = moved(
+        jnp.concatenate(
+            [given_sum, cross_rows[0:2, :], out_row[...]] + [jnp.zeros((4, D), F32)], axis=0
+        ),
+        2,
+    )
+    out[...] = jnp.zeros_like(out)
+    for z in range(splits):
+        for c in range(clips):
+            for j in range(6):
+                source, col = ((first, j), (gate, 0), (second, j - 3))[(j > 1) + (j > 2)]
+                out[z, c * 6 + j : c * 6 + j + 1, :] = source[c : c + 1, col * D : (col + 1) * D]
+        for d in range(n_dp):
+            span = slice(d * WIN, (d + 1) * WIN)
+            parts = [heads[z : z + 1, span], hidden[z : z + 1, span]]
+            parts += [rows[r : r + 1, span] for r in range(4)]
+            spot = clips * 6 + d
+            out[z, spot : spot + 1, :] = jnp.concatenate(parts, axis=1)
+
+
+def self_backward(n_p, splits, low, high, small, *refs):
     scal = refs[0]
     frames = refs[1 : 1 + splits]
     given_ref, hidden_t, kv_in, q_in, att_in, lse = refs[1 + splits : 7 + splits]
@@ -538,6 +583,9 @@
     if not first:
         back_in, bias_in = rest[:2]
         rest = rest[2:]
+    if small:
+        table, cross_bias, inner_bias, cross_rows, out_row, gate, second = rest[:7]
+        rest = rest[7:]
     n_o = 2 if n_p > 1 else 1
     grads = rest[:n_o]
     bias_grad = rest[n_o]
@@ -545,8 +593,14 @@
     if last:
         own = rest[0]
         parts = rest[1:splits]
-        row_grads, sums, back = rest[splits : splits + 3]
-        rest = rest[splits + 3 :]
+        row_grads, sums = rest[splits : splits + 2]
+        rest = rest[splits + 2 :]
+        if small:
+            own_small, small_rows, back = rest[0], rest[1], rest[2]
+            rest = rest[3:]
+        else:
+            back = rest[0]
+            rest = rest[1:]
     else:
         back = rest[0]
         rest = rest[1:]
@@ -609,13 +663,18 @@
         return carry
 
     lax.fori_loop(0, high - low, one, 0)
-    for i in range(high - low):
-        for copy in store_copies(gbuf, i, grads, store_sems, scal):
-            copy.wait()
+
+    def finish_stores():
+        for i in range(high - low):
+            for copy in store_copies(gbuf, i, grads, store_sems, scal):
+                copy.wait()
+
     if not last:
+        finish_stores()
         return
+    given_sum = jnp.sum(given_wide, axis=0, keepdims=True)
     row_grads[...] = jnp.zeros_like(row_grads)
-    row_grads[0:1, :] = jnp.sum(given_wide, axis=0, keepdims=True)
+    row_grads[0:1, :] = given_sum
     shift = jnp.zeros((8, D), F32)
     scale = jnp.zeros((8, D), F32)
     for block in range(splits):
@@ -623,13 +682,34 @@
         if block == 0:
             own[...] = value
         else:
-            parts[block - 1][...] = value.astype(BF16)
+            parts[block - 1][0:rows, :] = value.astype(BF16)
         normed, _ = normalize(frames[block][...].astype(F32))
         clip_row = own_clip_row(scal, rows, splits, block)
         shift = shift + clip_sums(clip_row, value)
         scale = scale + clip_sums(clip_row, value * normed)
     sums[:, 0:D] = shift
     sums[:, D:] = scale
+    if small:
+        pack_small(
+            table,
+            bias_grad,
+            cross_bias,
+            inner_bias,
+            given_sum,
+            cross_rows,
+            out_row,
+            sums,
+            gate,
+            second,
+            small_rows,
+        )
+        for k in range(splits):
+            value = small_rows[shard_index(scal, k, splits)]
+            if k == 0:
+                own_small[...] = value
+            else:
+                parts[k - 1][rows:, :] = value.astype(BF16)
+    finish_stores()
 
 
 def finish(splits, *refs):
@@ -639,50 +719,10 @@
     rows = frames.shape[0]
     value = own[...]
     for part in parts:
-        value = value + part[...].astype(F32)
+        value = value + part[0 : own.shape[0], :].astype(F32)
     normed, inverse = normalize(frames[...].astype(F32))
     scale = 1.0 + per_row(mod, 1, own_clip(scal, rows, splits))
     out[...] = d_after[...] + normalize_back(value * scale, normed, inverse)
-
-
-def pack_small(
-    table, own, cross, inner, own_rows, cross_rows, out_row, first, gate, second, packed
-):
-    n_dp = table.shape[1] // WIN
-    splits, clips = packed.shape[0], packed.shape[1] - 2
-    for z in range(splits):
-        packed[z, 0:clips, 0 : 2 * D] = first[0:clips, :]
-        packed[z, 0:clips, 2 * D : 3 * D] = gate[0:clips, :]
-        packed[z, 0:clips, 3 * D :] = second[0:clips, :]
-    packed[:, clips + 1, :] = jnp.zeros((splits, 6 * D), F32)
-    lane = lax.broadcasted_iota(jnp.int32, (D, n_dp * WIN), 0)
-
-    def moved(value, which):
-        choose = (lane == table[which : which + 1, :]).astype(F32).astype(BF16)
-        high = value.astype(BF16).astype(F32)
-        middle = (value - high).astype(BF16).astype(F32)
-        parts = jnp.concatenate([high, middle, value - high - middle], axis=0).astype(BF16)
-        found = nn(parts, choose)
-        count = value.shape[0]
-        return found[:count] + found[count : 2 * count] + found[2 * count :]
-
-    def by_shard(ref):
-        return jnp.concatenate([ref[z] for z in range(splits)], axis=0)
-
-    both = moved(jnp.concatenate([by_shard(own), by_shard(cross)], axis=0), 0)
-    heads = both[:splits] + pltpu.roll(both[splits:], 48, 1)
-    hidden = moved(by_shard(inner), 1)
-    rows = moved(
-        jnp.concatenate(
-            [own_rows[0:1, :], cross_rows[0:2, :], out_row[...]] + [jnp.zeros((4, D), F32)], axis=0
-        ),
-        2,
-    )
-    for d in range(n_dp):
-        span = slice(d * WIN, (d + 1) * WIN)
-        parts = [heads[:, span], hidden[:, span]]
-        parts += [jnp.broadcast_to(rows[r : r + 1, span], (splits, WIN)) for r in range(4)]
-        packed[:, clips + d // 6, d % 6 * D : (d % 6 + 1) * D] = jnp.concatenate(parts, axis=1)
 
 
 def bias_table(n_dp):
@@ -1246,7 +1286,7 @@
     )
     self_args = [d_attn, hidden_one, self_kv, self_q, self_att, self_lse]
     results = call(
-        partial(self_backward, n_p, splits, 0, half),
+        partial(self_backward, n_p, splits, 0, half, False),
         [("s", scal)] + vmem_of(frame_blocks) + vmem_of(self_args) + any_of(attn_gather.pieces()),
         kept_half + bias_type + [("v", (count, D), F32)],
         back_scratch(count),
@@ -1254,43 +1294,48 @@
         "self_backward_first",
     )
     results = list(results)
-    held = [text_got]
+    meet(
+        results,
+        sum_mlp[1].moved,
+        sum_cross[0].moved,
+        sum_cross[1].moved,
+    )
+    sum_self = [GradSum(ring, results[:n_o])]
+    self_bias_grad, self_back = results[n_o:]
+    sum_mlp[1].shard(2)
+    sum_cross[1].second()
+    sum_self[0].core()
+    small_args, small_outs, small_scratch, small_count = [], [], [], 0
+    if ring.square:
+        small_count = 32
+        small_args = [jnp.asarray(bias_table(n_dp)), cross_bias_grad, in_bias_grad]
+        small_args += [cross_rows, out_bias_grad, gate_sums, sums_two]
+        small_outs = [("v", (small_count, D), F32)]
+        small_scratch = [pltpu.VMEM((splits, small_count, D), F32)]
+    results = call(
+        partial(self_backward, n_p, splits, half, splits, ring.square),
+        [("s", scal)]
+        + vmem_of(frame_blocks)
+        + vmem_of(self_args)
+        + any_of(attn_gather.pieces())
+        + vmem_of([self_back, self_bias_grad] + small_args),
+        kept_half
+        + bias_type
+        + [("v", (rows, D), F32)]
+        + [("v", (rows + small_count, D), BF16)] * (splits - 1)
+        + [("v", (8, D), F32), ("v", (8, 2 * D), F32)]
+        + small_outs,
+        small_scratch + [pltpu.VMEM((count, D), F32)] + back_scratch(count),
+        18 * US,
+        "self_backward_last",
+    )
+    results = list(results)
+    held = [in_bias_grad, out_bias_grad, cross_bias_grad, cross_rows, gate_sums, sums_two]
+    held.append(text_got)
     meet(
         results,
         held,
         sum_mlp[0].arrived,
-        sum_mlp[1].moved,
-        sum_cross[0].moved,
-        sum_cross[1].moved,
-    )
-    text_got = held[0]
-    sum_self = [GradSum(ring, results[:n_o])]
-    self_bias_grad, self_back = results[n_o:]
-    sum_mlp[1].shard(2)
-    sum_cross[0].first()
-    sum_cross[1].second()
-    sum_self[0].core()
-    results = call(
-        partial(self_backward, n_p, splits, half, splits),
-        [("s", scal)]
-        + vmem_of(frame_blocks)
-        + vmem_of(self_args)
-        + any_of(attn_gather.pieces())
-        + vmem_of([self_back, self_bias_grad]),
-        kept_half
-        + bias_type
-        + [("v", (rows, D), F32)]
-        + [("v", (rows, D), BF16)] * (splits - 1)
-        + [("v", (8, D), F32), ("v", (8, 2 * D), F32)],
-        [pltpu.VMEM((count, D), F32)] + back_scratch(count),
-        18 * US,
-        "self_backward_last",
-    )
-    results = list(results)
-    held = [in_bias_grad, out_bias_grad, cross_bias_grad, cross_rows, gate_sums, sums_two]
-    meet(
-        results,
-        held,
         sum_mlp[1].arrived,
         sum_cross[0].moved,
         sum_cross[1].moved,
@@ -1299,51 +1344,38 @@
     sum_self.append(GradSum(ring, results[:n_o]))
     self_bias_grad, own_part = results[n_o : n_o + 2]
     parts = results[n_o + 2 : n_o + 1 + splits]
-    self_rows, sums_one = results[n_o + 1 + splits :]
-
+    self_rows, sums_one = results[n_o + 1 + splits : n_o + 3 + splits]
     sum_self[1].core()
-    sum_cross[1].first()
+    near_cross = join_first(*sum_cross)
     arrived = ring.z_back(parts)
-    in_bias_grad, out_bias_grad, cross_bias_grad, cross_rows, gate_sums, sums_two = held
-    small = [self_bias_grad, cross_bias_grad, in_bias_grad, self_rows, cross_rows, out_bias_grad]
-    small += [sums_one, gate_sums, sums_two]
+    in_bias_grad, out_bias_grad, cross_bias_grad, cross_rows, gate_sums, sums_two, text_got = held
     far = join_second(*sum_self)
-    early, late = arrived[0::2], arrived[1::2]
-    meet(small, far, sum_cross[1].moved, early)
+    early, late = arrived[:1], arrived[1:]
+    meet(far, near_cross, early)
     join_take(*sum_self, far)
+    join_take(*sum_cross, near_cross)
     near = join_first(*sum_self)
+    meet(late, near)
+    arrived = early + late
+    join_take(*sum_self, near)
+    last = join_shards([sum_cross, sum_self])
     if ring.square:
-        (packed,) = call(
-            pack_small,
-            vmem_of([jnp.asarray(bias_table(n_dp))] + small),
-            [("v", (splits, clips + 2, 6 * D), F32)],
-            [],
-            6 * US,
-            "pack_small",
-        )
-        held = [lax.all_to_all(packed, "head", 0, 0, tiled=True)]
-        got = jnp.sum(held[0], axis=0)
-        mod_low = got[:clips].astype(BF16).astype(F32)
-        bias_low = got[clips:].reshape(-1, 1, D)[:n_dp]
+        small = results[-1] + sum(part[rows:].astype(F32) for part in arrived)
+        mod_low = small[: 6 * clips].astype(BF16).astype(F32)
         sent = jnp.concatenate(
             [
                 jnp.broadcast_to(mod_low[None], (n_dp,) + mod_low.shape),
-                jnp.pad(bias_low, ((0, 0), (0, 0), (0, 5 * D))),
+                small[6 * clips : 6 * clips + n_dp, None],
             ],
             axis=1,
         )
         held = [lax.all_to_all(sent, "dp", 0, 0, tiled=True)]
-    meet(late, near)
-    arrived = early + late
-    join_take(*sum_self, near)
-    last = join_shards([sum_cross, sum_self])
-    self_bias_grad, cross_bias_grad, in_bias_grad, self_rows, cross_rows, out_bias_grad = small[:6]
     if ring.square:
-        mod_all = held[0][:, :clips].reshape(n_dp * clips, -1).astype(BF16)
-        bias_sum = jnp.sum(held[0][:, clips, :D], axis=0)
+        mod_all = held[0][:, : 6 * clips].reshape(n_dp * clips, -1).astype(BF16)
+        bias_sum = jnp.sum(held[0][:, 6 * clips], axis=0)
         places = [0, 24, 2 * WIN, 4 * WIN, 48, 72, 3 * WIN, WIN, 5 * WIN]
     else:
-        mod_all = mod_gradients(ring, small[6:], clips)
+        mod_all = mod_gradients(ring, [sums_one, gate_sums, sums_two], clips)
     step_part = lax.dot_general(
         mod_all, ada_weight, (((1,), (1,)), ((), ())), preferred_element_type=F32
     )

time: 400 us -> 384 us (0.960)
  starting transfers between devices: 82.6 us -> 66.3 us
    ppermute x3, waiting for transfers between devices: 14 us -> 26.4 us  [z_back(): lax.ppermute(parts[k - 1], 'head', [(s, (s - k) % n) for s in range(n)])]
    all_to_all x1 -> x0, waiting for transfers between devices: 10.4 us -> none  [on_device(): held = [lax.all_to_all(packed, 'head', 0, 0, tiled=True)]]
    all_to_all x1 -> x0, starting transfers between devices: 9.4 us -> none  [on_device(): held = [lax.all_to_all(packed, 'head', 0, 0, tiled=True)]]
    ppermute x6, waiting for transfers between devices: 8.75 us -> 0.02 us  [z_move(): return lax.ppermute(value, 'head', [(s, (s - k) % n) for s in range(n)])]
    ppermute x37 -> x36, waiting for transfers between devices: 10.5 us -> 16 us  [across(): return lax.ppermute(value, 'dp', how)]
    ppermute x6, starting transfers between devices: 15.8 us -> 10.5 us  [z_move(): return lax.ppermute(value, 'head', [(s, (s - k) % n) for s in range(n)])]
    all_to_all x1, waiting for transfers between devices: 1.63 us -> 6.73 us  [on_device(): held = [lax.all_to_all(sent, 'dp', 0, 0, tiled=True)]]
    pallas_call x10 -> x9, Pallas kernels: 138 us -> 136 us  [call(): pl.pallas_call(body, out_shape=tuple((jax.ShapeDtypeStruct(s, t) for _, s...]
  transfers between devices with their start and end apart: 60 -> 58, of which waited for: 11 -> 12; matrix products, arithmetic and copies ran while one was open for 13% -> 13% of each run, Pallas kernels for 35% -> 36%
where the time goes in v4:
time: 384 us; the launch traced here: 376 us
  Pallas kernels  136 us (35%)
  waiting for transfers between devices  72.9 us (19%)
  starting transfers between devices  66.3 us (17%)
  other arithmetic  38.4 us (10%)
  local copies, waits for them, and re-layouts  32.4 us (8%)
  blocking collectives  24.9 us (6%)
    pallas_call x9, Pallas kernels, call(): pl.pallas_call(body, out_shape=tuple((jax.ShapeDtypeStruct(s, t) for _, s...  136 us
    ppermute x3, waiting for transfers between devices, z_back(): lax.ppermute(parts[k - 1], 'head', [(s, (s - k) % n) for s in range(n)])  26.4 us
    all_to_all x1, blocking collectives, on_device(): got = lax.all_to_all(sent, both, 0, 0, tiled=True)  24.9 us
    ppermute x36, starting transfers between devices, across(): return lax.ppermute(value, 'dp', how)  21.2 us
    all_to_all x1, waiting for transfers between devices, on_device(): lax.all_to_all(mod_part.reshape(n_dp, clips, -1), 'dp', 0, 0, tiled=True)  18.1 us
    ppermute x36, waiting for transfers between devices, across(): return lax.ppermute(value, 'dp', how)  16 us
    ppermute x9, starting transfers between devices, z_pieces(): lax.ppermute(value, 'head', [(s, (s + k) % n) for s in range(n)])  15.1 us
    unnamed x124, local copies, waits for them, and re-layouts  12.2 us
  transfers between devices with their start and end apart: 58, of which 12 were waited for; matrix products, arithmetic and copies ran while one was open for 13% of the time, Pallas kernels for 36%

profile of v4, /device:TPU:0, one launch (start us, length us, event | category | flops | bytes accessed | tf_op | source)
XLA Modules:
  0.0 376.0 jit_solution(8308743181020429747)
XLA Ops:
  4.1 5.1 %collective-permute-start.5 = (bf16[96,1536]{1,0:T(8,128)(2,1)S(1)}, bf16[96,1536]{1,0:T(8,128)(2,1)S(1)}, u32[]{:S(2)}, u32[]{:S(2)}) collective-permute-start(bf16[96,1536]{1,0:T(8,128)(2,1)S(1)} %concatenate.72), channel_id=1, source_target_pairs={{0,3},{1,0},{2,1},{3,2},{4,7},{5,4},{6,5},{7,6},{8,11},{9,8},{10,9... | collective-permute-start | bytes 884744 | tf_op jit(solution)/shard_map/ppermute | solution.py:792
  12.9 24.9 %all_to_all.33 = bf16[32,2,720]{2,1,0:T(2,128)(2,1)S(1)} all-to-all(bf16[32,2,720]{2,1,0:T(2,128)(2,1)S(1)} %reshape.418), channel_id=1, replica_groups=mesh['dp'=8,'head'=4] {'dp','head'}, dimensions={0} | all-to-all | bytes 184320 | tf_op jit(solution)/shard_map/all_to_all | solution.py:1033
  39.6 3.9 %collective-permute-start.2 = (bf16[256,768]{1,0:T(8,128)(2,1)}, bf16[256,768]{1,0:T(8,128)(2,1)}, u32[]{:S(2)}, u32[]{:S(2)}) collective-permute-start(bf16[256,768]{1,0:T(8,128)(2,1)} %refs_1_.7), channel_id=1, source_target_pairs={{0,3},{1,0},{2,1},{3,2},{4,7},{5,4},{6,5},{7,6},{8,11},{9,8},{10,9... | collective-permute-start | bytes 1179656 | tf_op jit(solution)/shard_map/ppermute | solution.py:792
  46.2 3.6 all-to-all-start.1
  51.0 3.9 %stack.102.refs_0_ = s32[16]{0:T(128)} concatenate(s32[1]{0:T(128)} %bitcast, s32[1]{0:T(128)} %bitcast.2, s32[1]{0:T(128)} %bitcast.3, s32[1]{0:T(128)} %bitcast.4, s32[1]{0:T(128)} %bitcast.5, s32[1]{0:T(128)} %bitcast.6, s32[2]{0:T(128)S(1)} %broadcast.19, s32[1]{0:T(128)} %bitcast.7, s32[1]{0:T(128)} %bitcast.8, s32[1]{0:T(128)} %bitcast.9, s32[1]{0:T(128)} %bitcast.10, ...), dimensions={0} | concatenate | bytes 128 | tf_op jit(solution)/shard_map/stack | solution.py:999
  54.9 18.1 %all-to-all-done.1 = f32[8,3,4608]{2,1,0:T(4,128)S(1)} async-done(((f32[8,3,4608]{2,1,0:T(4,128)}), f32[8,3,4608]{2,1,0:T(4,128)S(1)}, u32[]{:S(2)}, u32[]{:S(2)}) %all-to-all-start.1) | async-done | bytes 442400 | tf_op jit(solution)/shard_map/all_to_all | solution.py:1069
  79.7 5.7 %collective-permute-done.13 = bf16[96,1536]{1,0:T(8,128)(2,1)} collective-permute-done((bf16[96,1536]{1,0:T(8,128)(2,1)S(1)}, bf16[96,1536]{1,0:T(8,128)(2,1)}, u32[]{:S(2)}, u32[]{:S(2)}) %collective-permute-start.13) | collective-permute-done | bytes 294944 | tf_op jit(solution)/shard_map/ppermute | solution.py:792
  85.3 4.2 %collective-permute-done.8.refs_11_.refs_9_.refs_15_.refs_14_ = bf16[4,96,1536]{2,1,0:T(8,128)(2,1)} collective-permute-done((bf16[4,96,1536]{2,1,0:T(8,128)(2,1)}, bf16[4,96,1536]{2,1,0:T(8,128)(2,1)}, u32[]{:S(2)}, u32[]{:S(2)}) %collective-permute-start.8) | collective-permute-done | bytes 1179680 | tf_op jit(solution)/shard_map/ppermute | solution.py:804
  91.2 3.8 %collective-permute-start.18 = (bf16[96,1536]{1,0:T(8,128)(2,1)S(1)}, bf16[96,1536]{1,0:T(8,128)(2,1)S(1)}, u32[]{:S(2)}, u32[]{:S(2)}) collective-permute-start(bf16[96,1536]{1,0:T(8,128)(2,1)S(1)} %pad_maximum_fusion.7), channel_id=1, source_target_pairs={{0,3},{1,0},{2,1},{3,2},{4,7},{5,4},{6,5},{7,6},{8,11},{9,8},{10,9... | collective-permute-start | bytes 884744 | tf_op jit(solution)/shard_map/ppermute | solution.py:792
  98.6 19.1 %self_forward.1 = (bf16[768,1024]{1,0:T(8,128)(2,1)}, bf16[4,1024,512]{2,1,0:T(8,128)(2,1)}, bf16[4,256,256]{2,1,0:T(8,128)(2,1)}, bf16[4,256,256]{2,1,0:T(8,128...) custom-call(s32[16]{0:T(128)} %stack.102.refs_0_, bf16[256,768]{1,0:T(8,128)(2,1)} %refs_1_.7, ...), custom_call_target="tpu_custom_call" | custom-call | flops 25300000768 | bytes 19502144 | tf_op jit(solution)/shard_map/self_forward/pallas_call | solution.py:748
  121.2 17.4 %cross_forward.1 = (bf16[768,256]{1,0:T(8,128)(2,1)}, bf16[768,768]{1,0:T(8,128)(2,1)}, bf16[4,768,512]{2,1,0:T(8,128)(2,1)}, bf16[4,256,256]{2,1,0:T(8,128)(2,1...) custom-call(s32[16]{0:T(128)} %stack.102.refs_0_, ...), custom_call_target="tpu_custom_call" | custom-call | flops 19549999104 | bytes 18008128 | tf_op jit(solution)/shard_map/cross_forward/pallas_call | solution.py:748
  145.5 11.1 %feed_forward_first.1 = (bf16[4,2,96,1536]{3,2,1,0:T(8,128)(2,1)}, bf16[4,2,96,1536]{3,2,1,0:T(8,128)(2,1)}, f32[4,1,768]{2,1,0:T(1,128)}, f32[256,768]{1,0:T(8,128)}, f32[256,768]{1,0:T(8,128)}) custom-call(s32[16]{0:T(128)} %stack.102.refs_0_, f32[256,768]{1,0:T(8,128)} %get-tuple-element.236.refs_1_, bf16[256,768]{1,0:T(8,128)(2,1)} %refs_2_.5, ...), custom_call_target="tpu_custom_call" | custom-call | flops 10350000128 | bytes 12272704 | tf_op jit(solution)/shard_map/feed_forward_first/pallas_call | solution.py:748
  158.6 5.1 %collective-permute-done.29.refs_13_ = bf16[2,96,1536]{2,1,0:T(8,128)(2,1)S(1)} collective-permute-done((bf16[2,96,1536]{2,1,0:T(8,128)(2,1)}, bf16[2,96,1536]{2,1,0:T(8,128)(2,1)S(1)}, u32[]{:S(2)}, u32[]{:S(2)}) %collective-permute-start.29) | collective-permute-done | bytes 589856 | tf_op jit(solution)/shard_map/ppermute | solution.py:804
  164.5 11.8 %feed_forward_last.1 = (bf16[4,2,96,1536]{3,2,1,0:T(8,128)(2,1)}, bf16[4,2,96,1536]{3,2,1,0:T(8,128)(2,1)}, f32[4,1,768]{2,1,0:T(1,128)}, bf16[256,768]{1,0:T(8,...) custom-call(s32[16]{0:T(128)} %stack.102.refs_0_, f32[256,768]{1,0:T(8,128)} %get-tuple-element.236.refs_1_, ...), custom_call_target="tpu_custom_call" | custom-call | flops 11500000256 | bytes 13541440 | tf_op jit(solution)/shard_map/feed_forward_last/pallas_call | solution.py:748
  178.8 15.9 %cross_backward_first.1 = (bf16[4,2,96,768]{3,2,1,0:T(8,128)(2,1)}, bf16[4,2,96,768]{3,2,1,0:T(8,128)(2,1)}, f32[4,1,768]{2,1,0:T(1,128)}, f32[256,768]{1,0:T(8,128)}, f32[768,768]{1,0:T(8,128)}) custom-call(s32[16]{0:T(128)} %stack.102.refs_0_, f32[256,768]{1,0:T(8,128)} %get-tuple-element.271.refs_1_, f32[256,768]{1,0:T(8,128)} %get-tuple-element.214.refs_1_.refs_2_, ...), custom_call_target="tpu_custom_call" | custom-call | flops 16099999744 | bytes 23172160 | tf_op jit(solution)/shard_map/cross_backward_first/pallas_call | solution.py:748
  200.2 17.6 %cross_backward_last.1 = (bf16[4,2,96,768]{3,2,1,0:T(8,128)(2,1)}, bf16[4,2,96,768]{3,2,1,0:T(8,128)(2,1)}, f32[4,1,768]{2,1,0:T(1,128)}, f32[256,768]{1,0:T(8,1...) custom-call(s32[16]{0:T(128)} %stack.102.refs_0_, ...), custom_call_target="tpu_custom_call" | custom-call | flops 17250000896 | bytes 25592896 | tf_op jit(solution)/shard_map/cross_backward_last/pallas_call | solution.py:748
  219.3 4.0 %all-to-all-start.2 = ((bf16[4,192,768]{2,1,0:T(8,128)(2,1)}), bf16[4,192,768]{2,1,0:T(8,128)(2,1)S(1)}, u32[]{:S(2)}, u32[]{:S(2)}) async-start(bf16[4,192,768]{2,1,0:T(8,128)(2,1)} %bitcast.267), calls=%async_computation.2 | async-start | bytes 2359296 | tf_op jit(solution)/shard_map/all_to_all | solution.py:1284
  225.6 3.9 %collective-permute-start.39 = (bf16[96,1536]{1,0:T(8,128)(2,1)}, bf16[96,1536]{1,0:T(8,128)(2,1)}, u32[]{:S(2)}, u32[]{:S(2)}) collective-permute-start(bf16[96,1536]{1,0:T(8,128)(2,1)} %fusion.9), channel_id=1, source_target_pairs={{0,3},{1,0},{2,1},{3,2},{4,7},{5,4},{6,5},{7,6},{8,11},{9,8},{10,9... | collective-permute-start | bytes 884744 | tf_op jit(solution)/shard_map/ppermute | solution.py:808
  235.5 17.5 %self_backward_first.1 = (bf16[4,2,96,768]{3,2,1,0:T(8,128)(2,1)}, bf16[4,2,96,768]{3,2,1,0:T(8,128)(2,1)}, f32[4,1,768]{2,1,0:T(1,128)}, f32[1024,768]{1,0:T(8,128)}) custom-call(s32[16]{0:T(128)} %stack.102.refs_0_, bf16[256,768]{1,0:T(8,128)(2,1)} %refs_1_.7, bf16[256,768]{1,0:T(8,128)(2,1)} %collective-permute-done.refs_2_, ...), custom_call_target="tpu_custom_call" | custom-call | flops 19549999104 | bytes 23769152 | tf_op jit(solution)/shard_map/self_backward_first/pallas_call | solution.py:748
  258.7 22.2 %self_backward_last.1 = (bf16[4,2,96,768]{3,2,1,0:T(8,128)(2,1)}, bf16[4,2,96,768]{3,2,1,0:T(8,128)(2,1)}, f32[4,1,768]{2,1,0:T(1,128)}, f32[256,768]{1,0:T(8,12...) custom-call(s32[16]{0:T(128)} %stack.102.refs_0_, ...), custom_call_target="tpu_custom_call" | custom-call | flops 20700000256 | bytes 26250304 | tf_op jit(solution)/shard_map/self_backward_last/pallas_call | solution.py:748
  299.4 7.1 %collective-permute-done.47.refs_5_ = bf16[288,768]{1,0:T(8,128)(2,1)S(1)} collective-permute-done((bf16[288,768]{1,0:T(8,128)(2,1)}, bf16[288,768]{1,0:T(8,128)(2,1)S(1)}, u32[]{:S(2)}, u32[]{:S(2)}) %collective-permute-start.47) | collective-permute-done | bytes 442400 | tf_op jit(solution)/shard_map/ppermute | solution.py:799
  316.7 19.3 %collective-permute-done.48.refs_6_ = bf16[288,768]{1,0:T(8,128)(2,1)S(1)} collective-permute-done((bf16[288,768]{1,0:T(8,128)(2,1)}, bf16[288,768]{1,0:T(8,128)(2,1)S(1)}, u32[]{:S(2)}, u32[]{:S(2)}) %collective-permute-start.48) | collective-permute-done | bytes 442400 | tf_op jit(solution)/shard_map/ppermute | solution.py:799
  338.2 5.2 %collective-permute-start.52 = (bf16[96,1536]{1,0:T(8,128)(2,1)S(1)}, bf16[96,1536]{1,0:T(8,128)(2,1)}, u32[]{:S(2)}, u32[]{:S(2)}) collective-permute-start(bf16[96,1536]{1,0:T(8,128)(2,1)S(1)} %pad_maximum_fusion.9), channel_id=1, source_target_pairs={{0,2},{1,3},{2,0},{3,1},{4,6},{5,7},{6,4},{7,5},{8,10},{9,11},{10,... | collective-permute-start | bytes 884744 | tf_op jit(solution)/shard_map/ppermute | solution.py:808
  351.5 6.7 %all-to-all-done.3 = f32[8,19,768]{2,1,0:T(8,128)S(1)} async-done(((f32[8,19,768]{2,1,0:T(8,128)}), f32[8,19,768]{2,1,0:T(8,128)S(1)}, u32[]{:S(2)}, u32[]{:S(2)}) %all-to-all-start.3) | async-done | bytes 466976 | tf_op jit(solution)/shard_map/all_to_all | solution.py:1372
  (386 shorter events, 116.3 us)
Async XLA Ops:
  4.1 34.0 %collective-permute-start.5 = (bf16[96,1536]{1,0:T(8,128)(2,1)S(1)}, bf16[96,1536]{1,0:T(8,128)(2,1)S(1)}, u32[]{:S(2)}, u32[]{:S(2)}) collective-permute-start(bf16[96,1536]{1,0:T(8,128)(2,1)S(1)} %concatenate.72), channel_id=1, source_target_pairs={{0,3},{1,0},{2,1},{3,2},{4,7},{5,4},{6,5},{7,6},{8,11},{9,8},{10,9... | collective-permute-start | bytes 884744 | tf_op jit(solution)/shard_map/ppermute | solution.py:792
  9.2 28.9 %collective-permute-start.4 = (bf16[96,1536]{1,0:T(8,128)(2,1)S(1)}, bf16[96,1536]{1,0:T(8,128)(2,1)S(1)}, u32[]{:S(2)}, u32[]{:S(2)}) collective-permute-start(bf16[96,1536]{1,0:T(8,128)(2,1)S(1)} %concatenate.72), channel_id=1, source_target_pairs={{0,2},{1,3},{2,0},{3,1},{4,6},{5,7},{6,4},{7,5},{8,10},{9,11},{10,... | collective-permute-start | bytes 884744 | tf_op jit(solution)/shard_map/ppermute | solution.py:792
  9.2 28.9 %collective-permute-start.3 = (bf16[96,1536]{1,0:T(8,128)(2,1)S(1)}, bf16[96,1536]{1,0:T(8,128)(2,1)S(1)}, u32[]{:S(2)}, u32[]{:S(2)}) collective-permute-start(bf16[96,1536]{1,0:T(8,128)(2,1)S(1)} %concatenate.72), channel_id=1, source_target_pairs={{0,1},{1,2},{2,3},{3,0},{4,5},{5,6},{6,7},{7,4},{8,9},{9,10},{10,1... | collective-permute-start | bytes 884744 | tf_op jit(solution)/shard_map/ppermute | solution.py:792
  38.2 34.8 %collective-permute-start.7 = (bf16[4,96,1536]{2,1,0:T(8,128)(2,1)S(1)}, bf16[4,96,1536]{2,1,0:T(8,128)(2,1)}, u32[]{:S(2)}, u32[]{:S(2)}) collective-permute-start(bf16[4,96,1536]{2,1,0:T(8,128)(2,1)S(1)} %pad_maximum_fusion.refs_8_.refs_6_.refs_12_.refs_11_), channel_id=1, source_target_pairs={{0,16},{4,12},{8,24},{12,4},{16,0},{20,28},{24,8},{28,20},{1,17},{... | collective-permute-start | bytes 3538952 | tf_op jit(solution)/shard_map/ppermute | solution.py:804
  39.0 34.0 %collective-permute-start.6 = (bf16[4,96,1536]{2,1,0:T(8,128)(2,1)S(1)}, bf16[4,96,1536]{2,1,0:T(8,128)(2,1)}, u32[]{:S(2)}, u32[]{:S(2)}) collective-permute-start(bf16[4,96,1536]{2,1,0:T(8,128)(2,1)S(1)} %pad_maximum_fusion.refs_8_.refs_6_.refs_12_.refs_11_), channel_id=1, source_target_pairs={{0,8},{4,20},{8,0},{12,28},{16,24},{20,4},{24,16},{28,12},{1,9},{5... | collective-permute-start | bytes 3538952 | tf_op jit(solution)/shard_map/ppermute | solution.py:804
  39.6 39.5 %collective-permute-start.2 = (bf16[256,768]{1,0:T(8,128)(2,1)}, bf16[256,768]{1,0:T(8,128)(2,1)}, u32[]{:S(2)}, u32[]{:S(2)}) collective-permute-start(bf16[256,768]{1,0:T(8,128)(2,1)} %refs_1_.7), channel_id=1, source_target_pairs={{0,3},{1,0},{2,1},{3,2},{4,7},{5,4},{6,5},{7,6},{8,11},{9,8},{10,9... | collective-permute-start | bytes 1179656 | tf_op jit(solution)/shard_map/ppermute | solution.py:792
  43.5 35.6 %collective-permute-start.1 = (bf16[256,768]{1,0:T(8,128)(2,1)}, bf16[256,768]{1,0:T(8,128)(2,1)}, u32[]{:S(2)}, u32[]{:S(2)}) collective-permute-start(bf16[256,768]{1,0:T(8,128)(2,1)} %refs_1_.7), channel_id=1, source_target_pairs={{0,2},{1,3},{2,0},{3,1},{4,6},{5,7},{6,4},{7,5},{8,10},{9,11},{10,... | collective-permute-start | bytes 1179656 | tf_op jit(solution)/shard_map/ppermute | solution.py:792
  43.5 47.7 %collective-permute-start = (bf16[256,768]{1,0:T(8,128)(2,1)}, bf16[256,768]{1,0:T(8,128)(2,1)}, u32[]{:S(2)}, u32[]{:S(2)}) collective-permute-start(bf16[256,768]{1,0:T(8,128)(2,1)} %refs_1_.7), channel_id=1, source_target_pairs={{0,1},{1,2},{2,3},{3,0},{4,5},{5,6},{6,7},{7,4},{8,9},{9,10},{10,1... | collective-permute-start | bytes 1179656 | tf_op jit(solution)/shard_map/ppermute | solution.py:792
  46.2 26.8 %all-to-all-start.1 = ((f32[8,3,4608]{2,1,0:T(4,128)}), f32[8,3,4608]{2,1,0:T(4,128)S(1)}, u32[]{:S(2)}, u32[]{:S(2)}) async-start(f32[8,3,4608]{2,1,0:T(4,128)} %copy.164), calls=%async_computation.1 | async-start | bytes 1179648 | tf_op jit(solution)/shard_map/all_to_all | solution.py:1069
  91.2 26.5 %collective-permute-start.18 = (bf16[96,1536]{1,0:T(8,128)(2,1)S(1)}, bf16[96,1536]{1,0:T(8,128)(2,1)S(1)}, u32[]{:S(2)}, u32[]{:S(2)}) collective-permute-start(bf16[96,1536]{1,0:T(8,128)(2,1)S(1)} %pad_maximum_fusion.7), channel_id=1, source_target_pairs={{0,3},{1,0},{2,1},{3,2},{4,7},{5,4},{6,5},{7,6},{8,11},{9,8},{10,9... | collective-permute-start | bytes 884744 | tf_op jit(solution)/shard_map/ppermute | solution.py:792
  95.1 22.7 %collective-permute-start.17 = (bf16[96,1536]{1,0:T(8,128)(2,1)S(1)}, bf16[96,1536]{1,0:T(8,128)(2,1)S(1)}, u32[]{:S(2)}, u32[]{:S(2)}) collective-permute-start(bf16[96,1536]{1,0:T(8,128)(2,1)S(1)} %pad_maximum_fusion.7), channel_id=1, source_target_pairs={{0,2},{1,3},{2,0},{3,1},{4,6},{5,7},{6,4},{7,5},{8,10},{9,11},{10,... | collective-permute-start | bytes 884744 | tf_op jit(solution)/shard_map/ppermute | solution.py:792
  95.1 22.7 %collective-permute-start.16 = (bf16[2,96,1536]{2,1,0:T(8,128)(2,1)S(1)}, bf16[2,96,1536]{2,1,0:T(8,128)(2,1)S(1)}, u32[]{:S(2)}, u32[]{:S(2)}) collective-permute-start(bf16[2,96,1536]{2,1,0:T(8,128)(2,1)S(1)} %pad_maximum_fusion.2.refs_6_), channel_id=1, source_target_pairs={{0,4},{4,0},{8,12},{12,8},{16,20},{20,16},{24,28},{28,24},{1,5},{5... | collective-permute-start | bytes 1769480 | tf_op jit(solution)/shard_map/ppermute | solution.py:804
  219.3 62.4 %all-to-all-start.2 = ((bf16[4,192,768]{2,1,0:T(8,128)(2,1)}), bf16[4,192,768]{2,1,0:T(8,128)(2,1)S(1)}, u32[]{:S(2)}, u32[]{:S(2)}) async-start(bf16[4,192,768]{2,1,0:T(8,128)(2,1)} %bitcast.267), calls=%async_computation.2 | async-start | bytes 2359296 | tf_op jit(solution)/shard_map/all_to_all | solution.py:1284
  225.6 55.4 %collective-permute-start.39 = (bf16[96,1536]{1,0:T(8,128)(2,1)}, bf16[96,1536]{1,0:T(8,128)(2,1)}, u32[]{:S(2)}, u32[]{:S(2)}) collective-permute-start(bf16[96,1536]{1,0:T(8,128)(2,1)} %fusion.9), channel_id=1, source_target_pairs={{0,3},{1,0},{2,1},{3,2},{4,7},{5,4},{6,5},{7,6},{8,11},{9,8},{10,9... | collective-permute-start | bytes 884744 | tf_op jit(solution)/shard_map/ppermute | solution.py:808
  255.2 25.8 %collective-permute-start.41 = (bf16[96,1536]{1,0:T(8,128)(2,1)S(1)}, bf16[96,1536]{1,0:T(8,128)(2,1)S(1)}, u32[]{:S(2)}, u32[]{:S(2)}) collective-permute-start(bf16[96,1536]{1,0:T(8,128)(2,1)S(1)} %get-tuple-element.503), channel_id=1, source_target_pairs={{0,1},{1,2},{2,3},{3,0},{4,5},{5,6},{6,7},{7,4},{8,9},{9,10},{10,1... | collective-permute-start | bytes 884744 | tf_op jit(solution)/shard_map/ppermute | solution.py:808
  255.5 26.2 %collective-permute-start.40 = (bf16[96,1536]{1,0:T(8,128)(2,1)S(1)}, bf16[96,1536]{1,0:T(8,128)(2,1)}, u32[]{:S(2)}, u32[]{:S(2)}) collective-permute-start(bf16[96,1536]{1,0:T(8,128)(2,1)S(1)} %get-tuple-element.504), channel_id=1, source_target_pairs={{0,2},{1,3},{2,0},{3,1},{4,6},{5,7},{6,4},{7,5},{8,10},{9,11},{10,... | collective-permute-start | bytes 884744 | tf_op jit(solution)/shard_map/ppermute | solution.py:808
  257.6 24.2 %collective-permute-start.42 = (bf16[2,2,96,768]{3,2,1,0:T(8,128)(2,1)}, bf16[2,2,96,768]{3,2,1,0:T(8,128)(2,1)}, u32[]{:S(2)}, u32[]{:S(2)}) collective-permute-start(bf16[2,2,96,768]{3,2,1,0:T(8,128)(2,1)} %add_convert_fusion.4), channel_id=1, source_target_pairs={{0,16},{4,12},{8,24},{12,4},{16,0},{20,28},{24,8},{28,20},{1,17},{... | collective-permute-start | bytes 1769480 | tf_op jit(solution)/shard_map/ppermute | solution.py:804
  258.7 23.0 %collective-permute-start.43 = (bf16[4,2,96,768]{3,2,1,0:T(8,128)(2,1)}, bf16[4,2,96,768]{3,2,1,0:T(8,128)(2,1)}, u32[]{:S(2)}, u32[]{:S(2)}) collective-permute-start(bf16[4,2,96,768]{3,2,1,0:T(8,128)(2,1)} %get-tuple-element.345), channel_id=1, source_target_pairs={{0,4},{4,0},{8,12},{12,8},{16,20},{20,16},{24,28},{28,24},{1,5},{5... | collective-permute-start | bytes 3538952 | tf_op jit(solution)/shard_map/ppermute | solution.py:804
  287.4 22.8 %collective-permute-start.45 = (bf16[2,4,96,768]{3,2,1,0:T(8,128)(2,1)}, bf16[2,4,96,768]{3,2,1,0:T(8,128)(2,1)}, u32[]{:S(2)}, u32[]{:S(2)}) collective-permute-start(bf16[2,4,96,768]{3,2,1,0:T(8,128)(2,1)} %pad_maximum_fusion.1), channel_id=1, source_target_pairs={{0,16},{4,12},{8,24},{12,4},{16,0},{20,28},{24,8},{28,20},{1,17},{... | collective-permute-start | bytes 3538952 | tf_op jit(solution)/shard_map/ppermute | solution.py:804
  295.5 40.4 %collective-permute-start.48 = (bf16[288,768]{1,0:T(8,128)(2,1)}, bf16[288,768]{1,0:T(8,128)(2,1)S(1)}, u32[]{:S(2)}, u32[]{:S(2)}) collective-permute-start(bf16[288,768]{1,0:T(8,128)(2,1)} %get-tuple-element.357), channel_id=1, source_target_pairs={{0,2},{1,3},{2,0},{3,1},{4,6},{5,7},{6,4},{7,5},{8,10},{9,11},{10,... | collective-permute-start | bytes 1327112 | tf_op jit(solution)/shard_map/ppermute | solution.py:799
  297.5 38.5 %collective-permute-start.49 = (bf16[288,768]{1,0:T(8,128)(2,1)}, bf16[288,768]{1,0:T(8,128)(2,1)S(1)}, u32[]{:S(2)}, u32[]{:S(2)}) collective-permute-start(bf16[288,768]{1,0:T(8,128)(2,1)} %get-tuple-element.358), channel_id=1, source_target_pairs={{0,1},{1,2},{2,3},{3,0},{4,5},{5,6},{6,7},{7,4},{8,9},{9,10},{10,1... | collective-permute-start | bytes 1327112 | tf_op jit(solution)/shard_map/ppermute | solution.py:799
  311.9 24.1 %collective-permute-start.50 = (bf16[4,96,768]{2,1,0:T(8,128)(2,1)S(1)}, bf16[4,96,768]{2,1,0:T(8,128)(2,1)S(1)}, u32[]{:S(2)}, u32[]{:S(2)}) collective-permute-start(bf16[4,96,768]{2,1,0:T(8,128)(2,1)S(1)} %pad_maximum_fusion.5), channel_id=1, source_target_pairs={{0,8},{4,20},{8,0},{12,28},{16,24},{20,4},{24,16},{28,12},{1,9},{5... | collective-permute-start | bytes 1769480 | tf_op jit(solution)/shard_map/ppermute | solution.py:804
  338.1 30.5 %collective-permute-start.51 = (bf16[96,1536]{1,0:T(8,128)(2,1)S(1)}, bf16[96,1536]{1,0:T(8,128)(2,1)S(1)}, u32[]{:S(2)}, u32[]{:S(2)}) collective-permute-start(bf16[96,1536]{1,0:T(8,128)(2,1)S(1)} %pad_maximum_fusion.8), channel_id=1, source_target_pairs={{0,3},{1,0},{2,1},{3,2},{4,7},{5,4},{6,5},{7,6},{8,11},{9,8},{10,9... | collective-permute-start | bytes 884744 | tf_op jit(solution)/shard_map/ppermute | solution.py:808
  338.2 30.5 %collective-permute-start.52 = (bf16[96,1536]{1,0:T(8,128)(2,1)S(1)}, bf16[96,1536]{1,0:T(8,128)(2,1)}, u32[]{:S(2)}, u32[]{:S(2)}) collective-permute-start(bf16[96,1536]{1,0:T(8,128)(2,1)S(1)} %pad_maximum_fusion.9), channel_id=1, source_target_pairs={{0,2},{1,3},{2,0},{3,1},{4,6},{5,7},{6,4},{7,5},{8,10},{9,11},{10,... | collective-permute-start | bytes 884744 | tf_op jit(solution)/shard_map/ppermute | solution.py:808
  (93 other events, 1057.4 us)
